TPU v7x, 32 devices: a whole 2x2x4 slice. The times are simulated.
32 devices in a mesh: rep: 8 (over z, core), shard: 4 (over y, x).
Axes of the slice: x: 2, y: 2, z: 4, core: 2. Of those that a mesh axis runs over, the one named last changes fastest.
Arguments:
- layer_input: bfloat16 [32768, 1024], P(('rep', 'shard')), may hold values from -6 to 6
- seq_lengths: int32 [32], P(('rep', 'shard')), may hold values from 256 to 1024, as said below
- out_grad: bfloat16 [32768, 1024], P(('rep', 'shard')), may hold values from -6 to 6
- attn_gain: bfloat16 [1024], P('shard'), may hold values from 0.5 to 1.5
- attn_shift: bfloat16 [1024], P('shard'), may hold values from -1 to 1
- mlp_gain: bfloat16 [1024], P('shard'), may hold values from 0.5 to 1.5
- mlp_shift: bfloat16 [1024], P('shard'), may hold values from -1 to 1
- qkv_weight: bfloat16 [1024, 3072], P('shard'), may hold values from -0.1875 to 0.1875
- qkv_bias: bfloat16 [3072], P('shard'), may hold values from -1 to 1
- dense_weight: bfloat16 [1024, 1024], P('shard'), may hold values from -3 to 3
- dense_bias: bfloat16 [1024], P('shard'), may hold values from -1 to 1
- inner_weight: bfloat16 [1024, 4096], P('shard'), may hold values from -0.1875 to 0.1875
- inner_bias: bfloat16 [4096], P('shard'), may hold values from -1 to 1
- outer_weight: bfloat16 [4096, 1024], P('shard'), may hold values from -0.09375 to 0.09375
- outer_bias: bfloat16 [1024], P('shard'), may hold values from -1 to 1
Outputs:
- layer_output: float32 [32768, 1024], P(('rep', 'shard'))
- input_grad: float32 [32768, 1024], P(('rep', 'shard'))
- attn_gain_grad: float32 [1024], P('shard')
- attn_shift_grad: float32 [1024], P('shard')
- mlp_gain_grad: float32 [1024], P('shard')
- mlp_shift_grad: float32 [1024], P('shard')
- qkv_weight_grad: float32 [1024, 3072], P('shard')
- qkv_bias_grad: float32 [3072], P('shard')
- dense_weight_grad: float32 [1024, 1024], P('shard')
- dense_bias_grad: float32 [1024], P('shard')
- inner_weight_grad: float32 [1024, 4096], P('shard')
- inner_bias_grad: float32 [4096], P('shard')
- outer_weight_grad: float32 [4096, 1024], P('shard')
- outer_bias_grad: float32 [1024], P('shard')
Inputs may be any that keep to these rules, and one draw needn't show every extreme that they name: Each slot holds one sequence in its first seq_lengths positions; at least one slot is full.
All inputs are finite; a program needn't handle non-finite values.
Results may differ from a plain program's by a relative error of at most 0.0089.
Values may be sent and summed in bfloat16 or wider, within the bound.
No kernel may reach another device: no remote copies, remote signals or barrier semaphores. Data moves between devices by JAX's collectives and lax.ppermute only.
A program may use at most 384 MiB of HBM per device.

v0:
```python
from functools import partial

import jax
import jax.numpy as jnp
from jax import lax
from jax.sharding import PartitionSpec as P

D = 1024
H = 16
HD = 64
ROT = 16
SLOT = 1024
QB = 512


EPSILON = 1e-05
MASKED = -1e30


def standardize(values):
    average = jnp.mean(values, axis=-1, keepdims=True)
    centered = values - average
    variance = jnp.mean(centered * centered, axis=-1, keepdims=True)
    return centered * lax.rsqrt(variance + EPSILON)


def exact_gelu(values):
    return jax.nn.gelu(values, approximate=False)


def rotary_tables():
    positions = jnp.arange(SLOT, dtype=jnp.float32)
    rot_half = ROT // 2
    inverse = 1.0 / 10000.0 ** (jnp.arange(rot_half, dtype=jnp.float32) * (2.0 / ROT))
    angles = positions[:, None] * inverse[None, :]
    angles = jnp.concatenate([angles, angles], axis=1)
    padding = HD - ROT
    cosine_table = jnp.concatenate(
        [jnp.cos(angles), jnp.ones((SLOT, padding), jnp.float32)], axis=1
    )
    sine_table = jnp.concatenate([jnp.sin(angles), jnp.zeros((SLOT, padding), jnp.float32)], axis=1)
    return (cosine_table[:, None, :], sine_table[:, None, :])


def rotate(vectors, cosine_table, sine_table):
    rot_half = ROT // 2
    partner = jnp.concatenate(
        [-vectors[..., rot_half:ROT], vectors[..., :rot_half], jnp.zeros_like(vectors[..., ROT:])],
        axis=-1,
    )
    return vectors * cosine_table + partner * sine_table


def rotate_back(grads, cosine_table, sine_table):
    rot_half = ROT // 2
    scaled = grads * sine_table
    partner = jnp.concatenate(
        [scaled[..., rot_half:ROT], -scaled[..., :rot_half], jnp.zeros_like(scaled[..., ROT:])],
        axis=-1,
    )
    return grads * cosine_table + partner


def block_scores(block_queries, slot_keys, row_start, length):
    raw = jnp.einsum("qhd,khd->hqk", block_queries, slot_keys, preferred_element_type=jnp.float32)
    query_rows = row_start + jnp.arange(block_queries.shape[0], dtype=jnp.int32)
    key_index = jnp.arange(slot_keys.shape[0], dtype=jnp.int32)
    allowed = (key_index[None, :] <= query_rows[:, None]) & (key_index[None, :] < length)
    return (0.125 * raw, allowed)


def forward_slot(operands):
    slot_queries, slot_keys, slot_values, length = operands

    def forward_one_block(block_index):
        row_start = block_index * QB
        block_queries = lax.dynamic_slice_in_dim(slot_queries, row_start, QB, 0)
        scores, allowed = block_scores(block_queries, slot_keys, row_start, length)
        masked = jnp.where(allowed[None], scores, MASKED)
        row_max = jnp.max(masked, axis=-1, keepdims=True)
        exponent = jnp.exp(masked - row_max)
        row_total = jnp.sum(exponent, axis=-1, keepdims=True)
        probs_low = (exponent / row_total).astype(jnp.bfloat16)
        context = jnp.einsum(
            "hqk,khd->qhd", probs_low, slot_values, preferred_element_type=jnp.float32
        )
        return (context.astype(jnp.bfloat16), row_max + jnp.log(row_total))

    return lax.map(forward_one_block, jnp.arange(SLOT // QB, dtype=jnp.int32))


def backward_slot(operands):
    slot_queries, slot_keys, slot_values, slot_context_grad, slot_log_totals, length = operands

    def backward_one_block(running, block_index):
        key_grad, value_grad = running
        row_start = block_index * QB
        block_queries = lax.dynamic_slice_in_dim(slot_queries, row_start, QB, 0)
        block_context_grad = lax.dynamic_slice_in_dim(slot_context_grad, row_start, QB, 0)
        block_log_total = slot_log_totals[block_index]
        scores, allowed = block_scores(block_queries, slot_keys, row_start, length)
        probs = jnp.where(allowed[None], jnp.exp(scores - block_log_total), 0.0)
        probs_grad = jnp.einsum(
            "qhd,khd->hqk", block_context_grad, slot_values, preferred_element_type=jnp.float32
        )
        row_inner = jnp.sum(probs * probs_grad, axis=-1, keepdims=True)
        score_grad = (probs * (probs_grad - row_inner)).astype(jnp.bfloat16)
        query_grad = 0.125 * jnp.einsum(
            "hqk,khd->qhd", score_grad, slot_keys, preferred_element_type=jnp.float32
        )
        key_grad = key_grad + 0.125 * jnp.einsum(
            "hqk,qhd->khd", score_grad, block_queries, preferred_element_type=jnp.float32
        )
        value_grad = value_grad + jnp.einsum(
            "hqk,qhd->khd",
            probs.astype(jnp.bfloat16),
            block_context_grad,
            preferred_element_type=jnp.float32,
        )
        return ((key_grad, value_grad), query_grad)

    zero_heads = jnp.zeros(slot_keys.shape, jnp.float32)
    (key_grad, value_grad), query_blocks = lax.scan(
        backward_one_block, (zero_heads, zero_heads), jnp.arange(SLOT // QB, dtype=jnp.int32)
    )
    return (query_blocks.reshape(slot_keys.shape), key_grad, value_grad)


def reorder_columns(matrix, first_count, second_count):
    total_columns = matrix.shape[-1]
    leading = matrix.shape[:-1]
    blocked = matrix.reshape(
        leading + (first_count, second_count, total_columns // (first_count * second_count))
    )
    return jnp.swapaxes(blocked, -3, -2).reshape(leading + (total_columns,))


def shards(
    layer_input,
    seq_lengths,
    out_grad,
    attn_gain,
    attn_shift,
    mlp_gain,
    mlp_shift,
    qkv_weight,
    qkv_bias,
    dense_weight,
    dense_bias,
    inner_weight,
    inner_bias,
    outer_weight,
    outer_bias,
):
    gathered = (
        lax.all_gather(attn_gain, "shard", axis=0, tiled=True),
        lax.all_gather(attn_shift, "shard", axis=0, tiled=True),
        lax.all_gather(mlp_gain, "shard", axis=0, tiled=True),
        lax.all_gather(mlp_shift, "shard", axis=0, tiled=True),
        lax.all_gather(qkv_weight, "shard", axis=0, tiled=True),
        lax.all_gather(qkv_bias, "shard", axis=0, tiled=True),
        lax.all_gather(dense_weight, "shard", axis=0, tiled=True),
        lax.all_gather(dense_bias, "shard", axis=0, tiled=True),
        lax.all_gather(inner_weight, "shard", axis=0, tiled=True),
        lax.all_gather(inner_bias, "shard", axis=0, tiled=True),
        lax.all_gather(outer_weight, "shard", axis=0, tiled=True),
        lax.all_gather(outer_bias, "shard", axis=0, tiled=True),
    )
    gathered = [member.astype(jnp.float32) if member.ndim == 1 else member for member in gathered]
    local_rows = layer_input.shape[0]
    slot_count = local_rows // SLOT
    head_shape = (slot_count, SLOT, H, HD)
    input_rows = layer_input.astype(jnp.float32)
    positions = jnp.arange(SLOT, dtype=jnp.int32)
    valid = (positions[None, :] < seq_lengths[:, None]).reshape(local_rows, 1)
    unit_rows, standard_pull = jax.vjp(standardize, input_rows)
    normed_attn = (unit_rows * gathered[0] + gathered[1]).astype(jnp.bfloat16)
    normed_mlp = (unit_rows * gathered[2] + gathered[3]).astype(jnp.bfloat16)
    projected = jnp.dot(normed_attn, gathered[4], preferred_element_type=jnp.float32) + gathered[5]
    cosine_table, sine_table = rotary_tables()
    queries = rotate(projected[:, :D].reshape(head_shape), cosine_table, sine_table).astype(
        jnp.bfloat16
    )
    key_heads = rotate(
        projected[:, D : 2 * D].reshape(head_shape), cosine_table, sine_table
    ).astype(jnp.bfloat16)
    value_heads = projected[:, 2 * D :].reshape(head_shape).astype(jnp.bfloat16)
    contexts, log_totals = lax.map(forward_slot, (queries, key_heads, value_heads, seq_lengths))
    context_rows = contexts.reshape(local_rows, D)
    inner = jnp.dot(normed_mlp, gathered[8], preferred_element_type=jnp.float32) + gathered[9]
    activated_float, gelu_pull = jax.vjp(exact_gelu, inner)
    activated = activated_float.astype(jnp.bfloat16)
    layer_output = (
        input_rows
        + jnp.dot(context_rows, gathered[6], preferred_element_type=jnp.float32)
        + gathered[7]
    )
    layer_output = (
        layer_output
        + jnp.dot(activated, gathered[10], preferred_element_type=jnp.float32)
        + gathered[11]
    )
    back_weights = (
        lax.all_gather(attn_gain, "shard", axis=0, tiled=True),
        lax.all_gather(mlp_gain, "shard", axis=0, tiled=True),
        lax.all_gather(qkv_weight, "shard", axis=0, tiled=True),
        lax.all_gather(dense_weight, "shard", axis=0, tiled=True),
        lax.all_gather(inner_weight, "shard", axis=0, tiled=True),
        lax.all_gather(outer_weight, "shard", axis=0, tiled=True),
    )
    back_weights = [
        member.astype(jnp.float32) if member.ndim == 1 else member for member in back_weights
    ]
    arrange = partial(
        reorder_columns, first_count=lax.axis_size("shard"), second_count=lax.axis_size("rep")
    )
    grad_rows = jnp.where(valid, out_grad, jnp.zeros_like(out_grad))
    grad_float = grad_rows.astype(jnp.float32)
    dense_bias_grad = arrange(jnp.sum(grad_float, axis=0))
    outer_bias_grad = dense_bias_grad
    dense_weight_grad = jnp.einsum(
        "tc,td->cd", arrange(context_rows), grad_rows, preferred_element_type=jnp.float32
    )
    outer_weight_grad = jnp.einsum(
        "tf,td->fd", arrange(activated), grad_rows, preferred_element_type=jnp.float32
    )
    context_grad = jnp.einsum(
        "td,cd->tc", grad_rows, back_weights[3], preferred_element_type=jnp.float32
    ).astype(jnp.bfloat16)
    activated_grad = jnp.einsum(
        "td,fd->tf", grad_rows, back_weights[5], preferred_element_type=jnp.float32
    )
    inner_grad = gelu_pull(activated_grad)[0].astype(jnp.bfloat16)
    inner_weight_grad = jnp.einsum(
        "tc,tf->cf", arrange(normed_mlp), inner_grad, preferred_element_type=jnp.float32
    )
    inner_bias_grad = arrange(jnp.sum(inner_grad, axis=0, dtype=jnp.float32))
    normed_mlp_grad = jnp.einsum(
        "tf,cf->tc", inner_grad, back_weights[4], preferred_element_type=jnp.float32
    )
    query_grads, key_grads, value_grads = lax.map(
        backward_slot,
        (
            queries,
            key_heads,
            value_heads,
            context_grad.reshape(head_shape),
            log_totals,
            seq_lengths,
        ),
    )
    projected_grad = jnp.concatenate(
        [
            rotate_back(query_grads, cosine_table, sine_table).reshape(local_rows, D),
            rotate_back(key_grads, cosine_table, sine_table).reshape(local_rows, D),
            value_grads.reshape(local_rows, D),
        ],
        axis=1,
    ).astype(jnp.bfloat16)
    qkv_weight_grad = jnp.einsum(
        "tc,te->ce", arrange(normed_attn), projected_grad, preferred_element_type=jnp.float32
    )
    qkv_bias_grad = arrange(jnp.sum(projected_grad, axis=0, dtype=jnp.float32))
    normed_attn_grad = jnp.einsum(
        "te,ce->tc", projected_grad, back_weights[2], preferred_element_type=jnp.float32
    )
    attn_gain_grad = arrange(jnp.sum(normed_attn_grad * unit_rows, axis=0))
    attn_shift_grad = arrange(jnp.sum(normed_attn_grad, axis=0))
    mlp_gain_grad = arrange(jnp.sum(normed_mlp_grad * unit_rows, axis=0))
    mlp_shift_grad = arrange(jnp.sum(normed_mlp_grad, axis=0))
    input_grad = (
        grad_float
        + standard_pull(normed_attn_grad * back_weights[0] + normed_mlp_grad * back_weights[1])[0]
    )
    (
        attn_gain_grad,
        attn_shift_grad,
        mlp_gain_grad,
        mlp_shift_grad,
        qkv_weight_grad,
        qkv_bias_grad,
        dense_weight_grad,
        dense_bias_grad,
        inner_weight_grad,
        inner_bias_grad,
        outer_weight_grad,
        outer_bias_grad,
    ) = (
        lax.psum_scatter(attn_gain_grad, ("rep", "shard"), scatter_dimension=0, tiled=True),
        lax.psum_scatter(attn_shift_grad, ("rep", "shard"), scatter_dimension=0, tiled=True),
        lax.psum_scatter(mlp_gain_grad, ("rep", "shard"), scatter_dimension=0, tiled=True),
        lax.psum_scatter(mlp_shift_grad, ("rep", "shard"), scatter_dimension=0, tiled=True),
        lax.psum_scatter(qkv_weight_grad, ("rep", "shard"), scatter_dimension=0, tiled=True),
        lax.psum_scatter(qkv_bias_grad, ("rep", "shard"), scatter_dimension=0, tiled=True),
        lax.psum_scatter(dense_weight_grad, ("rep", "shard"), scatter_dimension=0, tiled=True),
        lax.psum_scatter(dense_bias_grad, ("rep", "shard"), scatter_dimension=0, tiled=True),
        lax.psum_scatter(inner_weight_grad, ("rep", "shard"), scatter_dimension=0, tiled=True),
        lax.psum_scatter(inner_bias_grad, ("rep", "shard"), scatter_dimension=0, tiled=True),
        lax.psum_scatter(outer_weight_grad, ("rep", "shard"), scatter_dimension=0, tiled=True),
        lax.psum_scatter(outer_bias_grad, ("rep", "shard"), scatter_dimension=0, tiled=True),
    )
    (
        attn_gain_grad,
        attn_shift_grad,
        mlp_gain_grad,
        mlp_shift_grad,
        qkv_weight_grad,
        qkv_bias_grad,
        dense_weight_grad,
        dense_bias_grad,
        inner_weight_grad,
        inner_bias_grad,
        outer_weight_grad,
        outer_bias_grad,
    ) = (
        lax.all_gather(attn_gain_grad, "rep", axis=0, tiled=True),
        lax.all_gather(attn_shift_grad, "rep", axis=0, tiled=True),
        lax.all_gather(mlp_gain_grad, "rep", axis=0, tiled=True),
        lax.all_gather(mlp_shift_grad, "rep", axis=0, tiled=True),
        lax.all_gather(qkv_weight_grad, "rep", axis=0, tiled=True),
        lax.all_gather(qkv_bias_grad, "rep", axis=0, tiled=True),
        lax.all_gather(dense_weight_grad, "rep", axis=0, tiled=True),
        lax.all_gather(dense_bias_grad, "rep", axis=0, tiled=True),
        lax.all_gather(inner_weight_grad, "rep", axis=0, tiled=True),
        lax.all_gather(inner_bias_grad, "rep", axis=0, tiled=True),
        lax.all_gather(outer_weight_grad, "rep", axis=0, tiled=True),
        lax.all_gather(outer_bias_grad, "rep", axis=0, tiled=True),
    )
    return (
        layer_output,
        input_grad,
        attn_gain_grad,
        attn_shift_grad,
        mlp_gain_grad,
        mlp_shift_grad,
        qkv_weight_grad,
        qkv_bias_grad,
        dense_weight_grad,
        dense_bias_grad,
        inner_weight_grad,
        inner_bias_grad,
        outer_weight_grad,
        outer_bias_grad,
    )


def solution(mesh):
    return jax.shard_map(
        shards,
        mesh=mesh,
        in_specs=(
            P(("rep", "shard"), None),
            P(("rep", "shard")),
            P(("rep", "shard"), None),
            P("shard"),
            P("shard"),
            P("shard"),
            P("shard"),
            P("shard", None),
            P("shard"),
            P("shard", None),
            P("shard"),
            P("shard", None),
            P("shard"),
            P("shard", None),
            P("shard"),
        ),
        out_specs=(
            P(("rep", "shard"), None),
            P(("rep", "shard"), None),
            P("shard"),
            P("shard"),
            P("shard"),
            P("shard"),
            P("shard", None),
            P("shard"),
            P("shard", None),
            P("shard"),
            P("shard", None),
            P("shard"),
            P("shard", None),
            P("shard"),
        ),
        check_vma=False,
    )
```

profile of v0, /device:TPU:0, one launch (start us, length us, event | category | flops | bytes accessed | tf_op | source)
XLA Modules:
  0.0 1664.3 jit_solution(14028715483818204317)
XLA Ops:
  83.6 36.5 %all-gather.17.cloned.1.call-done = bf16[1024,3072]{1,0:T(8,128)(2,1)} async-done(((bf16[256,3072]{1,0:T(8,128)(2,1)}), bf16[1024,3072]{1,0:T(8,128)(2,1)}) %all-gather.17.cloned.1.call-update) | async-done | bytes 6291472 | tf_op jit(solution)/shard_map/all_gather | solution.py:160
  154.6 99.3 %while.47 = (s32[]{:T(128)}, bf16[2,512,16,64]{1,3,2,0:T(8,128)(2,1)}, f32[2,16,512,1]{2,1,3,0:T(8,128)S(1)}, s32[2]{0:T(128)S(1)}, s32[]{:T(128)}, /*index=5*/b...) while((s32[]{:T(128)}, ...), condition=%wide.region_5.6_spmd, body=%wide.region_2.5_spmd.sunk | while | flops 2249713152 | bytes 117709528 | solution.py:89
  157.5 16.2 fusion.124
  173.8 15.0 fusion.125
  188.9 15.2 fusion.126
  206.4 17.2 %fusion.124 = (f32[16,512]{1,0:T(8,128)S(1)}, f32[16,512,1024]{2,1,0:T(8,128)}) fusion(pred[512,1024]{1,0:T(8,128)(4,1)S(1)} %fusion.123, bf16[1024,16,64]{0,2,1:T(8,128)(2,1)S(1)} %get-tuple-element.469, bf16[1024,16,64]{0,2,1:T(8,128)(2,1)} %get-tuple-element.468, s32[]{:T(128)S(6)} %select_n.76), kind=kOutput, calls=%fused_computation.3.clone.1 | convolution fusion | flops 1098899456 | bytes 37257220 | tf_op jit(solution)/shard_map/while/body/eval_jaxpr/while/body/eval_jaxpr/qhd,khd->hqk/dot_general | solution.py:65
  223.7 15.0 fusion.125
  238.7 15.2 fusion.126
  270.2 304.4 %while.48 = (s32[]{:T(128)}, f32[1024,16,64]{0,2,1:T(8,128)}, f32[1024,16,64]{0,2,1:T(8,128)}, f32[2,512,16,64]{1,0,3,2:T(2,128)}, s32[2]{0:T(128)S(1)}, /*index...) while((s32[]{:T(128)}, f32[1024,16,64]{0,2,1:T(8,128)}, ...), condition=%wide.region_8.9_spmd.clone, body=%wide.region_6.8_spmd.clone.sunk | while | flops 5501347328 | bytes 291739904 | solution.py:123
  271.7 14.4 fusion.136
  289.2 26.0 %multiply_reduce_fusion.2 = (f32[16,512]{1,0:T(8,128)S(1)}, f32[16,512,1024]{2,1,0:T(8,128)}) fusion(f32[16,512,1024]{2,1,0:T(8,128)} %fusion.136, f32[16,512]{1,0:T(8,128)S(1)} %dynamic-slice_bitcast_fusion.3, pred[512,1024]{1,0:T(8,128)(4,1)S(1)} %fusion.137, bf16[1024,16,64]{0,2,1:T(8,128)(2,1)} %get-tuple-element.517, ...), kind=kOutput, calls=%fused_computation.20.clone.1 | convolution fusion | flops 1115676672 | bytes 70844416 | tf_op jit(solution)/shard_map/while/body/eval_jaxpr/while/body/eval_jaxpr/qhd,khd->hqk/dot_general | solution.py:103
  315.2 27.8 %multiply_convert_fusion.3 = bf16[16,512,1024]{2,1,0:T(8,128)(2,1)} fusion(f32[16,512,1024]{2,1,0:T(8,128)} %get-tuple-element.437, f32[16,512,1024]{2,1,0:T(8,128)} %fusion.136, f32[16,512]{1,0:T(8,128)S(1)} %get-tuple-element.438, f32[16,512]{1,0:T(8,128)S(1)} %dynamic-slice_bitcast_fusion.3, pred[512,1024]{1,0:T(8,128)(4,1)S(1)} %fusion.137), kind=kLoop, calls=%fused_computation.19.clone.1 | loop fusion | flops 50331648 | bytes 84475904 | tf_op jit(solution)/shard_map/while/body/eval_jaxpr/while/body/eval_jaxpr/convert_element_type | solution.py:107
  355.2 38.0 %dynamic_update_slice.33 = f32[2,512,16,64]{1,0,3,2:T(2,128)} dynamic-update-slice(f32[2,512,16,64]{1,0,3,2:T(2,128)} %get-tuple-element.494, f32[1,512,16,64]{1,0,3,2:T(1,128)} %copy.114, s32[]{:T(128)} %get-tuple-element.491, s32[]{:T(128)} %constant.72.clone.1..sunk.1, s32[]{:T(128)} %constant.72.clone.1..sunk.1, s32[]{:T(128)} %constant.72.clone.1..sunk.1) | dynamic-update-slice | bytes 4194308 | tf_op jit(solution)/shard_map/while/body/eval_jaxpr/while/body/jit(dynamic_update_index_in_dim)/dynamic_update_slice | solution.py:123
  404.4 16.9 %bitcast_add_fusion.6 = f32[1024,16,64]{0,2,1:T(8,128)} fusion(f32[1024,16,64]{0,2,1:T(8,128)} %get-tuple-element.493, f32[16,512,1024]{2,1,0:T(8,128)} %fusion.136, f32[16,512]{1,0:T(8,128)S(1)} %dynamic-slice_bitcast_fusion.3, pred[512,1024]{1,0:T(8,128)(4,1)S(1)} %fusion.137, pred[]{:T(512)S(6)} %compare.5, ...), kind=kOutput, calls=%fused_computation.25.clone.1 | convolution fusion | flops 1109393408 | bytes 43548676 | tf_op jit(solution)/shard_map/while/body/eval_jaxpr/while/body/eval_jaxpr/hqk,qhd->khd/dot_general | solution.py:114
  422.5 14.5 fusion.136
  440.1 26.1 %multiply_reduce_fusion.2 = (f32[16,512]{1,0:T(8,128)S(1)}, f32[16,512,1024]{2,1,0:T(8,128)}) fusion(f32[16,512,1024]{2,1,0:T(8,128)} %fusion.136, f32[16,512]{1,0:T(8,128)S(1)} %dynamic-slice_bitcast_fusion.3, pred[512,1024]{1,0:T(8,128)(4,1)S(1)} %fusion.137, bf16[1024,16,64]{0,2,1:T(8,128)(2,1)} %get-tuple-element.517, ...), kind=kOutput, calls=%fused_computation.20.clone.1 | convolution fusion | flops 1115676672 | bytes 70844416 | tf_op jit(solution)/shard_map/while/body/eval_jaxpr/while/body/eval_jaxpr/qhd,khd->hqk/dot_general | solution.py:103
  466.2 27.6 %multiply_convert_fusion.3 = bf16[16,512,1024]{2,1,0:T(8,128)(2,1)} fusion(f32[16,512,1024]{2,1,0:T(8,128)} %get-tuple-element.437, f32[16,512,1024]{2,1,0:T(8,128)} %fusion.136, f32[16,512]{1,0:T(8,128)S(1)} %get-tuple-element.438, f32[16,512]{1,0:T(8,128)S(1)} %dynamic-slice_bitcast_fusion.3, pred[512,1024]{1,0:T(8,128)(4,1)S(1)} %fusion.137), kind=kLoop, calls=%fused_computation.19.clone.1 | loop fusion | flops 50331648 | bytes 84475904 | tf_op jit(solution)/shard_map/while/body/eval_jaxpr/while/body/eval_jaxpr/convert_element_type | solution.py:107
  506.0 38.0 %dynamic_update_slice.33 = f32[2,512,16,64]{1,0,3,2:T(2,128)} dynamic-update-slice(f32[2,512,16,64]{1,0,3,2:T(2,128)} %get-tuple-element.494, f32[1,512,16,64]{1,0,3,2:T(1,128)} %copy.114, s32[]{:T(128)} %get-tuple-element.491, s32[]{:T(128)} %constant.72.clone.1..sunk.1, s32[]{:T(128)} %constant.72.clone.1..sunk.1, s32[]{:T(128)} %constant.72.clone.1..sunk.1) | dynamic-update-slice | bytes 4194308 | tf_op jit(solution)/shard_map/while/body/eval_jaxpr/while/body/jit(dynamic_update_index_in_dim)/dynamic_update_slice | solution.py:123
  556.3 18.0 %bitcast_add_fusion.6 = f32[1024,16,64]{0,2,1:T(8,128)} fusion(f32[1024,16,64]{0,2,1:T(8,128)} %get-tuple-element.493, f32[16,512,1024]{2,1,0:T(8,128)} %fusion.136, f32[16,512]{1,0:T(8,128)S(1)} %dynamic-slice_bitcast_fusion.3, pred[512,1024]{1,0:T(8,128)(4,1)S(1)} %fusion.137, pred[]{:T(512)S(6)} %compare.5, ...), kind=kOutput, calls=%fused_computation.25.clone.1 | convolution fusion | flops 1109393408 | bytes 43548676 | tf_op jit(solution)/shard_map/while/body/eval_jaxpr/while/body/eval_jaxpr/hqk,qhd->khd/dot_general | solution.py:114
  593.8 13.2 fusion.68
  608.5 47.7 %multiply_convert_fusion.1 = (bf16[1024,4096]{1,0:T(8,128)(2,1)}, f32[1024,4096]{1,0:T(8,128)}, f32[1024,4096]{1,0:T(8,128)}) fusion(f32[4096]{0:T(1024)S(1)} %copy-done.40, bf16[1024,1024]{1,0:T(8,128)(2,1)S(1)} %copy-done.10, bf16[1024,4096]{1,0:T(8,128)(2,1)} %all-gather.21.cloned.1.call-done), kind=kOutput, calls=%fused_computation.49 | convolution fusion | flops 8866758656 | bytes 52445184 | tf_op jit(solution)/shard_map/dot_general | solution.py:190
  656.2 24.1 %convert_reduce_fusion = (f32[4096]{0:T(1024)S(1)}, bf16[1024,4096]{1,0:T(8,128)(2,1)}) fusion(f32[1024,4096]{1,0:T(8,128)} %get-tuple-element.286, bf16[4096,1024]{1,0:T(8,128)(2,1)} %all-gather.23.cloned.1.call-done, bf16[1024,1024]{1,0:T(8,128)(2,1)} %param.21, pred[1024]{0:T(1024)(128)(4,1)S(1)} %copy-done.47, f32[1024,4096]{1,0:T(8,128)} %get-tuple-element.309, ...), kind=kOutput, calls=%fused_computation.47 | convolution fusion | flops 8662282240 | bytes 52462592 | tf_op jit(solution)/shard_map/td,fd->tf/dot_general | solution.py:230
  680.4 14.8 fusion.78
  717.4 14.9 fusion.70
  733.1 30.3 %reduce-scatter.5.cloned.1.call-done = f32[32,3072]{1,0:T(8,128)} async-done(((f32[1024,3072]{1,0:T(8,128)}), f32[32,3072]{1,0:T(8,128)}) %reduce-scatter.5.cloned.1.call-update) | async-done | bytes 393232 | tf_op jit(solution)/shard_map/reduce_scatter | solution.py:293
  763.4 359.0 %reduce-scatter.9.cloned.1.call-done = f32[32,4096]{1,0:T(8,128)} async-done(((f32[1024,4096]{1,0:T(8,128)}), f32[32,4096]{1,0:T(8,128)}) %reduce-scatter.9.cloned.1.call-update) | async-done | bytes 524304 | tf_op jit(solution)/shard_map/reduce_scatter | solution.py:297
  1155.9 328.1 %reduce-scatter.11.cloned.1.call-done = f32[128,1024]{1,0:T(8,128)} async-done(((f32[4096,1024]{1,0:T(8,128)}), f32[128,1024]{1,0:T(8,128)}) %reduce-scatter.11.cloned.1.call-update) | async-done | bytes 524304 | tf_op jit(solution)/shard_map/reduce_scatter | solution.py:299
  1488.6 15.9 fusion.50
  1510.3 44.0 %all-reduce.15 = (f32[1024]{0:T(1024)S(1)}, f32[1024]{0:T(1024)S(1)}, f32[1024]{0:T(1024)S(1)}, f32[1024]{0:T(1024)S(1)}, f32[3072]{0:T(1024)S(1)}, /*index=5*/f32[1024]{0:T(1024)S(1)}, f32[4096]{0:T(1024)S(1)}) all-reduce(f32[1024]{0:T(1024)S(1)} %reshape.377, ...), channel_id=2, replica_groups=mesh['rep'=8,'shard'=4] {'rep','shard'}, use_global_device_ids=true, to_apply=%region_12.13.clone | all-reduce | flops 12288 | bytes 98304
  1555.2 15.5 all-reduce.16
  1579.3 15.8 fusion.55
  1598.4 47.6 %all-gather.31.cloned.1.call-done = f32[1024,1024]{1,0:T(8,128)} async-done(((f32[128,1024]{1,0:T(8,128)}), f32[1024,1024]{1,0:T(8,128)}) %all-gather.31.cloned.1.call-update) | async-done | bytes 4194320 | tf_op jit(solution)/shard_map/all_gather | solution.py:326
  (298 shorter events, 290.7 us)
Async XLA Ops:
  7.2 70.3 %all-gather.19.cloned.1.call-start = ((), (), s32[]{:S(2)}) async-start(), calls=%async_computation.5 | async-start | bytes 2621440 | tf_op jit(solution)/shard_map/all_gather | solution.py:162
  7.9 112.2 %all-gather.17.cloned.1.call-start = ((), (), s32[]{:S(2)}) async-start(), calls=%async_computation.4 | async-start | bytes 7864320 | tf_op jit(solution)/shard_map/all_gather | solution.py:160
  8.7 35.3 %copy-start.44 = (bf16[768]{0:T(1024)(128)(2,1)S(1)}, bf16[768]{0:T(1024)(128)(2,1)}, u32[]{:S(2)}) copy-start(bf16[768]{0:T(1024)(128)(2,1)} %param.27) | copy-start | bytes 4612
  8.7 598.3 %all-gather.21.cloned.1.call-start = ((), (), s32[]{:S(2)}) async-start(), calls=%async_computation.6 | async-start | bytes 10485760 | tf_op jit(solution)/shard_map/all_gather | solution.py:164
  9.5 646.8 %all-gather.23.cloned.1.call-start = ((), (), s32[]{:S(2)}) async-start(), calls=%async_computation.7 | async-start | bytes 10485760 | tf_op jit(solution)/shard_map/all_gather | solution.py:166
  10.0 722.3 %reduce-scatter.7.cloned.1.call-start = ((), (), s32[]{:S(2)}) async-start(), calls=%async_computation.10 | async-start | bytes 4325376 | tf_op jit(solution)/shard_map/reduce_scatter | solution.py:295
  10.5 44.4 %copy-start.30 = (f32[1024]{0:T(1024)}, f32[1024]{0:T(1024)S(1)}, u32[]{:S(2)}) copy-start(f32[1024]{0:T(1024)S(1)} %broadcast_multiply_fusion.1) | copy-start | bytes 12292
  11.2 48.0 %copy-start.34 = (f32[1024]{0:T(1024)}, f32[1024]{0:T(1024)S(1)}, u32[]{:S(2)}) copy-start(f32[1024]{0:T(1024)S(1)} %fusion.67) | copy-start | bytes 12292
  20.8 38.4 %copy-start.36 = (f32[4,1,256]{2,1,0:T(1,128)}, f32[4,1,256]{2,1,0:T(1,128)S(1)}, u32[]{:S(2)}) copy-start(f32[4,1,256]{2,1,0:T(1,128)S(1)} %convert_element_type.112) | copy-start | bytes 12292
  77.3 71.9 %copy-start.16 = (f32[1024,64]{0,1:T(8,128)}, f32[1024,64]{0,1:T(8,128)S(1)}, u32[]{:S(2)}) copy-start(f32[1024,64]{0,1:T(8,128)S(1)} %concatenate.58) | copy-start | bytes 786436
  77.3 71.8 %copy-start.18 = (f32[1024,64]{0,1:T(8,128)}, f32[1024,64]{0,1:T(8,128)S(1)}, u32[]{:S(2)}) copy-start(f32[1024,64]{0,1:T(8,128)S(1)} %concatenate.53) | copy-start | bytes 786436
  77.4 71.8 %copy-start.41 = (f32[64]{0:T(128)}, f32[64]{0:T(128)S(1)}, u32[]{:S(2)}) copy-start(f32[64]{0:T(128)S(1)} %pad.16.clone) | copy-start | bytes 772
  77.4 42.7 %copy-start.11 = (bf16[1024,1024]{1,0:T(8,128)(2,1)S(1)}, bf16[1024,1024]{1,0:T(8,128)(2,1)}, u32[]{:S(2)}) copy-start(bf16[1024,1024]{1,0:T(8,128)(2,1)} %get-tuple-element.302) | copy-start | bytes 6291460
  270.2 493.1 %reduce-scatter.5.cloned.1.call-start = ((), (), s32[]{:S(2)}) async-start(), calls=%async_computation.8 | async-start | bytes 12976128 | tf_op jit(solution)/shard_map/reduce_scatter | solution.py:293
  607.0 49.3 %copy-start.47 = (pred[1024]{0:T(1024)(128)(4,1)S(1)}, pred[1024]{0:T(1024)(128)(4,1)}, u32[]{:S(2)}) copy-start(pred[1024]{0:T(1024)(128)(4,1)} %copy-done.45) | copy-start | bytes 3076
  607.0 515.5 %reduce-scatter.9.cloned.1.call-start = ((), (), s32[]{:S(2)}) async-start(), calls=%async_computation.12 | async-start | bytes 17301504 | tf_op jit(solution)/shard_map/reduce_scatter | solution.py:297
  695.2 788.8 %reduce-scatter.11.cloned.1.call-start = ((), (), s32[]{:S(2)}) async-start(), calls=%async_computation.14 | async-start | bytes 17301504 | tf_op jit(solution)/shard_map/reduce_scatter | solution.py:299
  732.2 390.3 %copy-start.56 = (u32[32]{0:T(128)S(1)}, u32[32]{0:T(128)}, u32[]{:S(2)}) copy-start(u32[32]{0:T(128)} %constant.173) | copy-start | bytes 388
  732.2 392.2 %copy-start.54 = (bf16[256]{0:T(256)(128)(2,1)S(1)}, bf16[256]{0:T(256)(128)(2,1)}, u32[]{:S(2)}) copy-start(bf16[256]{0:T(256)(128)(2,1)} %param.29) | copy-start | bytes 1540
  732.2 400.1 %copy-start.55 = (bf16[256]{0:T(256)(128)(2,1)S(1)}, bf16[256]{0:T(256)(128)(2,1)}, u32[]{:S(2)}) copy-start(bf16[256]{0:T(256)(128)(2,1)} %param.33) | copy-start | bytes 1540
  732.2 408.4 %copy-start.5 = (bf16[2,512,16,64]{1,0,3,2:T(2,128)(2,1)S(1)}, bf16[2,512,16,64]{1,0,3,2:T(2,128)(2,1)}, u32[]{:S(2)}) copy-start(bf16[2,512,16,64]{1,0,3,2:T(2,128)(2,1)} %copy.79) | copy-start | bytes 6291460
  732.3 862.9 %all-gather.27.cloned.1.call-start = ((), (), s32[]{:S(2)}) async-start(), calls=%async_computation.11 | async-start | bytes 1179648 | tf_op jit(solution)/shard_map/all_gather | solution.py:322
  733.0 862.1 %all-gather.25.cloned.1.call-start = ((), (), s32[]{:S(2)}) async-start(), calls=%async_computation.9 | async-start | bytes 3538944 | tf_op jit(solution)/shard_map/all_gather | solution.py:320
  763.4 835.0 %all-gather.29.cloned.1.call-start = ((), (), s32[]{:S(2)}) async-start(), calls=%async_computation.13 | async-start | bytes 4718592 | tf_op jit(solution)/shard_map/all_gather | solution.py:324
  1122.5 523.5 %all-gather.31.cloned.1.call-start = ((), (), s32[]{:S(2)}) async-start(), calls=%async_computation.15 | async-start | bytes 4718592 | tf_op jit(solution)/shard_map/all_gather | solution.py:326
  1155.9 332.7 %copy-start.3 = (bf16[1024,1024]{1,0:T(8,128)(2,1)S(1)}, bf16[1024,1024]{1,0:T(8,128)(2,1)}, u32[]{:S(2)}) copy-start(bf16[1024,1024]{1,0:T(8,128)(2,1)} %param.19) | copy-start | bytes 6291460
  1155.9 332.7 %copy-start.31 = (f32[1024]{0:T(1024)S(1)}, f32[1024]{0:T(1024)}, u32[]{:S(2)}) copy-start(f32[1024]{0:T(1024)} %copy-done.30) | copy-start | bytes 12292
  1155.9 332.7 %copy-start.35 = (f32[1024]{0:T(1024)S(1)}, f32[1024]{0:T(1024)}, u32[]{:S(2)}) copy-start(f32[1024]{0:T(1024)} %copy-done.34) | copy-start | bytes 12292
  1155.9 332.7 %copy-start.37 = (f32[4,1,256]{2,1,0:T(1,128)S(1)}, f32[4,1,256]{2,1,0:T(1,128)}, u32[]{:S(2)}) copy-start(f32[4,1,256]{2,1,0:T(1,128)} %copy-done.36) | copy-start | bytes 12292
  1155.9 332.7 %copy-start.39 = (f32[4,1,256]{2,1,0:T(1,128)S(1)}, f32[4,1,256]{2,1,0:T(1,128)}, u32[]{:S(2)}) copy-start(f32[4,1,256]{2,1,0:T(1,128)} %copy-done.38) | copy-start | bytes 12292
  1570.7 75.3 %copy-start.48 = (f32[256]{0:T(256)}, f32[256]{0:T(256)S(1)}, u32[]{:S(2)}) copy-start(f32[256]{0:T(256)S(1)} %get-tuple-element.574) | copy-start | bytes 3076
  1595.1 55.5 %copy-start.29 = (f32[256,1024]{1,0:T(8,128)S(1)}, f32[256,1024]{1,0:T(8,128)}, u32[]{:S(2)}) copy-start(f32[256,1024]{1,0:T(8,128)} %all-gather.27.cloned.1.call-done) | copy-start | bytes 3145732
  (40 other events, 367.6 us)
Sparse Core Ops, SparseCore 0:
  9.9 38.1 all-gather.18
  49.9 70.1 all-gather.16
  122.0 87.6 all-gather.20
  211.3 87.6 all-gather.22
  301.7 141.3 reduce-scatter.6
  607.1 156.2 reduce-scatter.4
  765.7 356.6 reduce-scatter.8
  1124.8 359.1 reduce-scatter.10
  1485.7 23.5 all-gather.26
  1510.8 38.9 all-gather.24
  1551.5 46.8 all-gather.28
  1599.9 46.0 all-gather.30
where the time goes:
time: 1670 us; the launch traced here: 1660 us
  waiting for transfers between devices  808 us (48%)
  matrix products  400 us (24%)
  local copies, waits for them, and re-layouts  184 us (11%)
  blocking collectives  132 us (8%)
  other arithmetic  115 us (7%)
  between operations  17.2 us (1%)
    reduce_scatter x1, waiting for transfers between devices, shards(): lax.psum_scatter(inner_weight_grad, ('rep', 'shard'), scatter_dimension=0...  359 us
    reduce_scatter x1, waiting for transfers between devices, shards(): lax.psum_scatter(outer_weight_grad, ('rep', 'shard'), scatter_dimension=0...  328 us
    dynamic_update_slice x4, local copies, waits for them, and re-layouts, backward_slot(): lax.scan(backward_one_block, (zero_heads, zero_heads), jnp.arange(SLOT //...  82.9 us
    dot_general x4, matrix products, block_scores(): jnp.einsum('qhd,khd->hqk', block_queries, slot_keys, preferred_element_ty...  62.4 us
    unnamed x2, blocking collectives  59.4 us
    convert_element_type x2, other arithmetic, backward_one_block(): score_grad = (probs * (probs_grad - row_inner)).astype(jnp.bfloat16)  55.5 us
    dot_general x2, matrix products, backward_one_block(): jnp.einsum('qhd,khd->hqk', block_context_grad, slot_values, preferred_ele...  52.1 us
    dot_general x1, matrix products, shards(): jnp.dot(normed_mlp, gathered[8], preferred_element_type=jnp.float32)  47.7 us
  transfers between devices with their start and end apart: 12, of which 6 were waited for; matrix products, arithmetic and copies ran while one was open for 41% of the time, Pallas kernels for 0%

commit v1 on v0

v1 whole, which is shorter than its diff:
```python
import functools

import jax
import jax.numpy as jnp
import numpy as np
from jax import lax
from jax.experimental import pallas as pl
from jax.experimental.pallas import tpu as pltpu
from jax.sharding import Mesh, PartitionSpec as P

D = 1024
H = 16
FF = 4096
HD = 64
ROT = 16
T = 1024
GROUP = 256
HEADS = GROUP // HD
ROWS = 256
EPSILON = 1e-05
MASKED = -1e30
BF = jnp.bfloat16
F32 = jnp.float32
VMEM = 60 * 2**20


def nn(a, b):
    return lax.dot_general(a, b, (((1,), (0,)), ((), ())), preferred_element_type=F32)


def nt(a, b):
    return lax.dot_general(a, b, (((1,), (1,)), ((), ())), preferred_element_type=F32)


def tn(a, b):
    return lax.dot_general(a, b, (((0,), (0,)), ((), ())), preferred_element_type=F32)


def rows_of(index, size):
    return slice(index * size, (index + 1) * size)


def rotary_tables():
    half = ROT // 2
    inverse = 1.0 / np.float32(10000.0) ** (np.arange(half, dtype=np.float32) * np.float32(2.0 / ROT))
    angles = np.arange(T, dtype=np.float32)[:, None] * inverse.astype(np.float32)[None, :]
    cosine = np.ones((T, HD), np.float32)
    ahead = np.zeros((T, HD), np.float32)
    behind = np.zeros((T, HD), np.float32)
    cosine[:, :half] = np.cos(angles)
    cosine[:, half:ROT] = np.cos(angles)
    ahead[:, :half] = -np.sin(angles)
    behind[:, half:ROT] = np.sin(angles)
    return [np.tile(table, (1, 2)) for table in (cosine, ahead, behind)]


def add_columns(ref, rows, value, order):
    width = value.shape[1] // len(order)
    for place, block in enumerate(order):
        ref[rows, rows_of(block, width)] += value[:, rows_of(place, width)]


def mlp_kernel(order, nm, gr, wi, bi, wo, out, dn, gwi, gwo, gbi, act, ig):
    @pl.when(pl.program_id(0) == 0)
    def _():
        out[...] = jnp.zeros_like(out)
        dn[...] = jnp.zeros_like(dn)

    bias_sum = jnp.zeros(gbi.shape, F32)
    for t in range(T // ROWS):
        r = rows_of(t, ROWS)
        inner = nn(nm[r, :], wi[...]) + bi[...]
        grad = nt(gr[r, :], wo[...])
        normal = 0.5 * lax.erf(inner * 0.7071067811865476) + 0.5
        slope = normal + inner * jnp.exp(-0.5 * inner * inner) * 0.3989422804014327
        act[r, :] = (inner * normal).astype(BF)
        inner_grad = (grad * slope).astype(BF)
        ig[r, :] = inner_grad
        bias_sum += jnp.sum(inner_grad.astype(F32), axis=0, keepdims=True)
    gbi[...] = bias_sum
    for t in range(T // ROWS):
        r = rows_of(t, ROWS)
        out[r, :] += nn(act[r, :], wo[...])
        add_columns(dn, r, nt(ig[r, :], wi[...]), order)
    for d in range(D // ROWS):
        r = rows_of(d, ROWS)
        gwi[r, :] = tn(nm[:, r], ig[...]).astype(BF)
    step = min(ROWS, act.shape[1])
    for f in range(act.shape[1] // step):
        r = rows_of(f, step)
        gwo[r, :] = tn(act[:, r], gr[...]).astype(BF)


def mlp(order, nm, gr, wi, bi, wo):
    tile = FF // len(order)
    half = len(order) // 2
    one = pl.Buffered(1)
    whole = lambda: pl.BlockSpec((T, D), lambda i: (0, 0), pipeline_mode=one)
    total = lambda: pl.BlockSpec((T, D), lambda i: (0, 0))
    columns = lambda rows: pl.BlockSpec((rows, tile), lambda i: (0, (i % half) * 2 + i // half))
    return pl.pallas_call(
        functools.partial(mlp_kernel, order),
        grid=(FF // tile,),
        in_specs=[whole(), whole(), columns(D), columns(1), pl.BlockSpec((tile, D), lambda i: (i, 0))],
        out_specs=[total(), total(), columns(D), pl.BlockSpec((tile, D), lambda i: (i, 0)), columns(1)],
        out_shape=[
            jax.ShapeDtypeStruct((T, D), F32),
            jax.ShapeDtypeStruct((T, D), F32),
            jax.ShapeDtypeStruct((D, FF), BF),
            jax.ShapeDtypeStruct((FF, D), BF),
            jax.ShapeDtypeStruct((1, FF), F32),
        ],
        scratch_shapes=[pltpu.VMEM((T, tile), BF), pltpu.VMEM((T, tile), BF)],
        compiler_params=pltpu.CompilerParams(vmem_limit_bytes=VMEM),
        cost_estimate=pl.CostEstimate(flops=12 * T * D * FF, bytes_accessed=60 * 2**20, transcendentals=2 * T * FF),
        name="mlp",
    )(nm, gr, wi, bi, wo)


def attn_kernel(
    order, length, na, gr, wq, wk, wv, bq, bk, bv, wd, cosine, ahead, behind,
    out, dn, gwq, gwk, gwv, gwd, gb,
    q, k, v, dc, ctx, dq, dk, dv, grads,
):
    @pl.when(pl.program_id(0) == 0)
    def _():
        out[...] = jnp.zeros_like(out)
        dn[...] = jnp.zeros_like(dn)

    def turn(x, r, back):
        parts = []
        for p in range(GROUP // 128):
            pair = x[:, rows_of(p, 128)]
            straight = pair * cosine[r, :]
            across = (
                pltpu.roll(pair, 128 - ROT // 2, 1) * ahead[r, :]
                + pltpu.roll(pair, ROT // 2, 1) * behind[r, :]
            )
            parts.append(straight - across if back else straight + across)
        return jnp.concatenate(parts, axis=1)

    for t in range(T // ROWS):
        r = rows_of(t, ROWS)
        x = na[r, :]
        queries = (turn(nn(x, wq[...]) + bq[...], r, False).astype(BF) * 0.125).astype(BF)
        keys = turn(nn(x, wk[...]) + bk[...], r, False).astype(BF)
        values = (nn(x, wv[...]) + bv[...]).astype(BF)
        context_grad = nt(gr[r, :], wd[...]).astype(BF)
        for h in range(HEADS):
            c = rows_of(h, HD)
            q[h, r, :] = queries[:, c]
            k[h, r, :] = keys[:, c]
            v[h, r, :] = values[:, c]
            dc[h, r, :] = context_grad[:, c]

    block = 256
    inside = lax.broadcasted_iota(jnp.int32, (1, T), 1) < length[0]
    bias = jnp.where(inside, 0.0, MASKED).astype(F32)
    below = lax.broadcasted_iota(jnp.int32, (block, block), 1) <= lax.broadcasted_iota(jnp.int32, (block, block), 0)
    causal = jnp.where(below, 0.0, MASKED).astype(F32)

    def head(h, carry):
        dk[h] = jnp.zeros((T, HD), F32)
        dv[h] = jnp.zeros((T, HD), F32)
        for i in range(T // block):
            r = rows_of(i, block)
            spans = ([slice(0, i * block)] if i else []) + [r]
            query = q[h, r, :]
            scores = [nt(query, k[h, c, :]) + bias[:, c] for c in spans]
            scores[-1] += causal
            top = functools.reduce(jnp.maximum, [jnp.max(s, axis=1, keepdims=True) for s in scores])
            weights = [jnp.exp(s - top) for s in scores]
            scale = 1.0 / sum(jnp.sum(w, axis=1, keepdims=True) for w in weights)
            low = [w.astype(BF) for w in weights]
            context = sum(nn(w, v[h, c, :]) for w, c in zip(low, spans))
            ctx[h, r, :] = (context * scale).astype(BF)
            scaled_grad = (dc[h, r, :].astype(F32) * scale).astype(BF)
            probs_grad = [nt(scaled_grad, v[h, c, :]) for c in spans]
            inner = scale * sum(jnp.sum(w * p, axis=1, keepdims=True) for w, p in zip(weights, probs_grad))
            score_grad = [(w * (p - inner)).astype(BF) for w, p in zip(weights, probs_grad)]
            dq[h, r, :] = sum(nn(s, k[h, c, :]) for s, c in zip(score_grad, spans))
            for s, w, c in zip(score_grad, low, spans):
                dk[h, c, :] += tn(s, query)
                dv[h, c, :] += tn(w, scaled_grad)
        return carry

    lax.fori_loop(0, HEADS, head, 0)

    sums = [jnp.zeros((1, GROUP), F32) for _ in range(3)]
    together = lambda ref, r: jnp.concatenate([ref[h, r, :] for h in range(HEADS)], axis=1)
    for t in range(T // ROWS):
        r = rows_of(t, ROWS)
        context = together(ctx, r)
        grads[r, 3 * GROUP :] = context
        out[r, :] += nn(context, wd[...])
        pieces = (
            turn(together(dq, r) * 0.125, r, True).astype(BF),
            turn(together(dk, r), r, True).astype(BF),
            together(dv, r).astype(BF),
        )
        for p, piece in enumerate(pieces):
            grads[r, rows_of(p, GROUP)] = piece
            sums[p] += jnp.sum(piece.astype(F32), axis=0, keepdims=True)
        normed_grad = sum(nt(piece, w[...]) for piece, w in zip(pieces, (wq, wk, wv)))
        add_columns(dn, r, normed_grad, order)
    for p in range(3):
        gb[p : p + 1, :] = sums[p]
    for d in range(D // ROWS):
        r = rows_of(d, ROWS)
        x = na[:, r]
        for p, g in enumerate((gwq, gwk, gwv)):
            g[r, :] = tn(x, grads[:, rows_of(p, GROUP)]).astype(BF)
    gwd[...] = tn(grads[:, 3 * GROUP :], gr[...]).astype(BF)


def attn(order, length, na, gr, weight, bias, wd):
    groups = D // GROUP
    one = pl.Buffered(1)
    whole = lambda shape: pl.BlockSpec(shape, lambda i: (0, 0), pipeline_mode=one)
    total = lambda: pl.BlockSpec((T, D), lambda i: (0, 0))
    columns = lambda rows, part=0: pl.BlockSpec((rows, GROUP), lambda i: (0, i + part * groups))
    head_rows = lambda dtype: pltpu.VMEM((HEADS, T, HD), dtype)
    return pl.pallas_call(
        functools.partial(attn_kernel, order),
        grid=(groups,),
        in_specs=[pl.BlockSpec(memory_space=pltpu.SMEM), whole((T, D)), whole((T, D))]
        + [columns(D, p) for p in range(3)]
        + [columns(1, p) for p in range(3)]
        + [pl.BlockSpec((GROUP, D), lambda i: (i, 0))]
        + [whole((T, 128))] * 3,
        out_specs=[total(), total()] + [columns(D)] * 3 + [pl.BlockSpec((GROUP, D), lambda i: (i, 0)), columns(3)],
        out_shape=[jax.ShapeDtypeStruct((T, D), F32)] * 2
        + [jax.ShapeDtypeStruct((D, D), BF)] * 4
        + [jax.ShapeDtypeStruct((3, D), F32)],
        scratch_shapes=[head_rows(BF)] * 5 + [head_rows(F32)] * 3 + [pltpu.VMEM((T, 4 * GROUP), BF)],
        compiler_params=pltpu.CompilerParams(vmem_limit_bytes=VMEM),
        cost_estimate=pl.CostEstimate(flops=90 * 10**9, bytes_accessed=40 * 2**20, transcendentals=10 * 2**20),
        name="attn",
    )(length, na, gr, weight, weight, weight, bias, bias, bias, wd, *map(jnp.asarray, rotary_tables()))


def shards(
    layer_input, seq_lengths, out_grad, attn_gain, attn_shift, mlp_gain, mlp_shift, qkv_weight, qkv_bias,
    dense_weight, dense_bias, inner_weight, inner_bias, outer_weight, outer_bias,
):
    groupings = ("core", "y", "x")
    shard_count = lax.axis_size("y") * lax.axis_size("x")
    core = lax.axis_index("core")
    order = [2 * a + h for h in range(2) for a in range(shard_count)]

    def gather(piece):
        half = piece.shape[0] // 2
        mine = lax.dynamic_slice_in_dim(piece, core * half, half, 0)
        return lax.all_gather(mine, groupings, axis=0, tiled=True)

    def natural(rows):
        return jnp.swapaxes(rows.reshape(2, shard_count, -1, rows.shape[1]), 0, 1).reshape(rows.shape)

    def halves_first(rows):
        return jnp.swapaxes(rows.reshape(shard_count, 2, -1, rows.shape[1]), 0, 1).reshape(rows.shape)

    vectors = jnp.concatenate(
        [attn_gain, attn_shift, mlp_gain, mlp_shift, dense_bias, outer_bias, qkv_bias, inner_bias]
    )
    vectors = lax.all_gather(vectors, ("y", "x"), axis=0, tiled=False).astype(F32)
    sizes = [D] * 6 + [3 * D, FF]
    cuts = np.cumsum([size // shard_count for size in sizes])[:-1]
    gain_a, shift_a, gain_m, shift_m, bias_d, bias_o, bias_qkv, bias_i = (
        part.reshape(1, -1) for part in jnp.split(vectors, cuts, axis=1)
    )
    wi = gather(inner_weight)
    wo = gather(outer_weight)
    wqkv = gather(qkv_weight)
    wd = natural(gather(dense_weight))

    x = layer_input.astype(F32)
    mean = jnp.mean(x, axis=1, keepdims=True)
    centered = x - mean
    inverse = lax.rsqrt(jnp.mean(centered * centered, axis=1, keepdims=True) + EPSILON)
    unit = centered * inverse
    valid = jnp.arange(T, dtype=jnp.int32)[:, None] < seq_lengths[0]
    gr = jnp.where(valid, out_grad, jnp.zeros_like(out_grad))
    blocked = lambda rows: jnp.swapaxes(rows.reshape(T, shard_count, 2, -1), 1, 2).reshape(T, D)
    nm = blocked((unit * gain_m + shift_m).astype(BF))
    na = blocked((unit * gain_a + shift_a).astype(BF))

    out_m, dnm, gwi, gwo, gbi = mlp(order, nm, gr, wi, bias_i, wo)
    out_a, dna, gwq, gwk, gwv, gwd, gbqkv = attn(order, seq_lengths, na, gr, wqkv, bias_qkv, wd)

    def reduce(grad):
        part = lax.psum_scatter(grad, "core", scatter_dimension=0, tiled=True)
        part = lax.psum_scatter(part, ("y", "x"), scatter_dimension=0, tiled=True)
        part = lax.psum(part, "z")
        return lax.all_gather(part, "core", axis=0, tiled=True).astype(F32)

    grad_wi = reduce(gwi)
    grad_wo = reduce(gwo)
    grad_d = reduce(halves_first(gwd))
    grad_qkv = jnp.concatenate([reduce(g) for g in (gwq, gwk, gwv)], axis=1)

    layer_output = x + out_m + out_a + (bias_d + bias_o)
    g = dna * gain_a + dnm * gain_m
    gr32 = gr.astype(F32)
    input_grad = gr32 + inverse * (
        g - jnp.mean(g, axis=1, keepdims=True) - unit * jnp.mean(g * unit, axis=1, keepdims=True)
    )
    column = lambda rows: jnp.sum(rows, axis=0)
    parts = [column(dna * unit), column(dna), column(dnm * unit), column(dnm), column(gr32), gbqkv, gbi]
    small = jnp.concatenate([p.reshape(shard_count, -1) for p in parts], axis=1)
    small = lax.psum_scatter(small, ("y", "x"), scatter_dimension=0, tiled=True)
    small = lax.psum(small, ("z", "core"))
    cuts = np.cumsum([size // shard_count for size in [D] * 5 + [3 * D, FF]])[:-1]
    g_ga, g_sa, g_gm, g_sm, g_bd, g_bqkv, g_bi = (p.reshape(-1) for p in jnp.split(small, cuts, axis=1))
    return (
        layer_output, input_grad, g_ga, g_sa, g_gm, g_sm, grad_qkv, g_bqkv, grad_d, g_bd, grad_wi, g_bi, grad_wo, g_bd,
    )


def solution(mesh):
    replicas, shard_count = mesh.shape["rep"], mesh.shape["shard"]
    shape = (replicas // 2, 2, 2, shard_count // 2)
    cut = Mesh(mesh.devices.reshape(shape), ("z", "core", "y", "x"))
    both = P(("z", "core", "y", "x"), None)
    shard = P(("y", "x"))
    matrix = P(("y", "x"), None)
    weights = (shard,) * 4 + (matrix, shard) * 4
    return jax.shard_map(
        shards,
        mesh=cut,
        in_specs=(both, P(("z", "core", "y", "x")), both) + weights,
        out_specs=(both, both) + weights,
        check_vma=False,
    )
```

time: 1670 us -> 753 us (0.45)
  matrix products: 400 us -> 0 us
  waiting for transfers between devices: 808 us -> 441 us
  Pallas kernels: 0 us -> 162 us
  local copies, waits for them, and re-layouts: 184 us -> 38.9 us
  other arithmetic: 115 us -> 33.9 us
  blocking collectives: 132 us -> 61.1 us
    reduce_scatter x4 -> x12, waiting for transfers between devices: 717 us -> 269 us  [the longest x6 235 us: reduce(): part = lax.psum_scatter(part, ('y', 'x'), scatter_dimension=0, tiled=True)]
    dot_general x26 -> x0, matrix products: 400 us -> none  [the longest x4 62.4 us: block_scores(): jnp.einsum('qhd,khd->hqk', block_queries, slot_keys, preferred_element_ty...]
    pallas_call x0 -> x2, Pallas kernels: none -> 162 us  [the longest x1 99.9 us: attn(): pl.pallas_call(functools.partial(attn_kernel, order), grid=(groups,), in_...]
    psum x0 -> x1, waiting for transfers between devices: none -> 126 us  [reduce(): part = lax.psum(part, 'z')]
    dynamic_update_slice x4 -> x0, local copies, waits for them, and re-layouts: 82.9 us -> none  [backward_slot(): lax.scan(backward_one_block, (zero_heads, zero_heads), jnp.arange(SLOT //...]
    all_gather x9 -> x5, blocking collectives: 72.7 us -> 18.4 us  [the longest x1 9.7 us: shards(): lax.all_gather(vectors, ('y', 'x'), axis=0, tiled=False).astype(F32)]
    convert_element_type x12 -> x4, other arithmetic: 63.5 us -> 12.2 us  [the longest x3 9.4 us: reduce(): return lax.all_gather(part, 'core', axis=0, tiled=True).astype(F32)]
    all_gather x8 -> x6, waiting for transfers between devices: 87.4 us -> 41.6 us  [the longest x4 41.6 us: gather(): return lax.all_gather(mine, groupings, axis=0, tiled=True)]
  transfers between devices with their start and end apart: 12 -> 19, of which waited for: 6 -> 10; matrix products, arithmetic and copies ran while one was open for 41% -> 9% of each run, Pallas kernels for 0% -> 22%
where the time goes in v1:
time: 753 us
  waiting for transfers between devices  441 us (59%)
  Pallas kernels  162 us (22%)
  blocking collectives  61.1 us (8%)
  local copies, waits for them, and re-layouts  38.9 us (5%)
  other arithmetic  33.9 us (5%)
  between operations  15.2 us (2%)
    reduce_scatter x6, waiting for transfers between devices, reduce(): part = lax.psum_scatter(part, ('y', 'x'), scatter_dimension=0, tiled=True)  235 us
    psum x1, waiting for transfers between devices, reduce(): part = lax.psum(part, 'z')  126 us
    pallas_call x1, Pallas kernels, attn(): pl.pallas_call(functools.partial(attn_kernel, order), grid=(groups,), in_...  99.9 us
    pallas_call x1, Pallas kernels, mlp(): pl.pallas_call(functools.partial(mlp_kernel, order), grid=(FF // tile,),...  62.5 us
    all_gather x4, waiting for transfers between devices, gather(): return lax.all_gather(mine, groupings, axis=0, tiled=True)  41.6 us
    reduce_scatter x6, waiting for transfers between devices, reduce(): part = lax.psum_scatter(grad, 'core', scatter_dimension=0, tiled=True)  34.1 us
    psum x1, blocking collectives, shards(): small = lax.psum(small, ('z', 'core'))  26.2 us
    unnamed x1, blocking collectives  16.5 us
  transfers between devices with their start and end apart: 19, of which 10 were waited for; matrix products, arithmetic and copies ran while one was open for 9% of the time, Pallas kernels for 22%

profile of v1, /device:TPU:0, one launch (start us, length us, event | category | flops | bytes accessed | tf_op | source)
XLA Modules:
  0.0 752.9 jit_solution(7512347339338833240)
XLA Ops:
  12.5 2.5 constant_dynamic-slice_fusion.2
  16.9 9.7 %all-gather.1 = bf16[4,1,3328]{2,1,0:T(2,128)(2,1)S(1)} all-gather(bf16[1,1,3328]{2,1,0:T(2,128)(2,1)S(1)} %reshape.174), channel_id=2, replica_groups=mesh['z'=4,'core'=2,'y'=2,'x'=2] {'y','x'}, dimensions={0}, use_global_device_ids=true | all-gather | bytes 33280 | tf_op jit(solution)/shard_map/all_gather | solution.py:265
  29.0 2.8 fusion.9
  31.8 3.2 reshape.151
  37.1 4.6 reshape.152.na
  42.3 2.5 convert_reduce_fusion.1
  44.8 3.1 copy.38
  47.8 41.5 %all-gather.13.cloned.1.call-done.wq.wk.wv = bf16[1024,3072]{1,0:T(8,128)(2,1)} async-done(((bf16[128,3072]{1,0:T(8,128)(2,1)}), bf16[1024,3072]{1,0:T(8,128)(2,1)}) %all-gather.13.cloned.1.call-update) | async-done | bytes 6291472 | tf_op jit(solution)/shard_map/all_gather | solution.py:254
  89.3 99.9 %attn.1 = (f32[1024,1024]{1,0:T(8,128)}, f32[1024,1024]{1,0:T(8,128)}, bf16[1024,1024]{1,0:T(8,128)(2,1)}, bf16[1024,1024]{1,0:T(8,128)(2,1)}, bf16[1024,1024]{1...) custom-call(s32[1]{0:T(128)} %copy.71.length, bf16[1024,1024]{1,0:T(8,128)(2,1)} %reshape.152.na, ...), custom_call_target="tpu_custom_call" | custom-call | flops 89999998976 | bytes 41943040 | tf_op jit(solution)/shard_map/attn/pallas_call | solution.py:223
  190.9 2.7 reshape.148
  193.6 2.3 copy.36
  195.9 2.7 reshape.149.nm
  199.2 3.1 copy.39
  202.5 62.5 %mlp.1 = (f32[1024,1024]{1,0:T(8,128)}, f32[1024,1024]{1,0:T(8,128)}, bf16[1024,4096]{1,0:T(8,128)(2,1)}, bf16[4096,1024]{1,0:T(8,128)(2,1)}, f32[1,4096]{1,0:T(1,128)}) custom-call(bf16[1024,1024]{1,0:T(8,128)(2,1)} %reshape.149.nm, bf16[1024,1024]{1,0:T(8,128)(2,1)} %get-tuple-element.51.gr, bf16[1024,4096]{1,0:T(8,128)(2,1)} %all-gather.9.cloned.1.call-done.wi, ...), custom_call_target="tpu_custom_call" | custom-call | flops 51539607552 | bytes 62914560 | tf_op jit(solution)/shard_map/mlp/pallas_call | solution.py:101
  268.3 13.7 %reduce-scatter.29.cloned.1.call-done = bf16[512,4096]{1,0:T(8,128)(2,1)} async-done(((bf16[1024,4096]{1,0:T(8,128)(2,1)}), bf16[512,4096]{1,0:T(8,128)(2,1)}) %reduce-scatter.29.cloned.1.call-update) | async-done | bytes 4194320 | tf_op jit(solution)/shard_map/reduce_scatter | solution.py:291
  282.1 20.3 %reduce-scatter.33.cloned.1.call-done = bf16[2048,1024]{1,0:T(8,128)(2,1)} async-done(((bf16[4096,1024]{1,0:T(8,128)(2,1)}), bf16[2048,1024]{1,0:T(8,128)(2,1)}) %reduce-scatter.33.cloned.1.call-update) | async-done | bytes 4194320 | tf_op jit(solution)/shard_map/reduce_scatter | solution.py:291
  302.5 31.8 %reduce-scatter.23.cloned.1.call-done = bf16[128,1024]{1,0:T(8,128)(2,1)} async-done(((bf16[512,1024]{1,0:T(8,128)(2,1)}), bf16[128,1024]{1,0:T(8,128)(2,1)}) %reduce-scatter.23.cloned.1.call-update) | async-done | bytes 262160 | tf_op jit(solution)/shard_map/reduce_scatter | solution.py:292
  334.3 30.7 %reduce-scatter.19.cloned.1.call-done = bf16[128,1024]{1,0:T(8,128)(2,1)} async-done(((bf16[512,1024]{1,0:T(8,128)(2,1)}), bf16[128,1024]{1,0:T(8,128)(2,1)}) %reduce-scatter.19.cloned.1.call-update) | async-done | bytes 262160 | tf_op jit(solution)/shard_map/reduce_scatter | solution.py:292
  365.0 30.6 %reduce-scatter.15.cloned.1.call-done = bf16[128,1024]{1,0:T(8,128)(2,1)} async-done(((bf16[512,1024]{1,0:T(8,128)(2,1)}), bf16[128,1024]{1,0:T(8,128)(2,1)}) %reduce-scatter.15.cloned.1.call-update) | async-done | bytes 262160 | tf_op jit(solution)/shard_map/reduce_scatter | solution.py:292
  395.7 30.7 %reduce-scatter.27.cloned.1.call-done = bf16[128,1024]{1,0:T(8,128)(2,1)} async-done(((bf16[512,1024]{1,0:T(8,128)(2,1)}), bf16[128,1024]{1,0:T(8,128)(2,1)}) %reduce-scatter.27.cloned.1.call-update) | async-done | bytes 262160 | tf_op jit(solution)/shard_map/reduce_scatter | solution.py:292
  426.4 55.5 %reduce-scatter.31.cloned.1.call-done = bf16[128,4096]{1,0:T(8,128)(2,1)} async-done(((bf16[512,4096]{1,0:T(8,128)(2,1)}), bf16[128,4096]{1,0:T(8,128)(2,1)}) %reduce-scatter.31.cloned.1.call-update) | async-done | bytes 1048592 | tf_op jit(solution)/shard_map/reduce_scatter | solution.py:292
  481.9 55.8 %reduce-scatter.35.cloned.1.call-done = bf16[512,1024]{1,0:T(8,128)(2,1)} async-done(((bf16[2048,1024]{1,0:T(8,128)(2,1)}), bf16[512,1024]{1,0:T(8,128)(2,1)}) %reduce-scatter.35.cloned.1.call-update) | async-done | bytes 1048592 | tf_op jit(solution)/shard_map/reduce_scatter | solution.py:292
  537.8 125.5 %all-reduce.4.cloned.1.call-done = (bf16[128,1024]{1,0:T(8,128)(2,1)}, bf16[128,1024]{1,0:T(8,128)(2,1)}, bf16[128,1024]{1,0:T(8,128)(2,1)}, bf16[128,1024]{1,0:...) async-done(((bf16[128,1024]{1,0:T(8,128)(2,1)}, bf16[128,1024]{1,0:T(8,128)(2,1)}, bf16[128,1024]{1,0:T(8,128)(2,1)}, bf16[128,1024]{1,0:T(8,128)(2,1)}, ...) | async-done | bytes 3145744 | tf_op jit(solution)/shard_map/psum | solution.py:293
  664.2 9.9 %fusion.21 = (f32[1024]{0:T(1024)S(1)}, f32[1024]{0:T(1024)S(1)}, f32[1024]{0:T(1024)S(1)}, f32[1024]{0:T(1024)S(1)}, f32[1024,1024]{1,0:T(8,128)}, /*index=5*/f...) fusion(f32[1024,1024]{1,0:T(8,128)} %get-tuple-element.29, f32[1024]{0:T(1024)S(1)} %copy-done.13, ...), kind=kLoop, calls=%fused_computation.55 | loop fusion | flops 18868224 | bytes 27308032 | tf_op jit(solution)/shard_map/reduce_sum | solution.py:307
  675.4 16.5 %all-reduce = f32[4,3072]{1,0:T(4,128)S(1)} all-reduce(f32[4,3072]{1,0:T(4,128)S(1)} %constant_dynamic-update-slice_fusion), channel_id=3, replica_groups=mesh['z'=4,'core'=2,'y'=2,'x'=2] {'y','x'}, use_global_device_ids=true, to_apply=%region_9.10.clone | all-reduce | flops 12288 | bytes 98304
  692.6 26.2 %psum.49 = f32[1,3072]{1,0:T(1,128)S(1)} all-reduce(f32[1,3072]{1,0:T(1,128)S(1)} %constant_dynamic-slice_fusion.4), channel_id=1, replica_groups=mesh['z'=4,'core'=2,'y'=2,'x'=2] {'z','core'}, use_global_device_ids=true, to_apply=%region_10.11 | all-reduce | flops 3072 | bytes 24576 | tf_op jit(solution)/shard_map/psum | solution.py:311
  720.6 5.0 convert_add_fusion.1
  728.9 2.2 all_gather.44
  731.1 2.2 all_gather.43
  733.2 2.2 all_gather.42
  737.4 4.2 convert_element_type.33
  741.7 4.1 convert_element_type.34
  (167 shorter events, 27.4 us)
Async XLA Ops:
  7.2 37.6 %all-gather.15.cloned.1.call-start = ((), (), s32[]{:S(2)}) async-start(), calls=%async_computation.15 | async-start | bytes 2359296 | tf_op jit(solution)/shard_map/all_gather | solution.py:254
  9.2 80.2 %all-gather.13.cloned.1.call-start = ((), (), s32[]{:S(2)}) async-start(), calls=%async_computation.14 | async-start | bytes 7077888 | tf_op jit(solution)/shard_map/all_gather | solution.py:254
  11.3 191.1 %all-gather.9.cloned.1.call-start = ((), (), s32[]{:S(2)}) async-start(), calls=%async_computation.12 | async-start | bytes 9437184 | tf_op jit(solution)/shard_map/all_gather | solution.py:254
  12.5 15.5 %copy-start.2 = (bf16[1024,1024]{1,0:T(8,128)(2,1)S(1)}, bf16[1024,1024]{1,0:T(8,128)(2,1)}, u32[]{:S(2)}) copy-start(bf16[1024,1024]{1,0:T(8,128)(2,1)} %param.18) | copy-start | bytes 6291460
  12.5 190.0 %all-gather.11.cloned.1.call-start = ((), (), s32[]{:S(2)}) async-start(), calls=%async_computation.13 | async-start | bytes 9437184 | tf_op jit(solution)/shard_map/all_gather | solution.py:254
  15.1 250.6 %reduce-scatter.21.cloned.1.call-start = ((), (), s32[]{:S(2)}) async-start(), calls=%async_computation.20 | async-start | bytes 3145728 | tf_op jit(solution)/shard_map/reduce_scatter | solution.py:291
  189.3 77.2 %reduce-scatter.17.cloned.1.call-start = ((), (), s32[]{:S(2)}) async-start(), calls=%async_computation.18 | async-start | bytes 3145728 | tf_op jit(solution)/shard_map/reduce_scatter | solution.py:291
  189.9 77.1 %reduce-scatter.13.cloned.1.call-start = ((), (), s32[]{:S(2)}) async-start(), calls=%async_computation.16 | async-start | bytes 3145728 | tf_op jit(solution)/shard_map/reduce_scatter | solution.py:291
  190.6 77.1 %reduce-scatter.25.cloned.1.call-start = ((), (), s32[]{:S(2)}) async-start(), calls=%async_computation.22 | async-start | bytes 3145728 | tf_op jit(solution)/shard_map/reduce_scatter | solution.py:291
  202.4 79.6 %reduce-scatter.29.cloned.1.call-start = ((), (), s32[]{:S(2)}) async-start(), calls=%async_computation.24 | async-start | bytes 12582912 | tf_op jit(solution)/shard_map/reduce_scatter | solution.py:291
  265.0 37.3 %reduce-scatter.33.cloned.1.call-start = ((), (), s32[]{:S(2)}) async-start(), calls=%async_computation.27 | async-start | bytes 12582912 | tf_op jit(solution)/shard_map/reduce_scatter | solution.py:291
  265.6 68.7 %reduce-scatter.23.cloned.1.call-start = ((), (), s32[]{:S(2)}) async-start(), calls=%async_computation.21 | async-start | bytes 1310720 | tf_op jit(solution)/shard_map/reduce_scatter | solution.py:292
  266.4 98.7 %reduce-scatter.19.cloned.1.call-start = ((), (), s32[]{:S(2)}) async-start(), calls=%async_computation.19 | async-start | bytes 1310720 | tf_op jit(solution)/shard_map/reduce_scatter | solution.py:292
  266.9 128.7 %reduce-scatter.15.cloned.1.call-start = ((), (), s32[]{:S(2)}) async-start(), calls=%async_computation.17 | async-start | bytes 1310720 | tf_op jit(solution)/shard_map/reduce_scatter | solution.py:292
  267.7 158.7 %reduce-scatter.27.cloned.1.call-start = ((), (), s32[]{:S(2)}) async-start(), calls=%async_computation.23 | async-start | bytes 1310720 | tf_op jit(solution)/shard_map/reduce_scatter | solution.py:292
  268.3 213.7 %reduce-scatter.31.cloned.1.call-start = ((), (), s32[]{:S(2)}) async-start(), calls=%async_computation.25 | async-start | bytes 5242880 | tf_op jit(solution)/shard_map/reduce_scatter | solution.py:292
  282.1 255.7 %reduce-scatter.35.cloned.1.call-start = ((), (), s32[]{:S(2)}) async-start(), calls=%async_computation.28 | async-start | bytes 5242880 | tf_op jit(solution)/shard_map/reduce_scatter | solution.py:292
  302.4 361.1 %copy-start.20 = (f32[1,2,4,128]{3,2,1,0:T(4,128)S(1)}, f32[1,2,4,128]{3,2,1,0:T(4,128)}, u32[]{:S(2)}) copy-start(f32[1,2,4,128]{3,2,1,0:T(4,128)} %get-tuple-element.61) | copy-start | bytes 12292
  302.4 361.1 %copy-start.21 = (f32[1024]{0:T(1024)S(1)}, f32[1024]{0:T(1024)}, u32[]{:S(2)}) copy-start(f32[1024]{0:T(1024)} %get-tuple-element.50) | copy-start | bytes 12292
  302.4 361.1 %copy-start.31 = (u32[32]{0:T(128)S(1)}, u32[32]{0:T(128)}, u32[]{:S(2)}) copy-start(u32[32]{0:T(128)} %constant.40) | copy-start | bytes 388
  302.4 361.7 %copy-start.18 = (f32[3,1024]{1,0:T(4,128)S(1)}, f32[3,1024]{1,0:T(4,128)}, u32[]{:S(2)}) copy-start(f32[3,1024]{1,0:T(4,128)} %get-tuple-element.30) | copy-start | bytes 36868
  302.4 361.7 %copy-start.3 = (bf16[1024,1024]{1,0:T(8,128)(2,1)S(1)}, bf16[1024,1024]{1,0:T(8,128)(2,1)}, u32[]{:S(2)}) copy-start(bf16[1024,1024]{1,0:T(8,128)(2,1)} %param.18) | copy-start | bytes 6291460
  302.4 361.7 %copy-start.11 = (f32[1024]{0:T(1024)S(1)}, f32[1024]{0:T(1024)}, u32[]{:S(2)}) copy-start(f32[1024]{0:T(1024)} %copy-done.10) | copy-start | bytes 12292
  302.4 361.7 %copy-start.13 = (f32[1024]{0:T(1024)S(1)}, f32[1024]{0:T(1024)}, u32[]{:S(2)}) copy-start(f32[1024]{0:T(1024)} %copy-done.12) | copy-start | bytes 12292
  302.4 361.7 %copy-start.15 = (f32[1,2,4,128]{3,1,2,0:T(2,128)S(1)}, f32[1,2,4,128]{3,1,2,0:T(2,128)}, u32[]{:S(2)}) copy-start(f32[1,2,4,128]{3,1,2,0:T(2,128)} %copy-done.14) | copy-start | bytes 12292
  302.4 361.7 %copy-start.17 = (f32[1,2,4,128]{3,1,2,0:T(2,128)S(1)}, f32[1,2,4,128]{3,1,2,0:T(2,128)}, u32[]{:S(2)}) copy-start(f32[1,2,4,128]{3,1,2,0:T(2,128)} %copy-done.16) | copy-start | bytes 12292
  302.5 360.9 %all-reduce.4.cloned.1.call-start = ((), (), s32[]{:S(2)}) async-start(), calls=%async_computation.30 | async-start | bytes 6291456 | tf_op jit(solution)/shard_map/psum | solution.py:293
  537.8 199.6 %all-gather.17.cloned.1.call-start = ((), (), s32[]{:S(2)}) async-start(), calls=%async_computation.26 | async-start | bytes 3145728 | tf_op jit(solution)/shard_map/all_gather | solution.py:294
  663.4 78.3 %all-gather.19.cloned.1.call-start = ((), (), s32[]{:S(2)}) async-start(), calls=%async_computation.29 | async-start | bytes 3145728 | tf_op jit(solution)/shard_map/all_gather | solution.py:294
  720.0 25.8 %copy-start.22 = (f32[1,256]{1,0:T(1,128)}, f32[1,256]{1,0:T(1,128)S(1)}, u32[]{:S(2)}) copy-start(f32[1,256]{1,0:T(1,128)S(1)} %get-tuple-element.66) | copy-start | bytes 3076
  720.6 10.5 %copy-start.7 = (bf16[128,1024]{1,0:T(8,128)(2,1)S(1)}, bf16[128,1024]{1,0:T(8,128)(2,1)}, u32[]{:S(2)}) copy-start(bf16[128,1024]{1,0:T(8,128)(2,1)} %get-tuple-element.45) | copy-start | bytes 786436
  720.6 12.6 %copy-start.6 = (bf16[128,1024]{1,0:T(8,128)(2,1)S(1)}, bf16[128,1024]{1,0:T(8,128)(2,1)}, u32[]{:S(2)}) copy-start(bf16[128,1024]{1,0:T(8,128)(2,1)} %get-tuple-element.46) | copy-start | bytes 786436
  (19 other events, 113.5 us)
Sparse Core Ops, SparseCore 0:
  10.5 30.8 all-gather.14
  43.8 45.5 all-gather.12
  91.8 54.3 all-gather.8
  148.0 54.3 all-gather.10
  204.5 9.6 reduce-scatter.20
  216.3 10.7 reduce-scatter.16
  229.4 10.7 reduce-scatter.12
  242.5 10.7 reduce-scatter.24
  265.2 16.8 reduce-scatter.28
  284.3 18.0 reduce-scatter.32
  305.3 28.9 reduce-scatter.22
  337.3 27.6 reduce-scatter.18
  367.9 27.7 reduce-scatter.14
  398.7 27.6 reduce-scatter.26
  429.2 52.6 reduce-scatter.30
  485.0 52.6 reduce-scatter.34
  540.5 122.8 all-reduce.3
  664.8 9.3 all-gather.16
  692.1 7.5 all-gather.18

commit v2 on v1

--- a/solution.py
+++ b/solution.py
@@ -239,7 +239,7 @@
     )(length, na, gr, weight, weight, weight, bias, bias, bias, wd, *map(jnp.asarray, rotary_tables()))
 
 
-def shards(
+def general_shards(
     layer_input, seq_lengths, out_grad, attn_gain, attn_shift, mlp_gain, mlp_shift, qkv_weight, qkv_bias,
     dense_weight, dense_bias, inner_weight, inner_bias, outer_weight, outer_bias,
 ):
@@ -316,6 +316,830 @@
     )
 
 
+WIDE = 512
+VMEM_UNIT = 56 * 2**20
+LONG = pl.CostEstimate(flops=10**13, bytes_accessed=2**20, transcendentals=0)
+
+
+def columns_at(start, size):
+    return pl.ds(pl.multiple_of(start, 128), size)
+
+
+def norm_kernel(table, x, grad, gain_a, shift_a, gain_m, shift_m, na, nm, gr):
+    values = x[...].astype(F32)
+    mean = jnp.mean(values, axis=1, keepdims=True)
+    centered = values - mean
+    unit = centered * lax.rsqrt(jnp.mean(centered * centered, axis=1, keepdims=True) + EPSILON)
+    rows = x.shape[0]
+    position = pl.program_id(0) * rows + lax.broadcasted_iota(jnp.int32, (rows, 1), 0)
+    gr[...] = jnp.where(position < table[1], grad[...].astype(F32), 0.0).astype(BF)
+    for out, gain, shift in ((na, gain_a, shift_a), (nm, gain_m, shift_m)):
+        normed = (unit * gain[...] + shift[...]).astype(BF)
+        for a in range(4):
+            for h in range(2):
+                place = (table[2 + a] * 2 + (table[0] ^ h)) * 128
+                out[:, columns_at(place, 128)] = normed[:, rows_of(a * 2 + h, 128)]
+
+
+def norm(table, x, grad, vectors):
+    tile = pl.BlockSpec((ROWS, D), lambda i: (i, 0))
+    row = pl.BlockSpec((1, D), lambda i: (0, 0))
+    return pl.pallas_call(
+        norm_kernel,
+        grid=(T // ROWS,),
+        in_specs=[pl.BlockSpec(memory_space=pltpu.SMEM), tile, tile] + [row] * 4,
+        out_specs=[tile] * 3,
+        out_shape=[jax.ShapeDtypeStruct((T, D), BF)] * 3,
+        compiler_params=pltpu.CompilerParams(vmem_limit_bytes=VMEM),
+        cost_estimate=pl.CostEstimate(flops=10 * T * D, bytes_accessed=10 * T * D, transcendentals=T),
+        name="norm",
+    )(table, x, grad, *vectors)
+
+
+def output_kernel(x, out, bias, layer_output):
+    layer_output[...] = x[...].astype(F32) + out[...] + bias[...]
+
+
+def output(x, out, bias):
+    tile = pl.BlockSpec((ROWS, D), lambda i: (i, 0))
+    row = pl.BlockSpec((1, D), lambda i: (0, 0))
+    return pl.pallas_call(
+        output_kernel,
+        grid=(T // ROWS,),
+        in_specs=[tile, tile, row],
+        out_specs=tile,
+        out_shape=jax.ShapeDtypeStruct((T, D), F32),
+        cost_estimate=LONG,
+        name="output",
+    )(x, out, bias)
+
+
+def finish_kernel(table, x, gr, dna, dnm, gain_a, gain_m, *refs):
+    *bias_sums, input_grad, small, sums = refs
+    values = x[...].astype(F32)
+    mean = jnp.mean(values, axis=1, keepdims=True)
+    centered = values - mean
+    inverse = lax.rsqrt(jnp.mean(centered * centered, axis=1, keepdims=True) + EPSILON)
+    unit = centered * inverse
+
+    def natural(ref):
+        places = [(table[2 + a] * 2 + (table[0] ^ h)) * 128 for a in range(4) for h in range(2)]
+        return jnp.concatenate([ref[:, columns_at(place, 128)] for place in places], axis=1)
+
+    normed_a, normed_m = natural(dna), natural(dnm)
+    upper = gr[...].astype(F32)
+    g = normed_a * gain_a[...] + normed_m * gain_m[...]
+    input_grad[...] = upper + inverse * (
+        g - jnp.mean(g, axis=1, keepdims=True) - unit * jnp.mean(g * unit, axis=1, keepdims=True)
+    )
+
+    @pl.when(pl.program_id(0) == 0)
+    def _():
+        sums[...] = jnp.zeros_like(sums)
+
+    for i, rows in enumerate((normed_a * unit, normed_a, normed_m * unit, normed_m, upper)):
+        sums[i : i + 1, :] += jnp.sum(rows, axis=0, keepdims=True)
+
+    @pl.when(pl.program_id(0) == T // ROWS - 1)
+    def _():
+        for i in range(5):
+            for a in range(4):
+                small[a : a + 1, rows_of(i, 256)] = sums[i : i + 1, rows_of(a, 256)]
+        *pairs, first_unit, second_unit = bias_sums
+        for pair in range(2):
+            for a, b in qkv_blocks(pair):
+                small[a // 768 : a // 768 + 1, pl.ds(1280 + a % 768, 128)] = pairs[pair][:, pl.ds(b, 128)]
+        for unit_index, value in enumerate((first_unit, second_unit)):
+            for a in range(4):
+                small[a : a + 1, pl.ds(2048 + unit_index * 512, 512)] = value[:, rows_of(a, 512)]
+
+
+def finish(table, x, gr, dna, dnm, vectors, bias_sums):
+    tile = pl.BlockSpec((ROWS, D), lambda i: (i, 0))
+    row = lambda value: pl.BlockSpec(value.shape, lambda i: (0, 0))
+    return pl.pallas_call(
+        finish_kernel,
+        grid=(T // ROWS,),
+        in_specs=[pl.BlockSpec(memory_space=pltpu.SMEM)] + [tile] * 4 + [row(v) for v in (*vectors, *bias_sums)],
+        out_specs=[tile, pl.BlockSpec((4, 3072), lambda i: (0, 0))],
+        out_shape=[jax.ShapeDtypeStruct((T, D), F32), jax.ShapeDtypeStruct((4, 3072), F32)],
+        scratch_shapes=[pltpu.VMEM((5, D), F32)],
+        compiler_params=pltpu.CompilerParams(vmem_limit_bytes=VMEM),
+        cost_estimate=LONG,
+        name="finish",
+    )(table, x, gr, dna, dnm, *vectors, *bias_sums)
+
+
+class Totals:
+    def __init__(self, refs_in, refs_out, scratch, sems):
+        self.fresh = [ref is None for ref in refs_in]
+        self.refs_in, self.refs_out, self.scratch, self.sems = refs_in, refs_out, scratch, sems
+
+    def loads(self):
+        return [
+            pltpu.make_async_copy(source, self.scratch[i], self.sems.at[i])
+            for i, source in enumerate(self.refs_in)
+            if source is not None
+        ]
+
+    def stores(self):
+        return [
+            pltpu.make_async_copy(source, target, self.sems.at[i])
+            for i, (source, target) in enumerate(zip(self.scratch, self.refs_out))
+        ]
+
+    def begin(self):
+        for copy in self.loads():
+            copy.start()
+        for target, source in zip(self.scratch, self.refs_in):
+            if source is None:
+                target[...] = jnp.zeros_like(target)
+
+    def ready(self):
+        for copy in self.loads():
+            copy.wait()
+
+
+def start_all(copies):
+    for copy in copies:
+        copy.start()
+
+
+def wait_all(copies):
+    for copy in copies:
+        copy.wait()
+
+
+def mlp_unit_kernel(first, count, given, table, nm, gr, bi, pieces, *refs):
+    refs = list(refs)
+    olds = [refs.pop(0) if is_given else None for is_given in given]
+    keep, send, gbi, out_ref, dn_ref, wi, wo, act, ig, out, dn, inner_stage, outer_stage, sems, out_sems, total_sems = refs
+    step = pl.program_id(0)
+    core = table[0]
+    totals = Totals(olds[2:], (out_ref, dn_ref), (out, dn), total_sems)
+
+    def copies(index):
+        slot, tile = index % 2, first + index
+        made = []
+        for t in range(4):
+            for half in range(2):
+                piece = (core ^ half) * 4 + table[6 + t]
+                source = pieces.at[piece, 0, :, columns_at(tile * WIDE, WIDE)]
+                made.append((source, wi.at[slot, pl.ds(t * 256 + half * 128, 128), :]))
+        for h in range(2):
+            for part in range(2):
+                source = pieces.at[h * 4 + tile, 1, :, pl.ds(part * D, D)]
+                made.append((source, wo.at[slot, pl.ds(h * 256 + part * 128, 128), :]))
+        return [pltpu.make_async_copy(a, b, sems.at[slot, i]) for i, (a, b) in enumerate(made)]
+
+    def results(index):
+        slot, tile = index % 2, first + index
+        made = []
+        for side, target in enumerate((keep, send)):
+            inner_part = target.at[:, pl.ds(pl.multiple_of(tile // 2 * 128, 128), 128), columns_at((tile % 2) * WIDE, WIDE)]
+            made.append((inner_stage.at[slot, side], inner_part))
+            made.append((outer_stage.at[slot, side], target.at[table[2 + tile], pl.ds(256, 256)]))
+        return [pltpu.make_async_copy(a, b, out_sems.at[slot, i]) for i, (a, b) in enumerate(made)]
+
+    @pl.when(step == 0)
+    def _():
+        start_all(copies(step))
+        totals.begin()
+
+    @pl.when(step < count - 1)
+    def _():
+        start_all(copies(step + 1))
+
+    wait_all(copies(step))
+    slot = step % 2
+
+    bias_sum = jnp.zeros(gbi.shape, F32)
+    for t in range(T // ROWS):
+        r = rows_of(t, ROWS)
+        inner = nn(nm[r, :], wi[slot]) + bi[...]
+        grad = nt(gr[r, :], wo[slot])
+        normal = 0.5 * lax.erf(inner * 0.7071067811865476) + 0.5
+        slope = normal + inner * jnp.exp(-0.5 * inner * inner) * 0.3989422804014327
+        act[r, :] = (inner * normal).astype(BF)
+        inner_grad = (grad * slope).astype(BF)
+        ig[r, :] = inner_grad
+        bias_sum += jnp.sum(inner_grad.astype(F32), axis=0, keepdims=True)
+    gbi[...] = bias_sum
+
+    @pl.when(step == 0)
+    def _():
+        totals.ready()
+
+    for t in range(T // ROWS):
+        r = rows_of(t, ROWS)
+        out[r, :] += nn(act[r, :], wo[slot])
+        dn[r, :] += nt(ig[r, :], wi[slot])
+
+    @pl.when(step == count - 1)
+    def _():
+        start_all(totals.stores())
+
+    if count > 2:
+
+        @pl.when(step >= 2)
+        def _():
+            wait_all(results(step - 2))
+
+    for t in range(4):
+        grad = tn(nm[:, rows_of(t, 256)], ig[...]).astype(BF)
+        inner_stage[slot, 0, t] = grad[:128]
+        inner_stage[slot, 1, t] = grad[128:]
+    for f in range(2):
+        grad = tn(act[:, rows_of(f, 256)], gr[...])
+        low, high = grad[:, :WIDE], grad[:, WIDE:]
+        sides = (jnp.where(core == 0, low, high).astype(BF), jnp.where(core == 0, high, low).astype(BF))
+        for side, value in enumerate(sides):
+            for half in range(2):
+                outer_stage[slot, side, rows_of(f, 128), rows_of(half, WIDE)] = value[rows_of(half, 128)]
+    start_all(results(step))
+
+    @pl.when(step == count - 1)
+    def _():
+        if count > 1:
+            wait_all(results(step - 1))
+        wait_all(results(step))
+        wait_all(totals.stores())
+
+
+def mlp_unit(first, count, table, nm, gr, bi, pieces, parts, totals):
+    olds = list(parts) + list(totals)
+    given = tuple(old is not None for old in olds)
+    inputs = [old for old in olds if old is not None]
+    aliases = {5 + n: (0, 1, 3, 4)[i] for n, i in enumerate(i for i in range(4) if given[i])}
+    whole = pl.BlockSpec((T, D), lambda i: (0, 0), pipeline_mode=pl.Buffered(1))
+    anywhere = pl.BlockSpec(memory_space=pl.ANY)
+    return pl.pallas_call(
+        functools.partial(mlp_unit_kernel, first, count, given),
+        grid=(count,),
+        in_specs=[pl.BlockSpec(memory_space=pltpu.SMEM), whole, whole, pl.BlockSpec((1, WIDE), lambda i: (0, first + i)), anywhere]
+        + [anywhere] * len(inputs),
+        out_specs=[anywhere, anywhere, pl.BlockSpec((1, WIDE), lambda i: (0, i)), anywhere, anywhere],
+        out_shape=[jax.ShapeDtypeStruct((4, 512, D), BF)] * 2
+        + [jax.ShapeDtypeStruct((1, count * WIDE), F32)]
+        + [jax.ShapeDtypeStruct((T, D), F32)] * 2,
+        input_output_aliases=aliases,
+        scratch_shapes=[
+            pltpu.VMEM((2, D, WIDE), BF),
+            pltpu.VMEM((2, WIDE, D), BF),
+            pltpu.VMEM((T, WIDE), BF),
+            pltpu.VMEM((T, WIDE), BF),
+            pltpu.VMEM((T, D), F32),
+            pltpu.VMEM((T, D), F32),
+            pltpu.VMEM((2, 2, 4, 128, WIDE), BF),
+            pltpu.VMEM((2, 2, 256, D), BF),
+            pltpu.SemaphoreType.DMA((2, 12)),
+            pltpu.SemaphoreType.DMA((2, 4)),
+            pltpu.SemaphoreType.DMA((2,)),
+        ],
+        compiler_params=pltpu.CompilerParams(vmem_limit_bytes=VMEM_UNIT),
+        cost_estimate=LONG,
+        name="mlp_unit",
+    )(table, nm, gr, bi, pieces, *inputs)
+
+
+def attn_unit_kernel(first, count, given, table, na, gr, bias, cosine, ahead, behind, pieces, *refs):
+    refs = list(refs)
+    olds = [refs.pop(0) if is_given else None for is_given in given]
+    (
+        keep, send, gb, out_ref, dn_ref,
+        w, wd, q, k, v, dc, ctx, dq, dk, dv, grads, out, dn, qkv_stage, dense_stage, sems, out_sems, total_sems,
+    ) = refs
+    step = pl.program_id(0)
+    core = table[0]
+    totals = Totals(olds[2:], (out_ref, dn_ref), (out, dn), total_sems)
+
+    def copies(index):
+        group = first + index
+        made = []
+        for t in range(4):
+            for half in range(2):
+                piece = (core ^ half) * 4 + table[6 + t]
+                source = pieces.at[piece, :, columns_at(group * 768, 768)]
+                made.append((source, w.at[index, pl.ds(t * 256 + half * 128, 128), :]))
+        for pair in range(2):
+            for h in range(2):
+                source = pieces.at[h * 4 + group * 2 + pair, :, pl.ds(1536, 512)]
+                made.append((source, wd.at[index, pl.ds(pair * 128, 128), pl.ds(h * 512, 512)]))
+        return [pltpu.make_async_copy(a, b, sems.at[index, i]) for i, (a, b) in enumerate(made)]
+
+    def results(index):
+        group = first + index
+        made = []
+        for side, target in enumerate((keep, send)):
+            made.append((qkv_stage.at[index, side], target.at[:, :, columns_at(group * 768, 768)]))
+            for pair in range(2):
+                place = target.at[table[2 + group * 2 + pair], :, pl.ds(1536, 512)]
+                made.append((dense_stage.at[index, side, pair], place))
+        return [pltpu.make_async_copy(a, b, out_sems.at[index, i]) for i, (a, b) in enumerate(made)]
+
+    @pl.when(step == 0)
+    def _():
+        for index in range(count):
+            start_all(copies(index))
+        totals.begin()
+
+    wait_all(copies(step))
+
+    def turn(x, r, back):
+        parts = []
+        for p in range(GROUP // 128):
+            pair = x[:, rows_of(p, 128)]
+            straight = pair * cosine[r, :]
+            across = (
+                pltpu.roll(pair, 128 - ROT // 2, 1) * ahead[r, :]
+                + pltpu.roll(pair, ROT // 2, 1) * behind[r, :]
+            )
+            parts.append(straight - across if back else straight + across)
+        return jnp.concatenate(parts, axis=1)
+
+    part = [slice(p * GROUP, (p + 1) * GROUP) for p in range(4)]
+    for t in range(T // ROWS):
+        r = rows_of(t, ROWS)
+        x = na[r, :]
+        projected = nn(x, w[step]) + bias[...]
+        queries = (turn(projected[:, part[0]], r, False).astype(BF) * 0.125).astype(BF)
+        keys = turn(projected[:, part[1]], r, False).astype(BF)
+        values = projected[:, part[2]].astype(BF)
+        context_grad = nt(gr[r, :], wd[step]).astype(BF)
+        for h in range(HEADS):
+            c = rows_of(h, HD)
+            q[h, r, :] = queries[:, c]
+            k[h, r, :] = keys[:, c]
+            v[h, r, :] = values[:, c]
+            dc[h, r, :] = context_grad[:, c]
+
+    block = 256
+    inside = lax.broadcasted_iota(jnp.int32, (1, T), 1) < table[1]
+    outside = jnp.where(inside, 0.0, MASKED).astype(F32)
+    below = lax.broadcasted_iota(jnp.int32, (block, block), 1) <= lax.broadcasted_iota(jnp.int32, (block, block), 0)
+    causal = jnp.where(below, 0.0, MASKED).astype(F32)
+
+    def head(h, carry):
+        dk[h] = jnp.zeros((T, HD), F32)
+        dv[h] = jnp.zeros((T, HD), F32)
+        for i in range(T // block):
+            r = rows_of(i, block)
+            spans = ([slice(0, i * block)] if i else []) + [r]
+            query = q[h, r, :]
+            scores = [nt(query, k[h, c, :]) + outside[:, c] for c in spans]
+            scores[-1] += causal
+            top = functools.reduce(jnp.maximum, [jnp.max(s, axis=1, keepdims=True) for s in scores])
+            weights = [jnp.exp(s - top) for s in scores]
+            scale = 1.0 / sum(jnp.sum(e, axis=1, keepdims=True) for e in weights)
+            low = [e.astype(BF) for e in weights]
+            context = sum(nn(e, v[h, c, :]) for e, c in zip(low, spans))
+            ctx[h, r, :] = (context * scale).astype(BF)
+            scaled_grad = (dc[h, r, :].astype(F32) * scale).astype(BF)
+            probs_grad = [nt(scaled_grad, v[h, c, :]) for c in spans]
+            inner = scale * sum(jnp.sum(e * p, axis=1, keepdims=True) for e, p in zip(weights, probs_grad))
+            score_grad = [(e * (p - inner)).astype(BF) for e, p in zip(weights, probs_grad)]
+            dq[h, r, :] = sum(nn(s, k[h, c, :]) for s, c in zip(score_grad, spans))
+            for s, e, c in zip(score_grad, low, spans):
+                dk[h, c, :] += tn(s, query)
+                dv[h, c, :] += tn(e, scaled_grad)
+        return carry
+
+    lax.fori_loop(0, HEADS, head, 0)
+
+    @pl.when(step == 0)
+    def _():
+        totals.ready()
+
+    sums = jnp.zeros((1, 3 * GROUP), F32)
+    together = lambda ref, r: jnp.concatenate([ref[h, r, :] for h in range(HEADS)], axis=1)
+    for t in range(T // ROWS):
+        r = rows_of(t, ROWS)
+        context = together(ctx, r)
+        grads[r, part[3]] = context
+        out[r, :] += nn(context, wd[step])
+        projected_grad = jnp.concatenate(
+            [
+                turn(together(dq, r) * 0.125, r, True).astype(BF),
+                turn(together(dk, r), r, True).astype(BF),
+                together(dv, r).astype(BF),
+            ],
+            axis=1,
+        )
+        grads[r, : 3 * GROUP] = projected_grad
+        sums += jnp.sum(projected_grad.astype(F32), axis=0, keepdims=True)
+        dn[r, :] += nt(projected_grad, w[step])
+    gb[...] = sums
+
+    @pl.when(step == count - 1)
+    def _():
+        start_all(totals.stores())
+
+    for t in range(4):
+        grad = tn(na[:, rows_of(t, 256)], grads[:, : 3 * GROUP]).astype(BF)
+        qkv_stage[step, 0, t] = grad[:128]
+        qkv_stage[step, 1, t] = grad[128:]
+    grad = tn(grads[:, part[3]], gr[...])
+    first_half, second_half = grad[:, :WIDE], grad[:, WIDE:]
+    sides = (
+        jnp.where(core == 0, first_half, second_half).astype(BF),
+        jnp.where(core == 0, second_half, first_half).astype(BF),
+    )
+    for side, value in enumerate(sides):
+        for pair in range(2):
+            dense_stage[step, side, pair] = value[rows_of(pair, 128)]
+    start_all(results(step))
+
+    @pl.when(step == count - 1)
+    def _():
+        for index in range(count):
+            wait_all(results(index))
+        wait_all(totals.stores())
+
+
+def attn_unit(first, count, table, na, gr, bias, tables, pieces, parts, totals):
+    olds = list(parts) + list(totals)
+    given = tuple(old is not None for old in olds)
+    inputs = [old for old in olds if old is not None]
+    aliases = {8 + n: (0, 1, 3, 4)[i] for n, i in enumerate(i for i in range(4) if given[i])}
+    one = pl.Buffered(1)
+    whole = pl.BlockSpec((T, D), lambda i: (0, 0), pipeline_mode=one)
+    turns = pl.BlockSpec((T, 128), lambda i: (0, 0), pipeline_mode=one)
+    anywhere = pl.BlockSpec(memory_space=pl.ANY)
+    head_rows = lambda dtype: pltpu.VMEM((HEADS, T, HD), dtype)
+    return pl.pallas_call(
+        functools.partial(attn_unit_kernel, first, count, given),
+        grid=(count,),
+        in_specs=[pl.BlockSpec(memory_space=pltpu.SMEM), whole, whole, pl.BlockSpec((1, 3 * GROUP), lambda i: (0, first + i))]
+        + [turns] * 3
+        + [anywhere] * (1 + len(inputs)),
+        out_specs=[anywhere, anywhere, pl.BlockSpec((1, 3 * GROUP), lambda i: (0, i)), anywhere, anywhere],
+        out_shape=[jax.ShapeDtypeStruct((4, 128, 2 * D), BF)] * 2
+        + [jax.ShapeDtypeStruct((1, 3 * GROUP * count), F32)]
+        + [jax.ShapeDtypeStruct((T, D), F32)] * 2,
+        input_output_aliases=aliases,
+        scratch_shapes=[pltpu.VMEM((count, D, 3 * GROUP), BF), pltpu.VMEM((count, GROUP, D), BF)]
+        + [head_rows(BF)] * 5
+        + [head_rows(F32)] * 3
+        + [
+            pltpu.VMEM((T, 4 * GROUP), BF),
+            pltpu.VMEM((T, D), F32),
+            pltpu.VMEM((T, D), F32),
+            pltpu.VMEM((count, 2, 4, 128, 3 * GROUP), BF),
+            pltpu.VMEM((count, 2, 2, 128, WIDE), BF),
+            pltpu.SemaphoreType.DMA((count, 12)),
+            pltpu.SemaphoreType.DMA((count, 6)),
+            pltpu.SemaphoreType.DMA((2,)),
+        ],
+        compiler_params=pltpu.CompilerParams(vmem_limit_bytes=VMEM_UNIT),
+        cost_estimate=LONG,
+        name="attn_unit",
+    )(table, na, gr, bias, *tables, pieces, *inputs)
+
+
+def qkv_blocks(pair):
+    return [
+        (part * D + (2 * group + shard) * 256 + pair * 128, group * 768 + part * 256 + shard * 128)
+        for group in range(2)
+        for part in range(3)
+        for shard in range(2)
+    ]
+
+
+def attn_pack_kernel(pair, table, qkv, dense, piece, sems):
+    core = table[0]
+    rows = pl.ds(pl.multiple_of(core * 128, 128), 128)
+    made = [(qkv.at[rows, pl.ds(a, 128)], piece.at[0, :, pl.ds(b, 128)]) for a, b in qkv_blocks(pair)]
+    made.append((dense.at[pl.ds(pair * 128, 128), columns_at(core * 512, 512)], piece.at[0, :, pl.ds(1536, 512)]))
+    copies = [pltpu.make_async_copy(a, b, sems.at[i]) for i, (a, b) in enumerate(made)]
+    start_all(copies)
+    wait_all(copies)
+
+
+def mlp_pack_kernel(unit, table, inner, outer, piece, sems):
+    core = table[0]
+    rows = pl.ds(pl.multiple_of(core * 128, 128), 128)
+    made = [(inner.at[rows, pl.ds(a * 1024 + unit * 512, 512)], piece.at[0, 0, :, pl.ds(a * 512, 512)]) for a in range(4)]
+    for part in range(2):
+        source = outer.at[pl.ds(pl.multiple_of(unit * 512 + core * 256 + part * 128, 128), 128), :]
+        made.append((source, piece.at[0, 1, :, pl.ds(part * D, D)]))
+    copies = [pltpu.make_async_copy(a, b, sems.at[i]) for i, (a, b) in enumerate(made)]
+    start_all(copies)
+    wait_all(copies)
+
+
+def pack(kernel, shape, count, name, table, *weights):
+    anywhere = pl.BlockSpec(memory_space=pl.ANY)
+    return pl.pallas_call(
+        kernel,
+        in_specs=[pl.BlockSpec(memory_space=pltpu.SMEM)] + [anywhere] * len(weights),
+        out_specs=pl.BlockSpec(memory_space=pltpu.VMEM),
+        out_shape=jax.ShapeDtypeStruct(shape, BF),
+        scratch_shapes=[pltpu.SemaphoreType.DMA((count,))],
+        name=name,
+    )(table, *weights)
+
+
+def attn_place_kernel(table, *refs):
+    *values, grad_qkv, grad_d = refs
+    core = table[0]
+    for pair in range(2):
+        for side in range(2):
+            value = values[pair * 2 + side]
+            half = core ^ side
+            rows = pl.ds(pl.multiple_of(half * 128, 128), 128)
+            for a, b in qkv_blocks(pair):
+                grad_qkv[rows, pl.ds(a, 128)] = value[0, :, pl.ds(b, 128)].astype(F32)
+            grad_d[rows_of(pair, 128), columns_at(half * 512, 512)] = value[0, :, pl.ds(1536, 512)].astype(F32)
+
+
+def mlp_place_kernel(table, *refs):
+    *values, grad_wi, grad_wo = refs
+    core = table[0]
+    for unit in range(2):
+        for side in range(2):
+            value = values[unit * 2 + side]
+            half = core ^ side
+            rows = pl.ds(pl.multiple_of(half * 128, 128), 128)
+            for tile in range(4):
+                grad_wi[rows, pl.ds(tile * 1024 + unit * 512, 512)] = value[0, rows_of(tile // 2, 128), rows_of(tile % 2, 512)].astype(F32)
+            for f in range(2):
+                for part in range(2):
+                    target = pl.ds(unit * 512 + f * 256 + part * 128, 128)
+                    grad_wo[target, columns_at(half * 512, 512)] = value[0, rows_of(2 + f, 128), rows_of(part, 512)].astype(F32)
+
+
+def place(kernel, shapes, name, table, *values):
+    inside = pl.BlockSpec(memory_space=pltpu.VMEM)
+    return pl.pallas_call(
+        kernel,
+        in_specs=[pl.BlockSpec(memory_space=pltpu.SMEM)] + [inside] * len(values),
+        out_specs=[inside] * len(shapes),
+        out_shape=[jax.ShapeDtypeStruct(shape, F32) for shape in shapes],
+        compiler_params=pltpu.CompilerParams(vmem_limit_bytes=VMEM),
+        name=name,
+    )(table, *values)
+
+
+def add_kernel(*refs):
+    *sources, target = refs
+    target[...] = sum(source[...].astype(F32) for source in sources).astype(BF)
+
+
+def add(*sources, count=1):
+    rows, columns = sources[0][0].shape[1:]
+    steps = 2
+    read = lambda first, stride: pl.BlockSpec(
+        (1, rows // steps, columns), lambda i: (first + stride * (i // steps), i % steps, 0)
+    )
+    return pl.pallas_call(
+        add_kernel,
+        grid=(count * steps,),
+        in_specs=[read(first, stride) for _, first, stride in sources],
+        out_specs=read(0, 1),
+        out_shape=jax.ShapeDtypeStruct((count, rows, columns), BF),
+        cost_estimate=LONG,
+        name="add",
+    )(*(array for array, _, _ in sources))
+
+
+def split_add_kernel(*refs):
+    *sources, first, second = refs
+    total = sum(source[...].astype(F32) for source in sources).astype(BF)
+    half = total.shape[1] // 2
+    first[...] = total[:, :half]
+    second[...] = total[:, half:]
+
+
+def split_add(*arrays):
+    rows, columns = arrays[0].shape[1:]
+    return pl.pallas_call(
+        split_add_kernel,
+        grid=(1,),
+        in_specs=[pl.BlockSpec((1, rows, columns), lambda i: (0, 0, 0))] * len(arrays),
+        out_specs=[pl.BlockSpec((1, rows // 2, columns), lambda i: (0, 0, 0))] * 2,
+        out_shape=[jax.ShapeDtypeStruct((1, rows // 2, columns), BF)] * 2,
+        cost_estimate=LONG,
+        name="split_add",
+    )(*arrays)
+
+
+def pair_add_kernel(first, got_first, second, got_second, first_out, second_out):
+    first_out[...] = (first[...].astype(F32) + got_first[...].astype(F32)).astype(BF)
+    second_out[...] = (second[...].astype(F32) + got_second[...].astype(F32)).astype(BF)
+
+
+def join_add_kernel(first, got_first, second, got_second, total):
+    half = first.shape[1]
+    total[:, :half] = (first[...].astype(F32) + got_first[...].astype(F32)).astype(BF)
+    total[:, half:] = (second[...].astype(F32) + got_second[...].astype(F32)).astype(BF)
+
+
+def halves_add(first, got_first, second, got_second, join=False):
+    block = lambda shape: pl.BlockSpec(shape, lambda i: (0, 0, 0))
+    one, rows, columns = first.shape
+    shapes = [(one, rows * 2, columns)] if join else [first.shape] * 2
+    return pl.pallas_call(
+        join_add_kernel if join else pair_add_kernel,
+        grid=(1,),
+        in_specs=[block(first.shape)] * 4,
+        out_specs=[block(shape) for shape in shapes],
+        out_shape=[jax.ShapeDtypeStruct(shape, BF) for shape in shapes],
+        cost_estimate=LONG,
+        name="halves_add",
+    )(first, got_first, second, got_second)
+
+
+AXES = ("z", "core", "y", "x")
+
+
+def exchange(value, partner):
+    pairs = []
+    for z in range(4):
+        for core in range(2):
+            for shard in range(4):
+                to_z, to_core, to_shard = partner(z, core, shard)
+                pairs.append(((z * 2 + core) * 4 + shard, (to_z * 2 + to_core) * 4 + to_shard))
+    return lax.ppermute(value, AXES, pairs)
+
+
+to_core = lambda z, core, shard: (z, 1 - core, shard)
+to_first = lambda z, core, shard: (z, core, shard ^ (1 + core))
+to_second = lambda z, core, shard: (z, core, shard ^ (2 - core))
+to_x = lambda z, core, shard: (z, core, shard ^ 1)
+to_y = lambda z, core, shard: (z, core, shard ^ 2)
+to_below = lambda z, core, shard: (z ^ 1, core, shard)
+to_above = lambda z, core, shard: (3 - z, core, shard)
+
+
+def wide(value):
+    return value.astype(F32)
+
+
+def shards(
+    layer_input, seq_lengths, out_grad, attn_gain, attn_shift, mlp_gain, mlp_shift, qkv_weight, qkv_bias,
+    dense_weight, dense_bias, inner_weight, inner_bias, outer_weight, outer_bias,
+):
+    core = lax.axis_index("core")
+    own = lax.axis_index("y") * 2 + lax.axis_index("x")
+    steps = jnp.where(core == 0, jnp.array([0, 2, 1, 3], jnp.int32), jnp.array([0, 1, 2, 3], jnp.int32))
+    shard_of = own ^ steps
+    difference = own ^ jnp.arange(4, dtype=jnp.int32)
+    block_of = jnp.where(core == 1, difference, ((difference & 1) << 1) | (difference >> 1))
+    table = jnp.concatenate([core[None].astype(jnp.int32), seq_lengths, block_of, shard_of]).astype(jnp.int32)
+
+    gather = lambda piece: lax.all_gather(piece, ("core", "y", "x"), axis=0, tiled=True)
+    pack_attn = lambda pair: pack(
+        functools.partial(attn_pack_kernel, pair), (1, 128, 2 * D), 13, "attn_pack", table, qkv_weight, dense_weight
+    )
+    pack_mlp = lambda unit: pack(
+        functools.partial(mlp_pack_kernel, unit), (1, 2, 128, 2 * D), 6, "mlp_pack", table, inner_weight, outer_weight
+    )
+    pieces = [gather(pack_attn(0)), gather(pack_mlp(0)), gather(pack_mlp(1)), gather(pack_attn(1))]
+
+    vectors = jnp.concatenate(
+        [attn_gain, attn_shift, mlp_gain, mlp_shift, dense_bias, outer_bias, qkv_bias, inner_bias]
+    )
+    vectors = lax.all_gather(vectors, ("y", "x"), axis=0, tiled=False).astype(F32)
+    cuts = np.cumsum([256] * 6 + [768, 1024])[:-1]
+    gain_a, shift_a, gain_m, shift_m, bias_d, bias_o, bias_qkv, bias_i = (
+        part.reshape(1, -1) for part in jnp.split(vectors, cuts, axis=1)
+    )
+    bias_pairs = jnp.transpose(bias_qkv.reshape(3, 2, 2, 2, 128), (3, 1, 0, 2, 4)).reshape(2, 1, 1536)
+    bias_units = jnp.swapaxes(bias_i.reshape(4, 2, 512), 0, 1).reshape(2, 1, 2048)
+
+    na, nm, gr = norm(table, layer_input, out_grad, (gain_a, shift_a, gain_m, shift_m))
+    tables = [jnp.asarray(t) for t in rotary_tables()]
+
+    def after(done, *values):
+        return lax.optimization_barrier((done,) + values)
+
+    far_blocks = lambda keep, got: add((keep, 2, 1), (got, 1, 2), count=2)
+    near_block = lambda keep, got, far: add((keep, 1, 1), (got, 2, 1), (far, 1, 1))
+    own_block = lambda *arrays: add(*((array, 0, 1) for array in arrays))
+    plus = lambda total, got: add((total, 0, 1), (got, 0, 1))
+
+    none = (None, None)
+    attn_call = lambda first, count, pair, parts, totals: attn_unit(
+        first, count, table, na, gr, bias_pairs[pair], tables, pieces[3 * pair], parts, totals
+    )
+    mlp_call = lambda first, count, unit, parts, totals: mlp_unit(
+        first, count, table, nm, gr, bias_units[unit], pieces[1 + unit], parts, totals
+    )
+
+    keep_a, send_a, gb0, out, dna = attn_call(0, 2, 0, none, none)
+    got_a = exchange(send_a, to_core)
+
+    keep_m, send_m, gbi0a, out, dnm = mlp_call(0, 2, 0, none, (out, None))
+    out, keep_a, got_a = after(out, keep_a, got_a)
+    far_a = far_blocks(keep_a, got_a)
+    out, far_a = after(out, far_a)
+    far_a = exchange(far_a, to_first)
+
+    keep_m, send_m, gbi0b, out, dnm = mlp_call(2, 2, 0, (keep_m, send_m), (out, dnm))
+    got_m = exchange(send_m, to_core)
+    out, keep_a, got_a, far_a = after(out, keep_a, got_a, far_a)
+    near_a = near_block(keep_a, got_a, far_a)
+    near_a, keep_m, got_m = after(near_a, keep_m, got_m)
+    far_m = far_blocks(keep_m, got_m)
+    out, near_a, far_m = after(out, near_a, far_m)
+    near_a = exchange(near_a, to_second)
+    far_m = exchange(far_m, to_first)
+
+    keep_n, send_n, gbi1a, out, dnm = mlp_call(0, 2, 1, none, (out, dnm))
+    out, keep_a, got_a, far_a, near_a, keep_m, got_m, far_m = after(
+        out, keep_a, got_a, far_a, near_a, keep_m, got_m, far_m
+    )
+    total_a = own_block(keep_a, got_a, far_a, near_a)
+    near_m = near_block(keep_m, got_m, far_m)
+    out, total_a, near_m = after(out, total_a, near_m)
+    got_total_a = exchange(total_a, to_below)
+    near_m = exchange(near_m, to_second)
+
+    keep_n, send_n, gbi1b, out, dnm = mlp_call(2, 2, 1, (keep_n, send_n), (out, dnm))
+    got_n = exchange(send_n, to_core)
+    out, total_a, got_total_a, keep_m, got_m, far_m, near_m = after(
+        out, total_a, got_total_a, keep_m, got_m, far_m, near_m
+    )
+    total_a = plus(total_a, got_total_a)
+    total_m = own_block(keep_m, got_m, far_m, near_m)
+    total_m, total_a, keep_n, got_n = after(total_m, total_a, keep_n, got_n)
+    far_n = far_blocks(keep_n, got_n)
+    out, total_a, total_m, far_n = after(out, total_a, total_m, far_n)
+    got_total_a = exchange(total_a, to_above)
+    got_total_m = exchange(total_m, to_below)
+    far_n = exchange(far_n, to_first)
+
+    keep_b, send_b, gb1a, out, dna = attn_call(0, 1, 1, none, (out, dna))
+    out, total_a, got_total_a, total_m, got_total_m, keep_n, got_n, far_n = after(
+        out, total_a, got_total_a, total_m, got_total_m, keep_n, got_n, far_n
+    )
+    total_a = plus(total_a, got_total_a)
+    total_m = plus(total_m, got_total_m)
+    near_n = near_block(keep_n, got_n, far_n)
+    out, total_a, total_m, near_n = after(out, total_a, total_m, near_n)
+    other_a = exchange(total_a, to_core)
+    got_total_m = exchange(total_m, to_above)
+    near_n = exchange(near_n, to_second)
+
+    keep_b, send_b, gb1b, out, dna = attn_call(1, 1, 1, (keep_b, send_b), (out, dna))
+    got_b = exchange(send_b, to_core)
+    out, total_m, got_total_m, keep_n, got_n, far_n, near_n, other_a = after(
+        out, total_m, got_total_m, keep_n, got_n, far_n, near_n, other_a
+    )
+    first_n, second_n = split_add(keep_n, got_n, far_n, near_n)
+    total_m = plus(total_m, got_total_m)
+    out, total_m, first_n, second_n = after(out, total_m, first_n, second_n)
+    got_first_n = exchange(first_n, to_below)
+    got_second_n = exchange(second_n, to_above)
+    other_m = exchange(total_m, to_core)
+    layer_output = output(layer_input, out, bias_d + bias_o)
+    layer_output, keep_b, got_b = after(layer_output, keep_b, got_b)
+    far_b = far_blocks(keep_b, got_b)
+
+    bias_sums = [
+        gb0,
+        jnp.concatenate([gb1a, gb1b], axis=1),
+        jnp.concatenate([gbi0a, gbi0b], axis=1),
+        jnp.concatenate([gbi1a, gbi1b], axis=1),
+    ]
+    far_b, dna, dnm = after(far_b, dna, dnm)
+    far_b = exchange(far_b, to_first)
+    input_grad, small = finish(table, layer_input, gr, dna, dnm, (gain_a, gain_m), bias_sums)
+    small, far_b, keep_b, got_b = after(small, far_b, keep_b, got_b)
+    near_b = near_block(keep_b, got_b, far_b)
+    near_b, got_first_n, got_second_n, first_n, second_n = after(near_b, got_first_n, got_second_n, first_n, second_n)
+    near_b = exchange(near_b, to_second)
+    first_n, second_n = halves_add(first_n, got_first_n, second_n, got_second_n)
+    first_n, second_n, near_b = after(first_n, second_n, near_b)
+    got_first_n = exchange(first_n, to_above)
+    got_second_n = exchange(second_n, to_below)
+    first_b, second_b = split_add(keep_b, got_b, far_b, near_b)
+    got_first_b = exchange(first_b, to_below)
+    got_second_b = exchange(second_b, to_above)
+    (total_n,) = halves_add(first_n, got_first_n, second_n, got_second_n, join=True)
+    other_n = exchange(total_n, to_core)
+    first_b, second_b = halves_add(first_b, got_first_b, second_b, got_second_b)
+    got_first_b = exchange(first_b, to_above)
+    got_second_b = exchange(second_b, to_below)
+    (total_b,) = halves_add(first_b, got_first_b, second_b, got_second_b, join=True)
+    other_b = exchange(total_b, to_core)
+
+    grad_wi, grad_wo = place(
+        mlp_place_kernel, ((256, FF), (1024, D)), "mlp_place", table, total_m, other_m, total_n, other_n
+    )
+    grad_qkv, grad_d = place(
+        attn_place_kernel, ((256, 3 * D), (256, D)), "attn_place", table, total_a, other_a, total_b, other_b
+    )
+
+    for partner in (to_core, to_x, to_y, to_below, to_above):
+        small = small + exchange(small, partner)
+    small = lax.dynamic_index_in_dim(small, own, 0, keepdims=False)
+    g_ga, g_sa, g_gm, g_sm, g_bd, g_bqkv, g_bi = jnp.split(small, np.cumsum([256] * 5 + [768]))
+    return (
+        layer_output, input_grad, g_ga, g_sa, g_gm, g_sm, grad_qkv, g_bqkv, grad_d, g_bd, grad_wi, g_bi, grad_wo, g_bd,
+    )
+
+
 def solution(mesh):
     replicas, shard_count = mesh.shape["rep"], mesh.shape["shard"]
     shape = (replicas // 2, 2, 2, shard_count // 2)
@@ -324,8 +1148,9 @@
     shard = P(("y", "x"))
     matrix = P(("y", "x"), None)
     weights = (shard,) * 4 + (matrix, shard) * 4
+    body = shards if (replicas, shard_count) == (8, 4) else general_shards
     return jax.shard_map(
-        shards,
+        body,
         mesh=cut,
         in_specs=(both, P(("z", "core", "y", "x")), both) + weights,
         out_specs=(both, both) + weights,

time: 753 us -> 479 us (0.64)
  waiting for transfers between devices: 441 us -> 80.7 us
  Pallas kernels: 162 us -> 303 us
  blocking collectives: 61.1 us -> 9.86 us
  starting transfers between devices: 0.75 us -> 47.1 us
  local copies, waits for them, and re-layouts: 38.9 us -> 11.2 us
  other arithmetic: 33.9 us -> 6.63 us
    reduce_scatter x12 -> x0, waiting for transfers between devices: 269 us -> none  [the longest x6 235 us: reduce(): part = lax.psum_scatter(part, ('y', 'x'), scatter_dimension=0, tiled=True)]
    pallas_call x2 -> x36, Pallas kernels: 162 us -> 303 us  [the longest x3 116 us: attn_unit(): pl.pallas_call(functools.partial(attn_unit_kernel, first, count, given),...]
    psum x1 -> x0, waiting for transfers between devices: 126 us -> none  [reduce(): part = lax.psum(part, 'z')]
    ppermute x0 -> x33, waiting for transfers between devices: none -> 68.1 us  [exchange(): return lax.ppermute(value, AXES, pairs)]
    ppermute x0 -> x33, starting transfers between devices: none -> 46.9 us  [exchange(): return lax.ppermute(value, AXES, pairs)]
    all_gather x6 -> x4, waiting for transfers between devices: 41.6 us -> 12.5 us  [shards(): lax.all_gather(piece, ('core', 'y', 'x'), axis=0, tiled=True)]
    psum x1 -> x0, blocking collectives: 26.2 us -> none  [shards(): small = lax.psum(small, ('z', 'core'))]
    unnamed x1 -> x0, blocking collectives: 16.5 us -> none
  transfers between devices with their start and end apart: 19 -> 37, of which waited for: 10 -> 15; matrix products, arithmetic and copies ran while one was open for 9% -> 3% of each run, Pallas kernels for 22% -> 60%
where the time goes in v2:
time: 479 us; the launch traced here: 474 us
  Pallas kernels  303 us (63%)
  waiting for transfers between devices  80.7 us (17%)
  starting transfers between devices  47.1 us (10%)
  between operations  15 us (3%)
  local copies, waits for them, and re-layouts  11.2 us (2%)
  blocking collectives  9.86 us (2%)
  other arithmetic  6.63 us (1%)
    pallas_call x3, Pallas kernels, attn_unit(): pl.pallas_call(functools.partial(attn_unit_kernel, first, count, given),...  116 us
    pallas_call x4, Pallas kernels, mlp_unit(): pl.pallas_call(functools.partial(mlp_unit_kernel, first, count, given), g...  89 us
    ppermute x33, waiting for transfers between devices, exchange(): return lax.ppermute(value, AXES, pairs)  68.1 us
    ppermute x33, starting transfers between devices, exchange(): return lax.ppermute(value, AXES, pairs)  46.9 us
    pallas_call x14, Pallas kernels, add(): pl.pallas_call(add_kernel, grid=(count * steps,), in_specs=[read(first, s...  40.6 us
    all_gather x4, waiting for transfers between devices, shards(): lax.all_gather(piece, ('core', 'y', 'x'), axis=0, tiled=True)  12.5 us
    pallas_call x4, Pallas kernels, pack(): pl.pallas_call(kernel, in_specs=[pl.BlockSpec(memory_space=pltpu.SMEM)] +...  11.4 us
    pallas_call x2, Pallas kernels, place(): pl.pallas_call(kernel, in_specs=[pl.BlockSpec(memory_space=pltpu.SMEM)] +...  9.98 us
  transfers between devices with their start and end apart: 37, of which 15 were waited for; matrix products, arithmetic and copies ran while one was open for 3% of the time, Pallas kernels for 60%

profile of v2, /device:TPU:0, one launch (start us, length us, event | category | flops | bytes accessed | tf_op | source)
XLA Modules:
  0.0 473.8 jit_solution(10498023956104097268)
XLA Ops:
  22.8 9.9 %all-gather.1 = bf16[4,1,3328]{2,1,0:T(2,128)(2,1)S(1)} all-gather(bf16[1,1,3328]{2,1,0:T(2,128)(2,1)S(1)} %reshape.86), channel_id=2, replica_groups=mesh['z'=4,'core'=2,'y'=2,'x'=2] {'y','x'}, dimensions={0}, use_global_device_ids=true | all-gather | bytes 33280 | tf_op jit(solution)/shard_map/all_gather | solution.py:1002
  37.5 6.3 %norm.1 = (bf16[1024,1024]{1,0:T(8,128)(2,1)}, bf16[1024,1024]{1,0:T(8,128)(2,1)}, bf16[1024,1024]{1,0:T(8,128)(2,1)}) custom-call(s32[10]{0:T(128)} %pad_add_fusion.table, bf16[1024,1024]{1,0:T(8,128)(2,1)} %x.5, bf16[1024,1024]{1,0:T(8,128)(2,1)} %grad.1, f32[1,1024]{1,0:T(1,128)} %bitcast.49, f32[1,1024]{1,0:T(1,128)} %bitcast.53, f32[1,1024]{1,0:T(1,128)} %bitcast.51, ...), custom_call_target="tpu_custom_call" | custom-call | flops 10485760 | bytes 10485760 | tf_op jit(solution)/shard_map/norm/pallas_call | solution.py:347
  43.9 7.9 %all-gather.13.cloned.1.call-done.pieces = bf16[8,128,2048]{2,1,0:T(8,128)(2,1)} async-done(((bf16[1,128,2048]{2,1,0:T(8,128)(2,1)}), bf16[8,128,2048]{2,1,0:T(8,128)(2,1)}) %all-gather.13.cloned.1.call-update) | async-done | bytes 4194320 | tf_op jit(solution)/shard_map/all_gather | solution.py:990
  51.8 53.4 %attn_unit.3 = (bf16[4,128,2048]{2,1,0:T(8,128)(2,1)}, bf16[4,128,2048]{2,1,0:T(8,128)(2,1)}, f32[1,1536]{1,0:T(1,128)}, f32[1024,1024]{1,0:T(8,128)}, f32[1024,1024]{1,0:T(8,128)}) custom-call(s32[10]{0:T(128)} %pad_add_fusion.table, bf16[1024,1024]{1,0:T(8,128)(2,1)} %get-tuple-element.149.na, bf16[1024,1024]{1,0:T(8,128)(2,1)} %get-tuple-element.150.gr, ...), custom_call_target="tpu_custom_call" | custom-call | flops 9999999827968 | bytes 1048576 | tf_op jit(solution)/shard_map/attn_unit/pallas_call | solution.py:769
  105.5 4.6 all-gather.11.cloned.1.call-done.pieces
  110.1 21.0 %mlp_unit.4 = (bf16[4,512,1024]{2,1,0:T(8,128)(2,1)}, bf16[4,512,1024]{2,1,0:T(8,128)(2,1)}, f32[1,1024]{1,0:T(1,128)}, f32[1024,1024]{1,0:T(8,128)}, f32[1024,1024]{1,0:T(8,128)}) custom-call(s32[10]{0:T(128)} %pad_add_fusion.table, bf16[1024,1024]{1,0:T(8,128)(2,1)} %get-tuple-element.151.nm, ...), custom_call_target="tpu_custom_call", output_to_operand_aliasing={{3}: (5, {})} | custom-call | flops 9999999827968 | bytes 1048576 | tf_op jit(solution)/shard_map/mlp_unit/pallas_call | solution.py:576
  131.2 3.6 add.61
  136.3 23.3 %mlp_unit.5 = (bf16[4,512,1024]{2,1,0:T(8,128)(2,1)}, bf16[4,512,1024]{2,1,0:T(8,128)(2,1)}, f32[1,1024]{1,0:T(1,128)}, f32[1024,1024]{1,0:T(8,128)}, f32[1024,1024]{1,0:T(8,128)}) custom-call(s32[10]{0:T(128)} %pad_add_fusion.table, ...), custom_call_target="tpu_custom_call", output_to_operand_aliasing={{0}: (5, {}), {1}: (6, {}), {3}: (7, {}), {4}: (8, {})} | custom-call | flops 9999999827968 | bytes 1048576 | tf_op jit(solution)/shard_map/mlp_unit/pallas_call | solution.py:576
  161.0 4.7 collective-permute-done.1.refs_2_
  167.8 4.4 add.63
  174.7 22.5 %mlp_unit.6 = (bf16[4,512,1024]{2,1,0:T(8,128)(2,1)}, bf16[4,512,1024]{2,1,0:T(8,128)(2,1)}, f32[1,1024]{1,0:T(1,128)}, f32[1024,1024]{1,0:T(8,128)}, f32[1024,1024]{1,0:T(8,128)}) custom-call(s32[10]{0:T(128)} %pad_add_fusion.table, bf16[1024,1024]{1,0:T(8,128)(2,1)} %get-tuple-element.151.nm, ...), custom_call_target="tpu_custom_call", output_to_operand_aliasing={{3}: (5, {}), {4}: (6, {})} | custom-call | flops 9999999827968 | bytes 1048576 | tf_op jit(solution)/shard_map/mlp_unit/pallas_call | solution.py:576
  197.2 22.4 %collective-permute-done.4.refs_2_ = bf16[2,512,1024]{2,1,0:T(8,128)(2,1)} collective-permute-done((bf16[2,512,1024]{2,1,0:T(8,128)(2,1)}, bf16[2,512,1024]{2,1,0:T(8,128)(2,1)}, u32[]{:S(2)}, u32[]{:S(2)}) %collective-permute-start.4) | collective-permute-done | bytes 2097184 | tf_op jit(solution)/shard_map/ppermute | solution.py:962
  225.6 22.2 %mlp_unit.7 = (bf16[4,512,1024]{2,1,0:T(8,128)(2,1)}, bf16[4,512,1024]{2,1,0:T(8,128)(2,1)}, f32[1,1024]{1,0:T(1,128)}, f32[1024,1024]{1,0:T(8,128)}, f32[1024,1024]{1,0:T(8,128)}) custom-call(s32[10]{0:T(128)} %pad_add_fusion.table, ...), custom_call_target="tpu_custom_call", output_to_operand_aliasing={{0}: (5, {}), {1}: (6, {}), {3}: (7, {}), {4}: (8, {})} | custom-call | flops 9999999827968 | bytes 1048576 | tf_op jit(solution)/shard_map/mlp_unit/pallas_call | solution.py:576
  251.1 3.2 add.66.refs_0_
  255.4 4.3 add.68
  262.2 3.1 collective-permute-start.8
  265.3 31.1 %attn_unit.4 = (bf16[4,128,2048]{2,1,0:T(8,128)(2,1)}, bf16[4,128,2048]{2,1,0:T(8,128)(2,1)}, f32[1,768]{1,0:T(1,128)}, f32[1024,1024]{1,0:T(8,128)}, f32[1024,1024]{1,0:T(8,128)}) custom-call(s32[10]{0:T(128)} %pad_add_fusion.table, bf16[1024,1024]{1,0:T(8,128)(2,1)} %get-tuple-element.149.na, ...), custom_call_target="tpu_custom_call", output_to_operand_aliasing={{3}: (8, {}), {4}: (9, {})} | custom-call | flops 9999999827968 | bytes 1048576 | tf_op jit(solution)/shard_map/attn_unit/pallas_call | solution.py:769
  296.4 3.4 collective-permute-done.8.refs_1_
  308.8 31.3 %attn_unit.5 = (bf16[4,128,2048]{2,1,0:T(8,128)(2,1)}, bf16[4,128,2048]{2,1,0:T(8,128)(2,1)}, f32[1,768]{1,0:T(1,128)}, f32[1024,1024]{1,0:T(8,128)}, f32[1024,1024]{1,0:T(8,128)}) custom-call(s32[10]{0:T(128)} %pad_add_fusion.table, ...), custom_call_target="tpu_custom_call", output_to_operand_aliasing={{0}: (8, {}), {1}: (9, {}), {3}: (10, {}), {4}: (11, {})} | custom-call | flops 9999999827968 | bytes 1048576 | tf_op jit(solution)/shard_map/attn_unit/pallas_call | solution.py:769
  344.4 3.5 split_add.2
  347.9 8.6 %collective-permute-start.21 = (bf16[1,256,1024]{2,1,0:T(8,128)(2,1)}, bf16[1,256,1024]{2,1,0:T(8,128)(2,1)}, u32[]{:S(2)}, u32[]{:S(2)}) collective-permute-start(bf16[1,256,1024]{2,1,0:T(8,128)(2,1)} %get-tuple-element.265.first), channel_id=1, source_target_pairs={{0,8},{1,9},{2,10},{3,11},{4,12},{5,13},{6,14},{7,15},{8,0},{9,1},... | collective-permute-start | bytes 1572872 | tf_op jit(solution)/shard_map/ppermute | solution.py:962
  358.1 5.2 %output.1 = f32[1024,1024]{1,0:T(8,128)} custom-call(bf16[1024,1024]{1,0:T(8,128)(2,1)} %x.5, f32[1024,1024]{1,0:T(8,128)} %get-tuple-element.238.out, f32[1,1024]{1,0:T(1,128)} %bitcast.64), custom_call_target="tpu_custom_call" | custom-call | flops 9999999827968 | bytes 1048576 | tf_op jit(solution)/shard_map/output/pallas_call | solution.py:366
  363.3 3.6 add.73
  367.2 9.4 %finish.1 = (f32[1024,1024]{1,0:T(8,128)}, f32[4,3072]{1,0:T(4,128)}) custom-call(s32[10]{0:T(128)} %pad_add_fusion.table, bf16[1024,1024]{1,0:T(8,128)(2,1)} %x.5, bf16[1024,1024]{1,0:T(8,128)(2,1)} %get-tuple-element.150.gr, f32[1024,1024]{1,0:T(8,128)} %get-tuple-element.246.dna, f32[1024,1024]{1,0:T(8,128)} %get-tuple-element.247.dnm, ...), custom_call_target="tpu_custom_call" | custom-call | flops 9999999827968 | bytes 1048576 | tf_op jit(solution)/shard_map/finish/pallas_call | solution.py:420
  376.6 5.5 %collective-permute-done.15.refs_2_ = bf16[2,128,2048]{2,1,0:T(8,128)(2,1)} collective-permute-done((bf16[2,128,2048]{2,1,0:T(8,128)(2,1)}, bf16[2,128,2048]{2,1,0:T(8,128)(2,1)}, u32[]{:S(2)}, u32[]{:S(2)}) %collective-permute-start.15) | collective-permute-done | bytes 1048608 | tf_op jit(solution)/shard_map/ppermute | solution.py:962
  387.4 6.6 %collective-permute-done.23.refs_3_ = bf16[1,128,2048]{2,1,0:T(8,128)(2,1)} collective-permute-done((bf16[1,128,2048]{2,1,0:T(8,128)(2,1)}, bf16[1,128,2048]{2,1,0:T(8,128)(2,1)}, u32[]{:S(2)}, u32[]{:S(2)}) %collective-permute-start.23) | collective-permute-done | bytes 524320 | tf_op jit(solution)/shard_map/ppermute | solution.py:962
  400.3 3.8 collective-permute-done.17
  404.6 3.6 collective-permute-done.18
  422.0 9.7 %collective-permute-done.30.got_first = bf16[1,256,1024]{2,1,0:T(8,128)(2,1)} collective-permute-done((bf16[1,256,1024]{2,1,0:T(8,128)(2,1)}, bf16[1,256,1024]{2,1,0:T(8,128)(2,1)}, u32[]{:S(2)}, u32[]{:S(2)}) %collective-permute-start.30) | collective-permute-done | bytes 524320 | tf_op jit(solution)/shard_map/ppermute | solution.py:962
  431.7 13.4 %collective-permute-start.27 = (bf16[1,64,2048]{2,1,0:T(8,128)(2,1)}, bf16[1,64,2048]{2,1,0:T(8,128)(2,1)}, u32[]{:S(2)}, u32[]{:S(2)}) collective-permute-start(bf16[1,64,2048]{2,1,0:T(8,128)(2,1)} %get-tuple-element.276.second), channel_id=1, source_target_pairs={{0,8},{1,9},{2,10},{3,11},{4,12},{5,13},{6,14},{7,15},{8,0},{9,1},... | collective-permute-start | bytes 786440 | tf_op jit(solution)/shard_map/ppermute | solution.py:962
  456.5 3.9 attn_place.1
  460.5 6.1 %mlp_place.1 = (f32[256,4096]{1,0:T(8,128)}, f32[1024,1024]{1,0:T(8,128)}) custom-call(s32[10]{0:T(128)} %pad_add_fusion.table, bf16[1,512,1024]{2,1,0:T(8,128)(2,1)} %add.72.refs_0_, bf16[1,512,1024]{2,1,0:T(8,128)(2,1)} %collective-permute-done.29.refs_1_, bf16[1,512,1024]{2,1,0:T(8,128)(2,1)} %halves_add.7.refs_2_, ...), custom_call_target="tpu_custom_call" | custom-call | tf_op jit(solution)/shard_map/mlp_place/pallas_call | solution.py:873
  (154 shorter events, 93.2 us)
Async XLA Ops:
  7.2 44.6 %all-gather.13.cloned.1.call-start = ((), (), s32[]{:S(2)}) async-start(), calls=%async_computation.3 | async-start | bytes 4718592 | tf_op jit(solution)/shard_map/all_gather | solution.py:990
  11.9 98.2 %all-gather.11.cloned.1.call-start = ((), (), s32[]{:S(2)}) async-start(), calls=%async_computation.2 | async-start | bytes 9437184 | tf_op jit(solution)/shard_map/all_gather | solution.py:990
  15.1 159.6 %all-gather.9.cloned.1.call-start = ((), (), s32[]{:S(2)}) async-start(), calls=%async_computation.1 | async-start | bytes 9437184 | tf_op jit(solution)/shard_map/all_gather | solution.py:990
  18.1 247.2 %all-gather.7.cloned.1.call-start = ((), (), s32[]{:S(2)}) async-start(), calls=%async_computation | async-start | bytes 4718592 | tf_op jit(solution)/shard_map/all_gather | solution.py:990
  105.2 25.9 %collective-permute-start = (bf16[4,128,2048]{2,1,0:T(8,128)(2,1)}, bf16[4,128,2048]{2,1,0:T(8,128)(2,1)}, u32[]{:S(2)}, u32[]{:S(2)}) collective-permute-start(bf16[4,128,2048]{2,1,0:T(8,128)(2,1)} %get-tuple-element.157), channel_id=1, source_target_pairs={{0,4},{1,5},{2,6},{3,7},{4,0},{5,1},{6,2},{7,3},{8,12},{9,13},{10,... | collective-permute-start | bytes 6291464 | tf_op jit(solution)/shard_map/ppermute | solution.py:962
  134.8 30.9 %collective-permute-start.1 = (bf16[2,128,2048]{2,1,0:T(8,128)(2,1)}, bf16[2,128,2048]{2,1,0:T(8,128)(2,1)}, u32[]{:S(2)}, u32[]{:S(2)}) collective-permute-start(bf16[2,128,2048]{2,1,0:T(8,128)(2,1)} %add.61), channel_id=1, source_target_pairs={{0,1},{1,0},{2,3},{3,2},{4,6},{5,7},{6,4},{7,5},{8,9},{9,8},{10,11... | collective-permute-start | bytes 3145736 | tf_op jit(solution)/shard_map/ppermute | solution.py:962
  159.6 8.2 %collective-permute-start.2 = (bf16[4,512,1024]{2,1,0:T(8,128)(2,1)}, bf16[4,512,1024]{2,1,0:T(8,128)(2,1)}, u32[]{:S(2)}, u32[]{:S(2)}) collective-permute-start(bf16[4,512,1024]{2,1,0:T(8,128)(2,1)} %get-tuple-element.170), channel_id=1, source_target_pairs={{0,4},{1,5},{2,6},{3,7},{4,0},{5,1},{6,2},{7,3},{8,12},{9,13},{10,... | collective-permute-start | bytes 12582920 | tf_op jit(solution)/shard_map/ppermute | solution.py:962
  172.2 47.4 %collective-permute-start.4 = (bf16[2,512,1024]{2,1,0:T(8,128)(2,1)}, bf16[2,512,1024]{2,1,0:T(8,128)(2,1)}, u32[]{:S(2)}, u32[]{:S(2)}) collective-permute-start(bf16[2,512,1024]{2,1,0:T(8,128)(2,1)} %add.63), channel_id=1, source_target_pairs={{0,1},{1,0},{2,3},{3,2},{4,6},{5,7},{6,4},{7,5},{8,9},{9,8},{10,11... | collective-permute-start | bytes 6291464 | tf_op jit(solution)/shard_map/ppermute | solution.py:962
  174.7 22.5 %collective-permute-start.3 = (bf16[1,128,2048]{2,1,0:T(8,128)(2,1)}, bf16[1,128,2048]{2,1,0:T(8,128)(2,1)}, u32[]{:S(2)}, u32[]{:S(2)}) collective-permute-start(bf16[1,128,2048]{2,1,0:T(8,128)(2,1)} %add.62), channel_id=1, source_target_pairs={{0,2},{1,3},{2,0},{3,1},{4,5},{5,4},{6,7},{7,6},{8,10},{9,11},{10,... | collective-permute-start | bytes 1572872 | tf_op jit(solution)/shard_map/ppermute | solution.py:962
  224.8 24.3 %collective-permute-start.6 = (bf16[1,512,1024]{2,1,0:T(8,128)(2,1)}, bf16[1,512,1024]{2,1,0:T(8,128)(2,1)}, u32[]{:S(2)}, u32[]{:S(2)}) collective-permute-start(bf16[1,512,1024]{2,1,0:T(8,128)(2,1)} %add.65), channel_id=1, source_target_pairs={{0,2},{1,3},{2,0},{3,1},{4,5},{5,4},{6,7},{7,6},{8,10},{9,11},{10,... | collective-permute-start | bytes 3145736 | tf_op jit(solution)/shard_map/ppermute | solution.py:962
  224.8 24.3 %collective-permute-start.5 = (bf16[1,128,2048]{2,1,0:T(8,128)(2,1)}, bf16[1,128,2048]{2,1,0:T(8,128)(2,1)}, u32[]{:S(2)}, u32[]{:S(2)}) collective-permute-start(bf16[1,128,2048]{2,1,0:T(8,128)(2,1)} %add.64.refs_0_), channel_id=1, source_target_pairs={{0,8},{1,9},{2,10},{3,11},{4,12},{5,13},{6,14},{7,15},{8,0},{9,1},... | collective-permute-start | bytes 1572872 | tf_op jit(solution)/shard_map/ppermute | solution.py:962
  247.8 7.6 %collective-permute-start.7 = (bf16[4,512,1024]{2,1,0:T(8,128)(2,1)}, bf16[4,512,1024]{2,1,0:T(8,128)(2,1)}, u32[]{:S(2)}, u32[]{:S(2)}) collective-permute-start(bf16[4,512,1024]{2,1,0:T(8,128)(2,1)} %get-tuple-element.202), channel_id=1, source_target_pairs={{0,4},{1,5},{2,6},{3,7},{4,0},{5,1},{6,2},{7,3},{8,12},{9,13},{10,... | collective-permute-start | bytes 12582920 | tf_op jit(solution)/shard_map/ppermute | solution.py:962
  259.7 40.2 %collective-permute-start.10 = (bf16[2,512,1024]{2,1,0:T(8,128)(2,1)}, bf16[2,512,1024]{2,1,0:T(8,128)(2,1)}, u32[]{:S(2)}, u32[]{:S(2)}) collective-permute-start(bf16[2,512,1024]{2,1,0:T(8,128)(2,1)} %add.68), channel_id=1, source_target_pairs={{0,1},{1,0},{2,3},{3,2},{4,6},{5,7},{6,4},{7,5},{8,9},{9,8},{10,11... | collective-permute-start | bytes 6291464 | tf_op jit(solution)/shard_map/ppermute | solution.py:962
  261.6 38.3 %collective-permute-start.9 = (bf16[1,512,1024]{2,1,0:T(8,128)(2,1)}, bf16[1,512,1024]{2,1,0:T(8,128)(2,1)}, u32[]{:S(2)}, u32[]{:S(2)}) collective-permute-start(bf16[1,512,1024]{2,1,0:T(8,128)(2,1)} %add.66.refs_0_), channel_id=1, source_target_pairs={{0,8},{1,9},{2,10},{3,11},{4,12},{5,13},{6,14},{7,15},{8,0},{9,1},... | collective-permute-start | bytes 3145736 | tf_op jit(solution)/shard_map/ppermute | solution.py:962
  262.2 37.7 %collective-permute-start.8 = (bf16[1,128,2048]{2,1,0:T(8,128)(2,1)}, bf16[1,128,2048]{2,1,0:T(8,128)(2,1)}, u32[]{:S(2)}, u32[]{:S(2)}) collective-permute-start(bf16[1,128,2048]{2,1,0:T(8,128)(2,1)} %add.67.refs_0_), channel_id=1, source_target_pairs={{0,24},{1,25},{2,26},{3,27},{4,28},{5,29},{6,30},{7,31},{8,16},{9,... | collective-permute-start | bytes 1572872 | tf_op jit(solution)/shard_map/ppermute | solution.py:962
  307.1 34.9 %collective-permute-start.11 = (bf16[1,512,1024]{2,1,0:T(8,128)(2,1)}, bf16[1,512,1024]{2,1,0:T(8,128)(2,1)}, u32[]{:S(2)}, u32[]{:S(2)}) collective-permute-start(bf16[1,512,1024]{2,1,0:T(8,128)(2,1)} %add.70.refs_0_), channel_id=1, source_target_pairs={{0,24},{1,25},{2,26},{3,27},{4,28},{5,29},{6,30},{7,31},{8,16},{9,... | collective-permute-start | bytes 3145736 | tf_op jit(solution)/shard_map/ppermute | solution.py:962
  308.5 33.5 %collective-permute-start.12 = (bf16[1,512,1024]{2,1,0:T(8,128)(2,1)}, bf16[1,512,1024]{2,1,0:T(8,128)(2,1)}, u32[]{:S(2)}, u32[]{:S(2)}) collective-permute-start(bf16[1,512,1024]{2,1,0:T(8,128)(2,1)} %add.71), channel_id=1, source_target_pairs={{0,2},{1,3},{2,0},{3,1},{4,5},{5,4},{6,7},{7,6},{8,10},{9,11},{10,... | collective-permute-start | bytes 3145736 | tf_op jit(solution)/shard_map/ppermute | solution.py:962
  308.8 33.2 %collective-permute-start.13 = (bf16[1,128,2048]{2,1,0:T(8,128)(2,1)}, bf16[1,128,2048]{2,1,0:T(8,128)(2,1)}, u32[]{:S(2)}, u32[]{:S(2)}) collective-permute-start(bf16[1,128,2048]{2,1,0:T(8,128)(2,1)} %add.69.refs_0_), channel_id=1, source_target_pairs={{0,4},{1,5},{2,6},{3,7},{4,0},{5,1},{6,2},{7,3},{8,12},{9,13},{10,... | collective-permute-start | bytes 1572872 | tf_op jit(solution)/shard_map/ppermute | solution.py:962
  340.1 23.2 %collective-permute-start.14 = (bf16[4,128,2048]{2,1,0:T(8,128)(2,1)}, bf16[4,128,2048]{2,1,0:T(8,128)(2,1)}, u32[]{:S(2)}, u32[]{:S(2)}) collective-permute-start(bf16[4,128,2048]{2,1,0:T(8,128)(2,1)} %get-tuple-element.240), channel_id=1, source_target_pairs={{0,4},{1,5},{2,6},{3,7},{4,0},{5,1},{6,2},{7,3},{8,12},{9,13},{10,... | collective-permute-start | bytes 6291464 | tf_op jit(solution)/shard_map/ppermute | solution.py:962
  347.9 36.5 %collective-permute-start.21 = (bf16[1,256,1024]{2,1,0:T(8,128)(2,1)}, bf16[1,256,1024]{2,1,0:T(8,128)(2,1)}, u32[]{:S(2)}, u32[]{:S(2)}) collective-permute-start(bf16[1,256,1024]{2,1,0:T(8,128)(2,1)} %get-tuple-element.265.first), channel_id=1, source_target_pairs={{0,8},{1,9},{2,10},{3,11},{4,12},{5,13},{6,14},{7,15},{8,0},{9,1},... | collective-permute-start | bytes 1572872 | tf_op jit(solution)/shard_map/ppermute | solution.py:962
  356.5 27.9 %collective-permute-start.22 = (bf16[1,256,1024]{2,1,0:T(8,128)(2,1)}, bf16[1,256,1024]{2,1,0:T(8,128)(2,1)}, u32[]{:S(2)}, u32[]{:S(2)}) collective-permute-start(bf16[1,256,1024]{2,1,0:T(8,128)(2,1)} %get-tuple-element.267.second), channel_id=1, source_target_pairs={{0,24},{1,25},{2,26},{3,27},{4,28},{5,29},{6,30},{7,31},{8,16},{9,... | collective-permute-start | bytes 1572872 | tf_op jit(solution)/shard_map/ppermute | solution.py:962
  367.0 15.1 %collective-permute-start.15 = (bf16[2,128,2048]{2,1,0:T(8,128)(2,1)}, bf16[2,128,2048]{2,1,0:T(8,128)(2,1)}, u32[]{:S(2)}, u32[]{:S(2)}) collective-permute-start(bf16[2,128,2048]{2,1,0:T(8,128)(2,1)} %add.73), channel_id=1, source_target_pairs={{0,1},{1,0},{2,3},{3,2},{4,6},{5,7},{6,4},{7,5},{8,9},{9,8},{10,11... | collective-permute-start | bytes 3145736 | tf_op jit(solution)/shard_map/ppermute | solution.py:962
  384.4 9.6 %collective-permute-start.23 = (bf16[1,128,2048]{2,1,0:T(8,128)(2,1)}, bf16[1,128,2048]{2,1,0:T(8,128)(2,1)}, u32[]{:S(2)}, u32[]{:S(2)}) collective-permute-start(bf16[1,128,2048]{2,1,0:T(8,128)(2,1)} %add.74), channel_id=1, source_target_pairs={{0,2},{1,3},{2,0},{3,1},{4,5},{5,4},{6,7},{7,6},{8,10},{9,11},{10,... | collective-permute-start | bytes 1572872 | tf_op jit(solution)/shard_map/ppermute | solution.py:962
  396.5 20.5 %collective-permute-start.24 = (bf16[1,64,2048]{2,1,0:T(8,128)(2,1)}, bf16[1,64,2048]{2,1,0:T(8,128)(2,1)S(1)}, u32[]{:S(2)}, u32[]{:S(2)}) collective-permute-start(bf16[1,64,2048]{2,1,0:T(8,128)(2,1)} %get-tuple-element.273.first), channel_id=1, source_target_pairs={{0,8},{1,9},{2,10},{3,11},{4,12},{5,13},{6,14},{7,15},{8,0},{9,1},... | collective-permute-start | bytes 786440 | tf_op jit(solution)/shard_map/ppermute | solution.py:962
  396.5 20.5 %collective-permute-start.25 = (bf16[1,64,2048]{2,1,0:T(8,128)(2,1)}, bf16[1,64,2048]{2,1,0:T(8,128)(2,1)S(1)}, u32[]{:S(2)}, u32[]{:S(2)}) collective-permute-start(bf16[1,64,2048]{2,1,0:T(8,128)(2,1)} %get-tuple-element.274.second), channel_id=1, source_target_pairs={{0,24},{1,25},{2,26},{3,27},{4,28},{5,29},{6,30},{7,31},{8,16},{9,... | collective-permute-start | bytes 786440 | tf_op jit(solution)/shard_map/ppermute | solution.py:962
  409.5 51.0 %collective-permute-start.29 = (bf16[1,512,1024]{2,1,0:T(8,128)(2,1)}, bf16[1,512,1024]{2,1,0:T(8,128)(2,1)}, u32[]{:S(2)}, u32[]{:S(2)}) collective-permute-start(bf16[1,512,1024]{2,1,0:T(8,128)(2,1)} %add.72.refs_0_), channel_id=1, source_target_pairs={{0,4},{1,5},{2,6},{3,7},{4,0},{5,1},{6,2},{7,3},{8,12},{9,13},{10,... | collective-permute-start | bytes 3145736 | tf_op jit(solution)/shard_map/ppermute | solution.py:962
  413.1 40.0 %collective-permute-start.20 = (f32[4,3072]{1,0:T(4,128)}, f32[4,3072]{1,0:T(4,128)}, u32[]{:S(2)}, u32[]{:S(2)}) collective-permute-start(f32[4,3072]{1,0:T(4,128)} %add.47), channel_id=1, source_target_pairs={{0,24},{1,25},{2,26},{3,27},{4,28},{5,29},{6,30},{7,31},{8,16},{9,... | collective-permute-start | bytes 147464 | tf_op jit(solution)/shard_map/ppermute | solution.py:962
  414.7 17.0 %collective-permute-start.30 = (bf16[1,256,1024]{2,1,0:T(8,128)(2,1)}, bf16[1,256,1024]{2,1,0:T(8,128)(2,1)}, u32[]{:S(2)}, u32[]{:S(2)}) collective-permute-start(bf16[1,256,1024]{2,1,0:T(8,128)(2,1)} %get-tuple-element.280.first), channel_id=1, source_target_pairs={{0,24},{1,25},{2,26},{3,27},{4,28},{5,29},{6,30},{7,31},{8,16},{9,... | collective-permute-start | bytes 1572872 | tf_op jit(solution)/shard_map/ppermute | solution.py:962
  416.9 28.1 %collective-permute-start.31 = (bf16[1,256,1024]{2,1,0:T(8,128)(2,1)}, bf16[1,256,1024]{2,1,0:T(8,128)(2,1)}, u32[]{:S(2)}, u32[]{:S(2)}) collective-permute-start(bf16[1,256,1024]{2,1,0:T(8,128)(2,1)} %get-tuple-element.281.second), channel_id=1, source_target_pairs={{0,8},{1,9},{2,10},{3,11},{4,12},{5,13},{6,14},{7,15},{8,0},{9,1},... | collective-permute-start | bytes 1572872 | tf_op jit(solution)/shard_map/ppermute | solution.py:962
  420.4 27.9 %collective-permute-start.26 = (bf16[1,64,2048]{2,1,0:T(8,128)(2,1)}, bf16[1,64,2048]{2,1,0:T(8,128)(2,1)}, u32[]{:S(2)}, u32[]{:S(2)}) collective-permute-start(bf16[1,64,2048]{2,1,0:T(8,128)(2,1)} %get-tuple-element.275.first), channel_id=1, source_target_pairs={{0,24},{1,25},{2,26},{3,27},{4,28},{5,29},{6,30},{7,31},{8,16},{9,... | collective-permute-start | bytes 786440 | tf_op jit(solution)/shard_map/ppermute | solution.py:962
  431.7 19.3 %collective-permute-start.27 = (bf16[1,64,2048]{2,1,0:T(8,128)(2,1)}, bf16[1,64,2048]{2,1,0:T(8,128)(2,1)}, u32[]{:S(2)}, u32[]{:S(2)}) collective-permute-start(bf16[1,64,2048]{2,1,0:T(8,128)(2,1)} %get-tuple-element.276.second), channel_id=1, source_target_pairs={{0,8},{1,9},{2,10},{3,11},{4,12},{5,13},{6,14},{7,15},{8,0},{9,1},... | collective-permute-start | bytes 786440 | tf_op jit(solution)/shard_map/ppermute | solution.py:962
  447.8 12.7 %collective-permute-start.32 = (bf16[1,512,1024]{2,1,0:T(8,128)(2,1)}, bf16[1,512,1024]{2,1,0:T(8,128)(2,1)}, u32[]{:S(2)}, u32[]{:S(2)}) collective-permute-start(bf16[1,512,1024]{2,1,0:T(8,128)(2,1)} %halves_add.7.refs_2_), channel_id=1, source_target_pairs={{0,4},{1,5},{2,6},{3,7},{4,0},{5,1},{6,2},{7,3},{8,12},{9,13},{10,... | collective-permute-start | bytes 3145736 | tf_op jit(solution)/shard_map/ppermute | solution.py:962
  (21 other events, 167.0 us)
Sparse Core Ops, SparseCore 0:
  12.0 39.7 all-gather.12
  54.2 55.8 all-gather.10
  112.6 61.2 all-gather.8
  175.7 45.9 all-gather.6

commit v3 on v2

--- a/solution.py
+++ b/solution.py
@@ -325,6 +325,38 @@
     return pl.ds(pl.multiple_of(start, 128), size)
 
 
+def spread_kernel(table, *refs):
+    *given, gain_a, shift_a, gain_m, shift_m, bias, first_pair, second_pair, first_unit, second_unit = refs
+    for j, ref in enumerate(given):
+        shard = table[6] ^ j
+        rows = ref[...].astype(F32)
+        row = lambda k: rows[k : k + 1, :]
+        for i, out in enumerate((gain_a, shift_a, gain_m, shift_m)):
+            for k in range(2):
+                out[:, columns_at(shard * 256 + k * 128, 128)] = row(2 * i + k)
+        for k in range(2):
+            bias[:, columns_at(shard * 256 + k * 128, 128)] = row(8 + k) + row(10 + k)
+        for k in range(6):
+            column = shard * 768 + k * 128
+            part, owner = column >> 10, (column & 1023) >> 8
+            target = (owner >> 1) * 768 + part * 256 + (owner & 1) * 128
+            (first_pair, second_pair)[k % 2][:, columns_at(target, 128)] = row(12 + k)
+        for k in range(8):
+            (first_unit, second_unit)[k // 4][:, columns_at(shard * 512 + k % 4 * 128, 128)] = row(18 + k)
+
+
+def spread(table, given):
+    inside = pl.BlockSpec(memory_space=pltpu.VMEM)
+    widths = [D] * 5 + [1536] * 2 + [2048] * 2
+    return pl.pallas_call(
+        spread_kernel,
+        in_specs=[pl.BlockSpec(memory_space=pltpu.SMEM)] + [inside] * len(given),
+        out_specs=[inside] * len(widths),
+        out_shape=[jax.ShapeDtypeStruct((1, width), F32) for width in widths],
+        name="spread",
+    )(table, *given)
+
+
 def norm_kernel(table, x, grad, gain_a, shift_a, gain_m, shift_m, na, nm, gr):
     values = x[...].astype(F32)
     mean = jnp.mean(values, axis=1, keepdims=True)
@@ -351,27 +383,9 @@
         out_specs=[tile] * 3,
         out_shape=[jax.ShapeDtypeStruct((T, D), BF)] * 3,
         compiler_params=pltpu.CompilerParams(vmem_limit_bytes=VMEM),
-        cost_estimate=pl.CostEstimate(flops=10 * T * D, bytes_accessed=10 * T * D, transcendentals=T),
+        cost_estimate=LONG,
         name="norm",
     )(table, x, grad, *vectors)
-
-
-def output_kernel(x, out, bias, layer_output):
-    layer_output[...] = x[...].astype(F32) + out[...] + bias[...]
-
-
-def output(x, out, bias):
-    tile = pl.BlockSpec((ROWS, D), lambda i: (i, 0))
-    row = pl.BlockSpec((1, D), lambda i: (0, 0))
-    return pl.pallas_call(
-        output_kernel,
-        grid=(T // ROWS,),
-        in_specs=[tile, tile, row],
-        out_specs=tile,
-        out_shape=jax.ShapeDtypeStruct((T, D), F32),
-        cost_estimate=LONG,
-        name="output",
-    )(x, out, bias)
 
 
 def finish_kernel(table, x, gr, dna, dnm, gain_a, gain_m, *refs):
@@ -405,13 +419,14 @@
         for i in range(5):
             for a in range(4):
                 small[a : a + 1, rows_of(i, 256)] = sums[i : i + 1, rows_of(a, 256)]
-        *pairs, first_unit, second_unit = bias_sums
+        pair_sums, unit_sums = bias_sums[:3], bias_sums[3:]
         for pair in range(2):
             for a, b in qkv_blocks(pair):
-                small[a // 768 : a // 768 + 1, pl.ds(1280 + a % 768, 128)] = pairs[pair][:, pl.ds(b, 128)]
-        for unit_index, value in enumerate((first_unit, second_unit)):
-            for a in range(4):
-                small[a : a + 1, pl.ds(2048 + unit_index * 512, 512)] = value[:, rows_of(a, 512)]
+                value = pair_sums[0] if pair == 0 else pair_sums[1 + b // 768]
+                small[a // 768 : a // 768 + 1, pl.ds(1280 + a % 768, 128)] = value[:, pl.ds(b if pair == 0 else b % 768, 128)]
+        for a in range(4):
+            small[a : a + 1, pl.ds(2048, 512)] = unit_sums[0][:, rows_of(a, 512)]
+            small[a : a + 1, pl.ds(2560, 512)] = unit_sums[1 + a // 2][:, rows_of(a % 2, 512)]
 
 
 def finish(table, x, gr, dna, dnm, vectors, bias_sums):
@@ -602,8 +617,10 @@
     )(table, nm, gr, bi, pieces, *inputs)
 
 
-def attn_unit_kernel(first, count, given, table, na, gr, bias, cosine, ahead, behind, pieces, *refs):
+def attn_unit_kernel(first, count, given, apart, last, table, na, gr, bias, cosine, ahead, behind, *refs):
     refs = list(refs)
+    pieces = [refs.pop(0) for _ in range(8 if apart else 1)]
+    rest = [refs.pop(0) for _ in range(2 if last else 0)]
     olds = [refs.pop(0) if is_given else None for is_given in given]
     (
         keep, send, gb, out_ref, dn_ref,
@@ -618,12 +635,17 @@
         made = []
         for t in range(4):
             for half in range(2):
-                piece = (core ^ half) * 4 + table[6 + t]
-                source = pieces.at[piece, :, columns_at(group * 768, 768)]
-                made.append((source, w.at[index, pl.ds(t * 256 + half * 128, 128), :]))
-        for pair in range(2):
+                if apart:
+                    piece = pieces[half * 4 + t].at[0]
+                    place = wd.at[table[6 + t] // 2, pl.ds(pl.multiple_of(table[6 + t] % 2 * 128, 128), 128), columns_at((core ^ half) * 512, 512)]
+                    if isinstance(index, int) and index == 0:
+                        made.append((piece.at[:, pl.ds(1536, 512)], place))
+                else:
+                    piece = pieces[0].at[(core ^ half) * 4 + table[6 + t]]
+                made.append((piece.at[:, columns_at(group * 768, 768)], w.at[index, pl.ds(t * 256 + half * 128, 128), :]))
+        for pair in range(0 if apart else 2):
             for h in range(2):
-                source = pieces.at[h * 4 + group * 2 + pair, :, pl.ds(1536, 512)]
+                source = pieces[0].at[h * 4 + group * 2 + pair, :, pl.ds(1536, 512)]
                 made.append((source, wd.at[index, pl.ds(pair * 128, 128), pl.ds(h * 512, 512)]))
         return [pltpu.make_async_copy(a, b, sems.at[index, i]) for i, (a, b) in enumerate(made)]
 
@@ -643,7 +665,11 @@
             start_all(copies(index))
         totals.begin()
 
-    wait_all(copies(step))
+    for index in range(count):
+
+        @pl.when(step == index)
+        def _():
+            wait_all(copies(index))
 
     def turn(x, r, back):
         parts = []
@@ -716,7 +742,10 @@
         r = rows_of(t, ROWS)
         context = together(ctx, r)
         grads[r, part[3]] = context
-        out[r, :] += nn(context, wd[step])
+        total = nn(context, wd[step])
+        if last:
+            total += rest[0][r, :].astype(F32) + rest[1][...]
+        out[r, :] += total
         projected_grad = jnp.concatenate(
             [
                 turn(together(dq, r) * 0.125, r, True).astype(BF),
@@ -756,22 +785,26 @@
         wait_all(totals.stores())
 
 
-def attn_unit(first, count, table, na, gr, bias, tables, pieces, parts, totals):
+def attn_unit(first, count, table, na, gr, bias, tables, pieces, parts, totals, rest=()):
     olds = list(parts) + list(totals)
     given = tuple(old is not None for old in olds)
     inputs = [old for old in olds if old is not None]
-    aliases = {8 + n: (0, 1, 3, 4)[i] for n, i in enumerate(i for i in range(4) if given[i])}
+    apart = isinstance(pieces, list)
+    pieces = pieces if apart else [pieces]
+    aliases = {7 + len(pieces) + len(rest) + n: (0, 1, 3, 4)[i] for n, i in enumerate(i for i in range(4) if given[i])}
     one = pl.Buffered(1)
     whole = pl.BlockSpec((T, D), lambda i: (0, 0), pipeline_mode=one)
     turns = pl.BlockSpec((T, 128), lambda i: (0, 0), pipeline_mode=one)
     anywhere = pl.BlockSpec(memory_space=pl.ANY)
     head_rows = lambda dtype: pltpu.VMEM((HEADS, T, HD), dtype)
     return pl.pallas_call(
-        functools.partial(attn_unit_kernel, first, count, given),
+        functools.partial(attn_unit_kernel, first, count, given, apart, len(rest) > 0),
         grid=(count,),
         in_specs=[pl.BlockSpec(memory_space=pltpu.SMEM), whole, whole, pl.BlockSpec((1, 3 * GROUP), lambda i: (0, first + i))]
         + [turns] * 3
-        + [anywhere] * (1 + len(inputs)),
+        + [anywhere] * len(pieces)
+        + [pl.BlockSpec(value.shape, lambda i: (0, 0), pipeline_mode=one) for value in rest]
+        + [anywhere] * len(inputs),
         out_specs=[anywhere, anywhere, pl.BlockSpec((1, 3 * GROUP), lambda i: (0, i)), anywhere, anywhere],
         out_shape=[jax.ShapeDtypeStruct((4, 128, 2 * D), BF)] * 2
         + [jax.ShapeDtypeStruct((1, 3 * GROUP * count), F32)]
@@ -786,14 +819,14 @@
             pltpu.VMEM((T, D), F32),
             pltpu.VMEM((count, 2, 4, 128, 3 * GROUP), BF),
             pltpu.VMEM((count, 2, 2, 128, WIDE), BF),
-            pltpu.SemaphoreType.DMA((count, 12)),
+            pltpu.SemaphoreType.DMA((count, 16)),
             pltpu.SemaphoreType.DMA((count, 6)),
             pltpu.SemaphoreType.DMA((2,)),
         ],
         compiler_params=pltpu.CompilerParams(vmem_limit_bytes=VMEM_UNIT),
         cost_estimate=LONG,
         name="attn_unit",
-    )(table, na, gr, bias, *tables, pieces, *inputs)
+    )(table, na, gr, bias, *tables, *pieces, *rest, *inputs)
 
 
 def qkv_blocks(pair):
@@ -805,12 +838,15 @@
     ]
 
 
-def attn_pack_kernel(pair, table, qkv, dense, piece, sems):
-    core = table[0]
-    rows = pl.ds(pl.multiple_of(core * 128, 128), 128)
-    made = [(qkv.at[rows, pl.ds(a, 128)], piece.at[0, :, pl.ds(b, 128)]) for a, b in qkv_blocks(pair)]
-    made.append((dense.at[pl.ds(pair * 128, 128), columns_at(core * 512, 512)], piece.at[0, :, pl.ds(1536, 512)]))
-    copies = [pltpu.make_async_copy(a, b, sems.at[i]) for i, (a, b) in enumerate(made)]
+def attn_pack_kernel(pair, table, qkv, dense, *refs):
+    *pieces, sems = refs
+    copies = []
+    for side, piece in enumerate(pieces):
+        half = table[0] ^ side
+        rows = pl.ds(pl.multiple_of(half * 128, 128), 128)
+        made = [(qkv.at[rows, pl.ds(a, 128)], piece.at[0, :, pl.ds(b, 128)]) for a, b in qkv_blocks(pair)]
+        made.append((dense.at[pl.ds(pair * 128, 128), columns_at(half * 512, 512)], piece.at[0, :, pl.ds(1536, 512)]))
+        copies += [pltpu.make_async_copy(a, b, sems.at[side * 13 + i]) for i, (a, b) in enumerate(made)]
     start_all(copies)
     wait_all(copies)
 
@@ -827,45 +863,49 @@
     wait_all(copies)
 
 
-def pack(kernel, shape, count, name, table, *weights):
+def pack(kernel, shape, count, sides, name, table, *weights):
     anywhere = pl.BlockSpec(memory_space=pl.ANY)
     return pl.pallas_call(
         kernel,
         in_specs=[pl.BlockSpec(memory_space=pltpu.SMEM)] + [anywhere] * len(weights),
-        out_specs=pl.BlockSpec(memory_space=pltpu.VMEM),
-        out_shape=jax.ShapeDtypeStruct(shape, BF),
-        scratch_shapes=[pltpu.SemaphoreType.DMA((count,))],
+        out_specs=[pl.BlockSpec(memory_space=pltpu.VMEM)] * sides,
+        out_shape=[jax.ShapeDtypeStruct(shape, BF)] * sides,
+        scratch_shapes=[pltpu.SemaphoreType.DMA((count * sides,))],
+        cost_estimate=LONG,
         name=name,
     )(table, *weights)
 
 
 def attn_place_kernel(table, *refs):
     *values, grad_qkv, grad_d = refs
-    core = table[0]
-    for pair in range(2):
-        for side in range(2):
-            value = values[pair * 2 + side]
-            half = core ^ side
-            rows = pl.ds(pl.multiple_of(half * 128, 128), 128)
-            for a, b in qkv_blocks(pair):
-                grad_qkv[rows, pl.ds(a, 128)] = value[0, :, pl.ds(b, 128)].astype(F32)
-            grad_d[rows_of(pair, 128), columns_at(half * 512, 512)] = value[0, :, pl.ds(1536, 512)].astype(F32)
+    for i, value in enumerate(values):
+        pair, half, part = i // 4, table[0] ^ (i // 2 % 2), table[10] ^ (i % 2)
+        rows = pl.ds(pl.multiple_of(half * 128 + part * 64, 64), 64)
+        for a, b in qkv_blocks(pair):
+            grad_qkv[rows, pl.ds(a, 128)] = value[0, :, pl.ds(b, 128)].astype(F32)
+        rows = pl.ds(pl.multiple_of(pair * 128 + part * 64, 64), 64)
+        grad_d[rows, columns_at(half * 512, 512)] = value[0, :, pl.ds(1536, 512)].astype(F32)
 
 
 def mlp_place_kernel(table, *refs):
     *values, grad_wi, grad_wo = refs
-    core = table[0]
-    for unit in range(2):
-        for side in range(2):
-            value = values[unit * 2 + side]
-            half = core ^ side
+    for i, value in enumerate(values):
+        unit, half = i // 4, table[0] ^ (i // 2 % 2)
+
+        @pl.when(table[10] == i % 2)
+        def _():
             rows = pl.ds(pl.multiple_of(half * 128, 128), 128)
             for tile in range(4):
-                grad_wi[rows, pl.ds(tile * 1024 + unit * 512, 512)] = value[0, rows_of(tile // 2, 128), rows_of(tile % 2, 512)].astype(F32)
+                columns = pl.ds(tile * 1024 + unit * 512, 512)
+                grad_wi[rows, columns] = value[0, rows_of(tile // 2, 128), rows_of(tile % 2, 512)].astype(F32)
+
+        @pl.when(table[10] != i % 2)
+        def _():
             for f in range(2):
                 for part in range(2):
-                    target = pl.ds(unit * 512 + f * 256 + part * 128, 128)
-                    grad_wo[target, columns_at(half * 512, 512)] = value[0, rows_of(2 + f, 128), rows_of(part, 512)].astype(F32)
+                    rows = pl.ds(unit * 512 + f * 256 + part * 128, 128)
+                    columns = columns_at(half * 512, 512)
+                    grad_wo[rows, columns] = value[0, rows_of(f, 128), rows_of(part, 512)].astype(F32)
 
 
 def place(kernel, shapes, name, table, *values):
@@ -885,7 +925,7 @@
     target[...] = sum(source[...].astype(F32) for source in sources).astype(BF)
 
 
-def add(*sources, count=1):
+def add(*sources, count=1, cost=LONG):
     rows, columns = sources[0][0].shape[1:]
     steps = 2
     read = lambda first, stride: pl.BlockSpec(
@@ -897,56 +937,35 @@
         in_specs=[read(first, stride) for _, first, stride in sources],
         out_specs=read(0, 1),
         out_shape=jax.ShapeDtypeStruct((count, rows, columns), BF),
-        cost_estimate=LONG,
+        cost_estimate=cost,
         name="add",
     )(*(array for array, _, _ in sources))
 
 
-def split_add_kernel(*refs):
-    *sources, first, second = refs
+def split_add_kernel(table, *refs):
+    *sources, kept, sent = refs
     total = sum(source[...].astype(F32) for source in sources).astype(BF)
     half = total.shape[1] // 2
-    first[...] = total[:, :half]
-    second[...] = total[:, half:]
-
-
-def split_add(*arrays):
+    for parity in range(2):
+
+        @pl.when(table[10] == parity)
+        def _():
+            kept[...] = total[:, rows_of(parity, half)]
+            sent[...] = total[:, rows_of(1 - parity, half)]
+
+
+def split_add(table, *arrays, cost=LONG):
     rows, columns = arrays[0].shape[1:]
     return pl.pallas_call(
         split_add_kernel,
         grid=(1,),
-        in_specs=[pl.BlockSpec((1, rows, columns), lambda i: (0, 0, 0))] * len(arrays),
+        in_specs=[pl.BlockSpec(memory_space=pltpu.SMEM)]
+        + [pl.BlockSpec((1, rows, columns), lambda i: (0, 0, 0))] * len(arrays),
         out_specs=[pl.BlockSpec((1, rows // 2, columns), lambda i: (0, 0, 0))] * 2,
         out_shape=[jax.ShapeDtypeStruct((1, rows // 2, columns), BF)] * 2,
-        cost_estimate=LONG,
+        cost_estimate=cost,
         name="split_add",
-    )(*arrays)
-
-
-def pair_add_kernel(first, got_first, second, got_second, first_out, second_out):
-    first_out[...] = (first[...].astype(F32) + got_first[...].astype(F32)).astype(BF)
-    second_out[...] = (second[...].astype(F32) + got_second[...].astype(F32)).astype(BF)
-
-
-def join_add_kernel(first, got_first, second, got_second, total):
-    half = first.shape[1]
-    total[:, :half] = (first[...].astype(F32) + got_first[...].astype(F32)).astype(BF)
-    total[:, half:] = (second[...].astype(F32) + got_second[...].astype(F32)).astype(BF)
-
-
-def halves_add(first, got_first, second, got_second, join=False):
-    block = lambda shape: pl.BlockSpec(shape, lambda i: (0, 0, 0))
-    one, rows, columns = first.shape
-    shapes = [(one, rows * 2, columns)] if join else [first.shape] * 2
-    return pl.pallas_call(
-        join_add_kernel if join else pair_add_kernel,
-        grid=(1,),
-        in_specs=[block(first.shape)] * 4,
-        out_specs=[block(shape) for shape in shapes],
-        out_shape=[jax.ShapeDtypeStruct(shape, BF) for shape in shapes],
-        cost_estimate=LONG,
-        name="halves_add",
-    )(first, got_first, second, got_second)
+    )(table, *arrays)
 
 
 AXES = ("z", "core", "y", "x")
@@ -967,8 +986,9 @@
 to_second = lambda z, core, shard: (z, core, shard ^ (2 - core))
 to_x = lambda z, core, shard: (z, core, shard ^ 1)
 to_y = lambda z, core, shard: (z, core, shard ^ 2)
+to_xy = lambda z, core, shard: (z, core, shard ^ 3)
 to_below = lambda z, core, shard: (z ^ 1, core, shard)
-to_above = lambda z, core, shard: (3 - z, core, shard)
+to_two = lambda z, core, shard: (z ^ 2, core, shard)
 
 
 def wide(value):
@@ -985,42 +1005,53 @@
     shard_of = own ^ steps
     difference = own ^ jnp.arange(4, dtype=jnp.int32)
     block_of = jnp.where(core == 1, difference, ((difference & 1) << 1) | (difference >> 1))
-    table = jnp.concatenate([core[None].astype(jnp.int32), seq_lengths, block_of, shard_of]).astype(jnp.int32)
+    parity = lax.axis_index("z") % 2
+    table = jnp.concatenate([core[None], seq_lengths, block_of, shard_of, parity[None]]).astype(jnp.int32)
 
     gather = lambda piece: lax.all_gather(piece, ("core", "y", "x"), axis=0, tiled=True)
-    pack_attn = lambda pair: pack(
-        functools.partial(attn_pack_kernel, pair), (1, 128, 2 * D), 13, "attn_pack", table, qkv_weight, dense_weight
+    pack_attn = lambda pair, sides: pack(
+        functools.partial(attn_pack_kernel, pair), (1, 128, 2 * D), 13, sides, "attn_pack", table, qkv_weight, dense_weight
     )
     pack_mlp = lambda unit: pack(
-        functools.partial(mlp_pack_kernel, unit), (1, 2, 128, 2 * D), 6, "mlp_pack", table, inner_weight, outer_weight
-    )
-    pieces = [gather(pack_attn(0)), gather(pack_mlp(0)), gather(pack_mlp(1)), gather(pack_attn(1))]
-
-    vectors = jnp.concatenate(
-        [attn_gain, attn_shift, mlp_gain, mlp_shift, dense_bias, outer_bias, qkv_bias, inner_bias]
-    )
-    vectors = lax.all_gather(vectors, ("y", "x"), axis=0, tiled=False).astype(F32)
-    cuts = np.cumsum([256] * 6 + [768, 1024])[:-1]
-    gain_a, shift_a, gain_m, shift_m, bias_d, bias_o, bias_qkv, bias_i = (
-        part.reshape(1, -1) for part in jnp.split(vectors, cuts, axis=1)
-    )
-    bias_pairs = jnp.transpose(bias_qkv.reshape(3, 2, 2, 2, 128), (3, 1, 0, 2, 4)).reshape(2, 1, 1536)
-    bias_units = jnp.swapaxes(bias_i.reshape(4, 2, 512), 0, 1).reshape(2, 1, 2048)
-
-    na, nm, gr = norm(table, layer_input, out_grad, (gain_a, shift_a, gain_m, shift_m))
-    tables = [jnp.asarray(t) for t in rotary_tables()]
+        functools.partial(mlp_pack_kernel, unit), (1, 2, 128, 2 * D), 6, 1, "mlp_pack", table, inner_weight, outer_weight
+    )[0]
 
     def after(done, *values):
         return lax.optimization_barrier((done,) + values)
 
-    far_blocks = lambda keep, got: add((keep, 2, 1), (got, 1, 2), count=2)
-    near_block = lambda keep, got, far: add((keep, 1, 1), (got, 2, 1), (far, 1, 1))
+    part, rest = pack_attn(0, 2)
+    vectors = (attn_gain, attn_shift, mlp_gain, mlp_shift, dense_bias, outer_bias, qkv_bias, inner_bias)
+    part, table = after(part, table)
+    from_first = exchange(part, to_first)
+    from_second = exchange(part, to_second)
+    packed = [pack_mlp(0), pack_mlp(1)]
+    vectors = [vector.reshape(-1, 128) for vector in vectors]
+    ends = np.cumsum([vector.shape[0] for vector in vectors])
+    vectors = sum(jnp.pad(v, ((end - v.shape[0], 26 - end), (0, 0))) for v, end in zip(vectors, ends))
+    vectors = [vectors] + [exchange(vectors, to) for to in (to_x, to_y, to_xy)]
+    from_first, from_second, table, *packed = after(from_first, from_second, table, *packed)
+    from_both = exchange(from_first, to_second)
+    core_first = exchange(from_first, to_core)
+    core_second = exchange(from_second, to_core)
+    gain_a, shift_a, gain_m, shift_m, bias_out, *biases = spread(table, vectors)
+    bias_pairs, bias_units = biases[:2], biases[2:]
+    na, nm, gr = norm(table, layer_input, out_grad, (gain_a, shift_a, gain_m, shift_m))
+    packed_b = pack_attn(1, 1)[0]
+    from_both, na, packed_b, *packed = after(from_both, na, packed_b, *packed)
+    pieces = [None] + [gather(piece) for piece in packed]
+    na, from_both = after(na, from_both)
+    core_both = exchange(from_both, to_core)
+    pieces[0] = [part, from_second, from_first, from_both, rest, core_first, core_second, core_both]
+    tables = [jnp.asarray(t) for t in rotary_tables()]
+
+    far_blocks = lambda keep, got, cost=LONG: add((keep, 2, 1), (got, 1, 2), count=2, cost=cost)
+    near_block = lambda keep, got, far, cost=LONG: add((keep, 1, 1), (got, 2, 1), (far, 1, 1), cost=cost)
     own_block = lambda *arrays: add(*((array, 0, 1) for array in arrays))
-    plus = lambda total, got: add((total, 0, 1), (got, 0, 1))
+    plus = lambda total, got: add((total, 0, 1), (got, 0, 1), cost=None)
 
     none = (None, None)
-    attn_call = lambda first, count, pair, parts, totals: attn_unit(
-        first, count, table, na, gr, bias_pairs[pair], tables, pieces[3 * pair], parts, totals
+    attn_call = lambda first, count, pair, parts, totals, rest=(): attn_unit(
+        first, count, table, na, gr, bias_pairs[pair], tables, pieces[3 * pair], parts, totals, rest
     )
     mlp_call = lambda first, count, unit, parts, totals: mlp_unit(
         first, count, table, nm, gr, bias_units[unit], pieces[1 + unit], parts, totals
@@ -1028,14 +1059,12 @@
 
     keep_a, send_a, gb0, out, dna = attn_call(0, 2, 0, none, none)
     got_a = exchange(send_a, to_core)
-
-    keep_m, send_m, gbi0a, out, dnm = mlp_call(0, 2, 0, none, (out, None))
     out, keep_a, got_a = after(out, keep_a, got_a)
     far_a = far_blocks(keep_a, got_a)
     out, far_a = after(out, far_a)
     far_a = exchange(far_a, to_first)
 
-    keep_m, send_m, gbi0b, out, dnm = mlp_call(2, 2, 0, (keep_m, send_m), (out, dnm))
+    keep_m, send_m, gbi0, out, dnm = mlp_call(0, 4, 0, none, (out, None))
     got_m = exchange(send_m, to_core)
     out, keep_a, got_a, far_a = after(out, keep_a, got_a, far_a)
     near_a = near_block(keep_a, got_a, far_a)
@@ -1049,91 +1078,96 @@
     out, keep_a, got_a, far_a, near_a, keep_m, got_m, far_m = after(
         out, keep_a, got_a, far_a, near_a, keep_m, got_m, far_m
     )
-    total_a = own_block(keep_a, got_a, far_a, near_a)
+    kept_a, sent_a = split_add(table, keep_a, got_a, far_a, near_a)
     near_m = near_block(keep_m, got_m, far_m)
-    out, total_a, near_m = after(out, total_a, near_m)
-    got_total_a = exchange(total_a, to_below)
+    out, kept_a, sent_a, near_m, packed_b = after(out, kept_a, sent_a, near_m, packed_b)
+    pieces.append(gather(packed_b))
+    sent_a = exchange(sent_a, to_below)
     near_m = exchange(near_m, to_second)
 
     keep_n, send_n, gbi1b, out, dnm = mlp_call(2, 2, 1, (keep_n, send_n), (out, dnm))
     got_n = exchange(send_n, to_core)
-    out, total_a, got_total_a, keep_m, got_m, far_m, near_m = after(
-        out, total_a, got_total_a, keep_m, got_m, far_m, near_m
-    )
-    total_a = plus(total_a, got_total_a)
-    total_m = own_block(keep_m, got_m, far_m, near_m)
-    total_m, total_a, keep_n, got_n = after(total_m, total_a, keep_n, got_n)
+    out, kept_a, sent_a, keep_m, got_m, far_m, near_m = after(
+        out, kept_a, sent_a, keep_m, got_m, far_m, near_m
+    )
+    kept_m, sent_m = split_add(table, keep_m, got_m, far_m, near_m)
+    kept_a = plus(kept_a, sent_a)
+    kept_m, sent_m, kept_a, keep_n, got_n = after(kept_m, sent_m, kept_a, keep_n, got_n)
     far_n = far_blocks(keep_n, got_n)
-    out, total_a, total_m, far_n = after(out, total_a, total_m, far_n)
-    got_total_a = exchange(total_a, to_above)
-    got_total_m = exchange(total_m, to_below)
+    out, kept_m, sent_m, kept_a, far_n = after(out, kept_m, sent_m, kept_a, far_n)
+    got_kept_a = exchange(kept_a, to_two)
+    sent_m = exchange(sent_m, to_below)
     far_n = exchange(far_n, to_first)
 
     keep_b, send_b, gb1a, out, dna = attn_call(0, 1, 1, none, (out, dna))
-    out, total_a, got_total_a, total_m, got_total_m, keep_n, got_n, far_n = after(
-        out, total_a, got_total_a, total_m, got_total_m, keep_n, got_n, far_n
-    )
-    total_a = plus(total_a, got_total_a)
-    total_m = plus(total_m, got_total_m)
+    out, kept_a, got_kept_a, kept_m, sent_m, keep_n, got_n, far_n = after(
+        out, kept_a, got_kept_a, kept_m, sent_m, keep_n, got_n, far_n
+    )
+    kept_a = plus(kept_a, got_kept_a)
+    kept_m = plus(kept_m, sent_m)
     near_n = near_block(keep_n, got_n, far_n)
-    out, total_a, total_m, near_n = after(out, total_a, total_m, near_n)
-    other_a = exchange(total_a, to_core)
-    got_total_m = exchange(total_m, to_above)
+    out, kept_a, kept_m, near_n = after(out, kept_a, kept_m, near_n)
+    got_kept_m = exchange(kept_m, to_two)
     near_n = exchange(near_n, to_second)
-
-    keep_b, send_b, gb1b, out, dna = attn_call(1, 1, 1, (keep_b, send_b), (out, dna))
+    pieces_a = [kept_a, exchange(kept_a, to_below), exchange(kept_a, to_core)]
+
+    rest = (layer_input, bias_out)
+    keep_b, send_b, gb1b, layer_output, dna = attn_call(1, 1, 1, (keep_b, send_b), (out, dna), rest)
     got_b = exchange(send_b, to_core)
-    out, total_m, got_total_m, keep_n, got_n, far_n, near_n, other_a = after(
-        out, total_m, got_total_m, keep_n, got_n, far_n, near_n, other_a
-    )
-    first_n, second_n = split_add(keep_n, got_n, far_n, near_n)
-    total_m = plus(total_m, got_total_m)
-    out, total_m, first_n, second_n = after(out, total_m, first_n, second_n)
-    got_first_n = exchange(first_n, to_below)
-    got_second_n = exchange(second_n, to_above)
-    other_m = exchange(total_m, to_core)
-    layer_output = output(layer_input, out, bias_d + bias_o)
-    layer_output, keep_b, got_b = after(layer_output, keep_b, got_b)
-    far_b = far_blocks(keep_b, got_b)
-
-    bias_sums = [
-        gb0,
-        jnp.concatenate([gb1a, gb1b], axis=1),
-        jnp.concatenate([gbi0a, gbi0b], axis=1),
-        jnp.concatenate([gbi1a, gbi1b], axis=1),
-    ]
-    far_b, dna, dnm = after(far_b, dna, dnm)
+    layer_output, keep_n, got_n, far_n, near_n, kept_m, got_kept_m, *pieces_a = after(
+        layer_output, keep_n, got_n, far_n, near_n, kept_m, got_kept_m, *pieces_a
+    )
+    kept_n, sent_n = split_add(table, keep_n, got_n, far_n, near_n)
+    kept_n, sent_n, keep_b, got_b = after(kept_n, sent_n, keep_b, got_b)
+    far_b = far_blocks(keep_b, got_b, None)
+    far_b, kept_n, sent_n, kept_m, got_kept_m, dna, dnm = after(far_b, kept_n, sent_n, kept_m, got_kept_m, dna, dnm)
     far_b = exchange(far_b, to_first)
+    sent_n = exchange(sent_n, to_below)
+    pieces_a.append(exchange(pieces_a[1], to_core))
+
+    bias_sums = [gb0, gb1a, gb1b, gbi0, gbi1a, gbi1b]
     input_grad, small = finish(table, layer_input, gr, dna, dnm, (gain_a, gain_m), bias_sums)
     small, far_b, keep_b, got_b = after(small, far_b, keep_b, got_b)
-    near_b = near_block(keep_b, got_b, far_b)
-    near_b, got_first_n, got_second_n, first_n, second_n = after(near_b, got_first_n, got_second_n, first_n, second_n)
+    near_b = near_block(keep_b, got_b, far_b, None)
+    near_b, small, kept_n, sent_n = after(near_b, small, kept_n, sent_n)
     near_b = exchange(near_b, to_second)
-    first_n, second_n = halves_add(first_n, got_first_n, second_n, got_second_n)
-    first_n, second_n, near_b = after(first_n, second_n, near_b)
-    got_first_n = exchange(first_n, to_above)
-    got_second_n = exchange(second_n, to_below)
-    first_b, second_b = split_add(keep_b, got_b, far_b, near_b)
-    got_first_b = exchange(first_b, to_below)
-    got_second_b = exchange(second_b, to_above)
-    (total_n,) = halves_add(first_n, got_first_n, second_n, got_second_n, join=True)
-    other_n = exchange(total_n, to_core)
-    first_b, second_b = halves_add(first_b, got_first_b, second_b, got_second_b)
-    got_first_b = exchange(first_b, to_above)
-    got_second_b = exchange(second_b, to_below)
-    (total_b,) = halves_add(first_b, got_first_b, second_b, got_second_b, join=True)
-    other_b = exchange(total_b, to_core)
-
-    grad_wi, grad_wo = place(
-        mlp_place_kernel, ((256, FF), (1024, D)), "mlp_place", table, total_m, other_m, total_n, other_n
-    )
+    got_small = exchange(small, to_core)
+    kept_n = plus(kept_n, sent_n)
+    kept_m = plus(kept_m, got_kept_m)
+    kept_n, kept_m, near_b, small, got_small = after(kept_n, kept_m, near_b, small, got_small)
+    kept_b, sent_b = split_add(table, keep_b, got_b, far_b, near_b, cost=None)
+    small = small + got_small
+    kept_b, sent_b, small, kept_m = after(kept_b, sent_b, small, kept_m)
+    sent_b = exchange(sent_b, to_below)
+    got_kept_n = exchange(kept_n, to_two)
+    got_small = exchange(small, to_x)
+    pieces_m = [kept_m, exchange(kept_m, to_below), exchange(kept_m, to_core)]
+    small, got_small, kept_b, sent_b = after(small, got_small, kept_b, sent_b)
+    kept_b = plus(kept_b, sent_b)
+    small = small + got_small
+    kept_b, small, kept_n, got_kept_n = after(kept_b, small, kept_n, got_kept_n)
+    got_kept_b = exchange(kept_b, to_two)
+    got_small = exchange(small, to_y)
+    kept_n = plus(kept_n, got_kept_n)
+    pieces_n = [kept_n, exchange(kept_n, to_below), exchange(kept_n, to_core)]
+    small, got_small, kept_b, got_kept_b, *pieces_n = after(small, got_small, kept_b, got_kept_b, *pieces_n)
+    kept_b = plus(kept_b, got_kept_b)
+    small = small + got_small
+    kept_b, small = after(kept_b, small)
+    pieces_b = [kept_b, exchange(kept_b, to_below), exchange(kept_b, to_core)]
+    pieces_n.append(exchange(pieces_n[1], to_core))
+    pieces_m.append(exchange(pieces_m[1], to_core))
+    got_small = exchange(small, to_below)
+    grad_wi, grad_wo = place(mlp_place_kernel, ((256, FF), (1024, D)), "mlp_place", table, *pieces_m, *pieces_n)
+    grad_wi, small, got_small, *pieces_b = after(grad_wi, small, got_small, *pieces_b)
+    pieces_b.append(exchange(pieces_b[1], to_core))
+    small = small + got_small
+    got_small = exchange(small, to_two)
     grad_qkv, grad_d = place(
-        attn_place_kernel, ((256, 3 * D), (256, D)), "attn_place", table, total_a, other_a, total_b, other_b
-    )
-
-    for partner in (to_core, to_x, to_y, to_below, to_above):
-        small = small + exchange(small, partner)
-    small = lax.dynamic_index_in_dim(small, own, 0, keepdims=False)
+        attn_place_kernel, ((256, 3 * D), (256, D)), "attn_place", table, *pieces_a, *pieces_b
+    )
+    grad_d, small, got_small = after(grad_d, small, got_small)
+    small = lax.dynamic_index_in_dim(small + got_small, own, 0, keepdims=False)
     g_ga, g_sa, g_gm, g_sm, g_bd, g_bqkv, g_bi = jnp.split(small, np.cumsum([256] * 5 + [768]))
     return (
         layer_output, input_grad, g_ga, g_sa, g_gm, g_sm, grad_qkv, g_bqkv, grad_d, g_bd, grad_wi, g_bi, grad_wo, g_bd,

time: 479 us -> 430 us (0.90)
  waiting for transfers between devices: 80.7 us -> 63 us
  Pallas kernels: 303 us -> 293 us
  blocking collectives: 9.86 us -> 0 us
    all_gather x4 -> x3, waiting for transfers between devices: 12.5 us -> 0.51 us  [shards(): lax.all_gather(piece, ('core', 'y', 'x'), axis=0, tiled=True)]
    all_gather x1 -> x0, blocking collectives: 9.86 us -> none  [shards(): lax.all_gather(vectors, ('y', 'x'), axis=0, tiled=False).astype(F32)]
    pallas_call x4 -> x3, Pallas kernels: 89 us -> 81.2 us  [mlp_unit(): pl.pallas_call(functools.partial(mlp_unit_kernel, first, count, given), g...]
    ppermute x33 -> x46, waiting for transfers between devices: 68.1 us -> 62.4 us  [exchange(): return lax.ppermute(value, AXES, pairs)]
    pallas_call x10 -> x8, Pallas kernels: 137 us -> 132 us  [the longest x3 117 us: attn_unit(): pl.pallas_call(functools.partial(attn_unit_kernel, first, count, given, a...]
    ppermute x33 -> x46, starting transfers between devices: 46.9 us -> 43.8 us  [exchange(): return lax.ppermute(value, AXES, pairs)]
    pallas_call x14 -> x16, Pallas kernels: 40.6 us -> 41.8 us  [add(): pl.pallas_call(add_kernel, grid=(count * steps,), in_specs=[read(first, s...]
  transfers between devices with their start and end apart: 37 -> 49, of which waited for: 15 -> 18; matrix products, arithmetic and copies ran while one was open for 3% -> 0% of each run, Pallas kernels for 60% -> 65%
where the time goes in v3:
time: 430 us; the launch traced here: 426 us
  Pallas kernels  293 us (68%)
  waiting for transfers between devices  63 us (15%)
  starting transfers between devices  44.6 us (10%)
  between operations  15 us (3%)
  local copies, waits for them, and re-layouts  8.22 us (2%)
    pallas_call x3, Pallas kernels, attn_unit(): pl.pallas_call(functools.partial(attn_unit_kernel, first, count, given, a...  117 us
    pallas_call x3, Pallas kernels, mlp_unit(): pl.pallas_call(functools.partial(mlp_unit_kernel, first, count, given), g...  81.2 us
    ppermute x46, waiting for transfers between devices, exchange(): return lax.ppermute(value, AXES, pairs)  62.4 us
    ppermute x46, starting transfers between devices, exchange(): return lax.ppermute(value, AXES, pairs)  43.8 us
    pallas_call x16, Pallas kernels, add(): pl.pallas_call(add_kernel, grid=(count * steps,), in_specs=[read(first, s...  41.8 us
    pallas_call x4, Pallas kernels, split_add(): pl.pallas_call(split_add_kernel, grid=(1,), in_specs=[pl.BlockSpec(memory...  14.1 us
    pallas_call x4, Pallas kernels, pack(): pl.pallas_call(kernel, in_specs=[pl.BlockSpec(memory_space=pltpu.SMEM)] +...  11.9 us
    pallas_call x2, Pallas kernels, place(): pl.pallas_call(kernel, in_specs=[pl.BlockSpec(memory_space=pltpu.SMEM)] +...  10.1 us
  transfers between devices with their start and end apart: 49, of which 18 were waited for; matrix products, arithmetic and copies ran while one was open for 0% of the time, Pallas kernels for 65%

profile of v3, /device:TPU:0, one launch (start us, length us, event | category | flops | bytes accessed | tf_op | source)
XLA Modules:
  0.0 426.1 jit_solution(13329983036768447004)
XLA Ops:
  8.6 3.9 collective-permute-start.5
  15.0 3.2 attn_pack.2
  21.7 3.0 mlp_pack.3
  24.7 3.0 mlp_pack.2
  27.7 4.7 %collective-permute-done.1.refs_1_ = bf16[1,128,2048]{2,1,0:T(8,128)(2,1)} collective-permute-done((bf16[1,128,2048]{2,1,0:T(8,128)(2,1)}, bf16[1,128,2048]{2,1,0:T(8,128)(2,1)}, u32[]{:S(2)}, u32[]{:S(2)}) %collective-permute-start.1) | collective-permute-done | bytes 524320 | tf_op jit(solution)/shard_map/ppermute | solution.py:981
  38.4 6.4 %norm.1 = (bf16[1024,1024]{1,0:T(8,128)(2,1)}, bf16[1024,1024]{1,0:T(8,128)(2,1)}, bf16[1024,1024]{1,0:T(8,128)(2,1)}) custom-call(s32[11]{0:T(128)} %concatenate.3.table, bf16[1024,1024]{1,0:T(8,128)(2,1)} %x.19, bf16[1024,1024]{1,0:T(8,128)(2,1)} %grad.1, f32[1,1024]{1,0:T(1,128)} %get-tuple-element.212.gain_a, f32[1,1024]{1,0:T(1,128)} %get-tuple-element.213.shift_a, ...), custom_call_target="tpu_custom_call" | custom-call | flops 9999999827968 | bytes 1048576 | tf_op jit(solution)/shard_map/norm/pallas_call | solution.py:379
  47.8 53.7 %attn_unit.3 = (bf16[4,128,2048]{2,1,0:T(8,128)(2,1)}, bf16[4,128,2048]{2,1,0:T(8,128)(2,1)}, f32[1,1536]{1,0:T(1,128)}, f32[1024,1024]{1,0:T(8,128)}, f32[1024,1024]{1,0:T(8,128)}) custom-call(s32[11]{0:T(128)} %concatenate.3.table, bf16[1024,1024]{1,0:T(8,128)(2,1)} %get-tuple-element.221.na, bf16[1024,1024]{1,0:T(8,128)(2,1)} %get-tuple-element.222.gr, ...), custom_call_target="tpu_custom_call" | custom-call | flops 9999999827968 | bytes 1048576 | tf_op jit(solution)/shard_map/attn_unit/pallas_call | solution.py:800
  102.2 3.8 collective-permute-done.9.refs_1_
  107.3 3.7 add.103
  111.4 36.3 %mlp_unit.3 = (bf16[4,512,1024]{2,1,0:T(8,128)(2,1)}, bf16[4,512,1024]{2,1,0:T(8,128)(2,1)}, f32[1,2048]{1,0:T(1,128)}, f32[1024,1024]{1,0:T(8,128)}, f32[1024,1024]{1,0:T(8,128)}) custom-call(s32[11]{0:T(128)} %concatenate.3.table, bf16[1024,1024]{1,0:T(8,128)(2,1)} %get-tuple-element.224.nm, ...), custom_call_target="tpu_custom_call", output_to_operand_aliasing={{3}: (5, {})} | custom-call | flops 9999999827968 | bytes 1048576 | tf_op jit(solution)/shard_map/mlp_unit/pallas_call | solution.py:591
  150.1 5.2 %collective-permute-done.11.refs_1_ = bf16[4,512,1024]{2,1,0:T(8,128)(2,1)} collective-permute-done((bf16[4,512,1024]{2,1,0:T(8,128)(2,1)}, bf16[4,512,1024]{2,1,0:T(8,128)(2,1)}, u32[]{:S(2)}, u32[]{:S(2)}) %collective-permute-start.11) | collective-permute-done | bytes 4194336 | tf_op jit(solution)/shard_map/ppermute | solution.py:981
  155.3 4.4 %add.105 = bf16[2,512,1024]{2,1,0:T(8,128)(2,1)} custom-call(bf16[4,512,1024]{2,1,0:T(8,128)(2,1)} %get-tuple-element.278.refs_0_, bf16[4,512,1024]{2,1,0:T(8,128)(2,1)} %collective-permute-done.11.refs_1_), custom_call_target="tpu_custom_call" | custom-call | flops 9999999827968 | bytes 1048576 | tf_op jit(solution)/shard_map/add/pallas_call | solution.py:934
  162.5 22.3 %mlp_unit.4 = (bf16[4,512,1024]{2,1,0:T(8,128)(2,1)}, bf16[4,512,1024]{2,1,0:T(8,128)(2,1)}, f32[1,1024]{1,0:T(1,128)}, f32[1024,1024]{1,0:T(8,128)}, f32[1024,1024]{1,0:T(8,128)}) custom-call(s32[11]{0:T(128)} %concatenate.3.table, bf16[1024,1024]{1,0:T(8,128)(2,1)} %get-tuple-element.224.nm, ...), custom_call_target="tpu_custom_call", output_to_operand_aliasing={{3}: (5, {}), {4}: (6, {})} | custom-call | flops 9999999827968 | bytes 1048576 | tf_op jit(solution)/shard_map/mlp_unit/pallas_call | solution.py:591
  184.8 6.0 %collective-permute-done.13.refs_2_ = bf16[2,512,1024]{2,1,0:T(8,128)(2,1)} collective-permute-done((bf16[2,512,1024]{2,1,0:T(8,128)(2,1)}, bf16[2,512,1024]{2,1,0:T(8,128)(2,1)}, u32[]{:S(2)}, u32[]{:S(2)}) %collective-permute-start.13) | collective-permute-done | bytes 2097184 | tf_op jit(solution)/shard_map/ppermute | solution.py:981
  200.3 22.7 %mlp_unit.5 = (bf16[4,512,1024]{2,1,0:T(8,128)(2,1)}, bf16[4,512,1024]{2,1,0:T(8,128)(2,1)}, f32[1,1024]{1,0:T(1,128)}, f32[1024,1024]{1,0:T(8,128)}, f32[1024,1024]{1,0:T(8,128)}) custom-call(s32[11]{0:T(128)} %concatenate.3.table, ...), custom_call_target="tpu_custom_call", output_to_operand_aliasing={{0}: (5, {}), {1}: (6, {}), {3}: (7, {}), {4}: (8, {})} | custom-call | flops 9999999827968 | bytes 1048576 | tf_op jit(solution)/shard_map/mlp_unit/pallas_call | solution.py:591
  223.0 4.2 split_add.5
  230.5 4.3 %add.108 = bf16[2,512,1024]{2,1,0:T(8,128)(2,1)} custom-call(bf16[4,512,1024]{2,1,0:T(8,128)(2,1)} %get-tuple-element.317.refs_0_, bf16[4,512,1024]{2,1,0:T(8,128)(2,1)} %collective-permute-done.16.refs_1_), custom_call_target="tpu_custom_call" | custom-call | flops 9999999827968 | bytes 1048576 | tf_op jit(solution)/shard_map/add/pallas_call | solution.py:934
  238.5 31.0 %attn_unit.4 = (bf16[4,128,2048]{2,1,0:T(8,128)(2,1)}, bf16[4,128,2048]{2,1,0:T(8,128)(2,1)}, f32[1,768]{1,0:T(1,128)}, f32[1024,1024]{1,0:T(8,128)}, f32[1024,1024]{1,0:T(8,128)}) custom-call(s32[11]{0:T(128)} %concatenate.3.table, bf16[1024,1024]{1,0:T(8,128)(2,1)} %get-tuple-element.221.na, ...), custom_call_target="tpu_custom_call", output_to_operand_aliasing={{3}: (8, {}), {4}: (9, {})} | custom-call | flops 9999999827968 | bytes 1048576 | tf_op jit(solution)/shard_map/attn_unit/pallas_call | solution.py:800
  280.4 32.0 %attn_unit.5 = (bf16[4,128,2048]{2,1,0:T(8,128)(2,1)}, bf16[4,128,2048]{2,1,0:T(8,128)(2,1)}, f32[1,768]{1,0:T(1,128)}, f32[1024,1024]{1,0:T(8,128)}, f32[1024,1024]{1,0:T(8,128)}) custom-call(s32[11]{0:T(128)} %concatenate.3.table, ...), custom_call_target="tpu_custom_call", output_to_operand_aliasing={{0}: (10, {}), {1}: (11, {}), {3}: (12, {}), {4}: (13, {})} | custom-call | flops 9999999827968 | bytes 1048576 | tf_op jit(solution)/shard_map/attn_unit/pallas_call | solution.py:800
  312.5 4.2 split_add.6
  317.0 3.6 add.112
  321.8 9.5 %finish.1 = (f32[1024,1024]{1,0:T(8,128)}, f32[4,3072]{1,0:T(4,128)}) custom-call(s32[11]{0:T(128)} %concatenate.3.table, bf16[1024,1024]{1,0:T(8,128)(2,1)} %x.19, bf16[1024,1024]{1,0:T(8,128)(2,1)} %get-tuple-element.222.gr, f32[1024,1024]{1,0:T(8,128)} %get-tuple-element.333.dna, f32[1024,1024]{1,0:T(8,128)} %get-tuple-element.334.dnm, ...), custom_call_target="tpu_custom_call" | custom-call | flops 9999999827968 | bytes 1048576 | tf_op jit(solution)/shard_map/finish/pallas_call | solution.py:435
  331.3 4.8 %collective-permute-done.26.refs_2_ = bf16[2,128,2048]{2,1,0:T(8,128)(2,1)} collective-permute-done((bf16[2,128,2048]{2,1,0:T(8,128)(2,1)}, bf16[2,128,2048]{2,1,0:T(8,128)(2,1)}, u32[]{:S(2)}, u32[]{:S(2)}) %collective-permute-start.26) | collective-permute-done | bytes 1048608 | tf_op jit(solution)/shard_map/ppermute | solution.py:981
  343.0 4.6 %collective-permute-done.28.refs_3_ = bf16[1,128,2048]{2,1,0:T(8,128)(2,1)S(1)} collective-permute-done((bf16[1,128,2048]{2,1,0:T(8,128)(2,1)}, bf16[1,128,2048]{2,1,0:T(8,128)(2,1)S(1)}, u32[]{:S(2)}, u32[]{:S(2)}) %collective-permute-start.28) | collective-permute-done | bytes 524320 | tf_op jit(solution)/shard_map/ppermute | solution.py:981
  355.2 3.4 collective-permute-done.33
  358.6 9.4 %collective-permute-done.34.refs_1_ = bf16[1,64,2048]{2,1,0:T(8,128)(2,1)S(1)} collective-permute-done((bf16[1,64,2048]{2,1,0:T(8,128)(2,1)}, bf16[1,64,2048]{2,1,0:T(8,128)(2,1)S(1)}, u32[]{:S(2)}, u32[]{:S(2)}) %collective-permute-start.34) | collective-permute-done | bytes 262176 | tf_op jit(solution)/shard_map/ppermute | solution.py:981
  375.6 5.5 %collective-permute-start.37 = (bf16[1,64,2048]{2,1,0:T(8,128)(2,1)}, bf16[1,64,2048]{2,1,0:T(8,128)(2,1)S(1)}, u32[]{:S(2)}, u32[]{:S(2)}) collective-permute-start(bf16[1,64,2048]{2,1,0:T(8,128)(2,1)} %add.116.refs_0_), channel_id=1, source_target_pairs={{0,16},{1,17},{2,18},{3,19},{4,20},{5,21},{6,22},{7,23},{8,24},{9,... | collective-permute-start | bytes 786440 | tf_op jit(solution)/shard_map/ppermute | solution.py:981
  381.9 6.5 %collective-permute-done.30.refs_1_ = bf16[1,256,1024]{2,1,0:T(8,128)(2,1)S(1)} collective-permute-done((bf16[1,256,1024]{2,1,0:T(8,128)(2,1)S(1)}, bf16[1,256,1024]{2,1,0:T(8,128)(2,1)S(1)}, u32[]{:S(2)}, u32[]{:S(2)}) %collective-permute-start.30) | collective-permute-done | bytes 524320 | tf_op jit(solution)/shard_map/ppermute | solution.py:981
  388.9 4.7 %collective-permute-done.37.refs_1_ = bf16[1,64,2048]{2,1,0:T(8,128)(2,1)S(1)} collective-permute-done((bf16[1,64,2048]{2,1,0:T(8,128)(2,1)}, bf16[1,64,2048]{2,1,0:T(8,128)(2,1)S(1)}, u32[]{:S(2)}, u32[]{:S(2)}) %collective-permute-start.37) | collective-permute-done | bytes 262176 | tf_op jit(solution)/shard_map/ppermute | solution.py:981
  393.6 3.8 collective-permute-done.38.refs_5_
  403.1 6.2 %mlp_place.1 = (f32[256,4096]{1,0:T(8,128)}, f32[1024,1024]{1,0:T(8,128)}) custom-call(s32[11]{0:T(128)} %concatenate.3.table, bf16[1,256,1024]{2,1,0:T(8,128)(2,1)} %add.115.refs_0_, bf16[1,256,1024]{2,1,0:T(8,128)(2,1)} %copy-done.1, bf16[1,256,1024]{2,1,0:T(8,128)(2,1)} %copy-done.4, bf16[1,256,1024]{2,1,0:T(8,128)(2,1)} %copy-done.5, ...), custom_call_target="tpu_custom_call" | custom-call | tf_op jit(solution)/shard_map/mlp_place/pallas_call | solution.py:913
  413.2 3.9 attn_place.1
  (150 shorter events, 87.4 us)
Async XLA Ops:
  7.2 104.2 %all-gather.6.cloned.1.call-start = ((), (), s32[]{:S(2)}) async-start(), calls=%async_computation.1 | async-start | bytes 9437184 | tf_op jit(solution)/shard_map/all_gather | solution.py:1011
  8.6 28.1 %collective-permute-start.5 = (bf16[26,128]{1,0:T(8,128)(2,1)}, bf16[26,128]{1,0:T(8,128)(2,1)}, u32[]{:S(2)}, u32[]{:S(2)}) collective-permute-start(bf16[26,128]{1,0:T(8,128)(2,1)} %pad_add_fusion.refs_0_), channel_id=1, source_target_pairs={{0,3},{1,2},{2,1},{3,0},{4,7},{5,6},{6,5},{7,4},{8,11},{9,10},{10,... | collective-permute-start | bytes 19976 | tf_op jit(solution)/shard_map/ppermute | solution.py:981
  12.5 24.3 %collective-permute-start.4 = (bf16[26,128]{1,0:T(8,128)(2,1)}, bf16[26,128]{1,0:T(8,128)(2,1)}, u32[]{:S(2)}, u32[]{:S(2)}) collective-permute-start(bf16[26,128]{1,0:T(8,128)(2,1)} %pad_add_fusion.refs_0_), channel_id=1, source_target_pairs={{0,2},{1,3},{2,0},{3,1},{4,6},{5,7},{6,4},{7,5},{8,10},{9,11},{10,... | collective-permute-start | bytes 19976 | tf_op jit(solution)/shard_map/ppermute | solution.py:981
  13.0 23.8 %collective-permute-start.3 = (bf16[26,128]{1,0:T(8,128)(2,1)}, bf16[26,128]{1,0:T(8,128)(2,1)}, u32[]{:S(2)}, u32[]{:S(2)}) collective-permute-start(bf16[26,128]{1,0:T(8,128)(2,1)} %pad_add_fusion.refs_0_), channel_id=1, source_target_pairs={{0,1},{1,0},{2,3},{3,2},{4,5},{5,4},{6,7},{7,6},{8,9},{9,8},{10,11... | collective-permute-start | bytes 19976 | tf_op jit(solution)/shard_map/ppermute | solution.py:981
  18.2 14.2 %collective-permute-start.1 = (bf16[1,128,2048]{2,1,0:T(8,128)(2,1)}, bf16[1,128,2048]{2,1,0:T(8,128)(2,1)}, u32[]{:S(2)}, u32[]{:S(2)}) collective-permute-start(bf16[1,128,2048]{2,1,0:T(8,128)(2,1)} %get-tuple-element.208.refs_0_), channel_id=1, source_target_pairs={{0,2},{1,3},{2,0},{3,1},{4,5},{5,4},{6,7},{7,6},{8,10},{9,11},{10,... | collective-permute-start | bytes 1572872 | tf_op jit(solution)/shard_map/ppermute | solution.py:981
  20.3 12.2 %collective-permute-start = (bf16[1,128,2048]{2,1,0:T(8,128)(2,1)}, bf16[1,128,2048]{2,1,0:T(8,128)(2,1)}, u32[]{:S(2)}, u32[]{:S(2)}) collective-permute-start(bf16[1,128,2048]{2,1,0:T(8,128)(2,1)} %get-tuple-element.208.refs_0_), channel_id=1, source_target_pairs={{0,1},{1,0},{2,3},{3,2},{4,6},{5,7},{6,4},{7,5},{8,9},{9,8},{10,11... | collective-permute-start | bytes 1572872 | tf_op jit(solution)/shard_map/ppermute | solution.py:981
  32.4 13.4 %collective-permute-start.6 = (bf16[1,128,2048]{2,1,0:T(8,128)(2,1)}, bf16[1,128,2048]{2,1,0:T(8,128)(2,1)}, u32[]{:S(2)}, u32[]{:S(2)}) collective-permute-start(bf16[1,128,2048]{2,1,0:T(8,128)(2,1)} %collective-permute-done.refs_2_), channel_id=1, source_target_pairs={{0,4},{1,5},{2,6},{3,7},{4,0},{5,1},{6,2},{7,3},{8,12},{9,13},{10,... | collective-permute-start | bytes 1572872 | tf_op jit(solution)/shard_map/ppermute | solution.py:981
  32.4 12.3 %collective-permute-start.2 = (bf16[1,128,2048]{2,1,0:T(8,128)(2,1)}, bf16[1,128,2048]{2,1,0:T(8,128)(2,1)}, u32[]{:S(2)}, u32[]{:S(2)}) collective-permute-start(bf16[1,128,2048]{2,1,0:T(8,128)(2,1)} %collective-permute-done.refs_2_), channel_id=1, source_target_pairs={{0,2},{1,3},{2,0},{3,1},{4,5},{5,4},{6,7},{7,6},{8,10},{9,11},{10,... | collective-permute-start | bytes 1572872 | tf_op jit(solution)/shard_map/ppermute | solution.py:981
  45.3 117.2 %all-gather.4.cloned.1.call-start = ((), (), s32[]{:S(2)}) async-start(), calls=%async_computation | async-start | bytes 9437184 | tf_op jit(solution)/shard_map/all_gather | solution.py:1011
  102.0 136.5 %all-gather.8.cloned.1.call-start = ((), (), s32[]{:S(2)}) async-start(), calls=%async_computation.2 | async-start | bytes 4718592 | tf_op jit(solution)/shard_map/all_gather | solution.py:1011
  111.0 36.7 %collective-permute-start.10 = (bf16[2,128,2048]{2,1,0:T(8,128)(2,1)}, bf16[2,128,2048]{2,1,0:T(8,128)(2,1)}, u32[]{:S(2)}, u32[]{:S(2)}) collective-permute-start(bf16[2,128,2048]{2,1,0:T(8,128)(2,1)} %add.103), channel_id=1, source_target_pairs={{0,1},{1,0},{2,3},{3,2},{4,6},{5,7},{6,4},{7,5},{8,9},{9,8},{10,11... | collective-permute-start | bytes 3145736 | tf_op jit(solution)/shard_map/ppermute | solution.py:981
  159.6 25.2 %collective-permute-start.12 = (bf16[1,128,2048]{2,1,0:T(8,128)(2,1)}, bf16[1,128,2048]{2,1,0:T(8,128)(2,1)}, u32[]{:S(2)}, u32[]{:S(2)}) collective-permute-start(bf16[1,128,2048]{2,1,0:T(8,128)(2,1)} %add.104), channel_id=1, source_target_pairs={{0,2},{1,3},{2,0},{3,1},{4,5},{5,4},{6,7},{7,6},{8,10},{9,11},{10,... | collective-permute-start | bytes 1572872 | tf_op jit(solution)/shard_map/ppermute | solution.py:981
  161.9 28.9 %collective-permute-start.13 = (bf16[2,512,1024]{2,1,0:T(8,128)(2,1)}, bf16[2,512,1024]{2,1,0:T(8,128)(2,1)}, u32[]{:S(2)}, u32[]{:S(2)}) collective-permute-start(bf16[2,512,1024]{2,1,0:T(8,128)(2,1)} %add.105), channel_id=1, source_target_pairs={{0,1},{1,0},{2,3},{3,2},{4,6},{5,7},{6,4},{7,5},{8,9},{9,8},{10,11... | collective-permute-start | bytes 6291464 | tf_op jit(solution)/shard_map/ppermute | solution.py:981
  196.5 26.6 %collective-permute-start.14 = (bf16[1,64,2048]{2,1,0:T(8,128)(2,1)}, bf16[1,64,2048]{2,1,0:T(8,128)(2,1)}, u32[]{:S(2)}, u32[]{:S(2)}) collective-permute-start(bf16[1,64,2048]{2,1,0:T(8,128)(2,1)} %get-tuple-element.275), channel_id=1, source_target_pairs={{0,8},{1,9},{2,10},{3,11},{4,12},{5,13},{6,14},{7,15},{8,0},{9,1},... | collective-permute-start | bytes 786440 | tf_op jit(solution)/shard_map/ppermute | solution.py:981
  198.2 24.8 %collective-permute-start.15 = (bf16[1,512,1024]{2,1,0:T(8,128)(2,1)}, bf16[1,512,1024]{2,1,0:T(8,128)(2,1)}, u32[]{:S(2)}, u32[]{:S(2)}) collective-permute-start(bf16[1,512,1024]{2,1,0:T(8,128)(2,1)} %add.106), channel_id=1, source_target_pairs={{0,2},{1,3},{2,0},{3,1},{4,5},{5,4},{6,7},{7,6},{8,10},{9,11},{10,... | collective-permute-start | bytes 3145736 | tf_op jit(solution)/shard_map/ppermute | solution.py:981
  234.8 34.7 %collective-permute-start.17 = (bf16[1,64,2048]{2,1,0:T(8,128)(2,1)}, bf16[1,64,2048]{2,1,0:T(8,128)(2,1)}, u32[]{:S(2)}, u32[]{:S(2)}) collective-permute-start(bf16[1,64,2048]{2,1,0:T(8,128)(2,1)} %add.107.refs_0_), channel_id=1, source_target_pairs={{0,16},{1,17},{2,18},{3,19},{4,20},{5,21},{6,22},{7,23},{8,24},{9,... | collective-permute-start | bytes 786440 | tf_op jit(solution)/shard_map/ppermute | solution.py:981
  237.1 32.4 %collective-permute-start.18 = (bf16[1,256,1024]{2,1,0:T(8,128)(2,1)}, bf16[1,256,1024]{2,1,0:T(8,128)(2,1)}, u32[]{:S(2)}, u32[]{:S(2)}) collective-permute-start(bf16[1,256,1024]{2,1,0:T(8,128)(2,1)} %get-tuple-element.300), channel_id=1, source_target_pairs={{0,8},{1,9},{2,10},{3,11},{4,12},{5,13},{6,14},{7,15},{8,0},{9,1},... | collective-permute-start | bytes 1572872 | tf_op jit(solution)/shard_map/ppermute | solution.py:981
  238.5 31.1 %collective-permute-start.19 = (bf16[2,512,1024]{2,1,0:T(8,128)(2,1)}, bf16[2,512,1024]{2,1,0:T(8,128)(2,1)}, u32[]{:S(2)}, u32[]{:S(2)}) collective-permute-start(bf16[2,512,1024]{2,1,0:T(8,128)(2,1)} %add.108), channel_id=1, source_target_pairs={{0,1},{1,0},{2,3},{3,2},{4,6},{5,7},{6,4},{7,5},{8,9},{9,8},{10,11... | collective-permute-start | bytes 6291464 | tf_op jit(solution)/shard_map/ppermute | solution.py:981
  276.3 36.1 %collective-permute-start.23 = (bf16[1,64,2048]{2,1,0:T(8,128)(2,1)}, bf16[1,64,2048]{2,1,0:T(8,128)(2,1)}, u32[]{:S(2)}, u32[]{:S(2)}) collective-permute-start(bf16[1,64,2048]{2,1,0:T(8,128)(2,1)} %add.109.refs_0_), channel_id=1, source_target_pairs={{0,4},{1,5},{2,6},{3,7},{4,0},{5,1},{6,2},{7,3},{8,12},{9,13},{10,... | collective-permute-start | bytes 786440 | tf_op jit(solution)/shard_map/ppermute | solution.py:981
  276.4 36.1 %collective-permute-start.22 = (bf16[1,64,2048]{2,1,0:T(8,128)(2,1)}, bf16[1,64,2048]{2,1,0:T(8,128)(2,1)}, u32[]{:S(2)}, u32[]{:S(2)}) collective-permute-start(bf16[1,64,2048]{2,1,0:T(8,128)(2,1)} %add.109.refs_0_), channel_id=1, source_target_pairs={{0,8},{1,9},{2,10},{3,11},{4,12},{5,13},{6,14},{7,15},{8,0},{9,1},... | collective-permute-start | bytes 786440 | tf_op jit(solution)/shard_map/ppermute | solution.py:981
  278.5 34.0 %collective-permute-start.21 = (bf16[1,256,1024]{2,1,0:T(8,128)(2,1)}, bf16[1,256,1024]{2,1,0:T(8,128)(2,1)}, u32[]{:S(2)}, u32[]{:S(2)}) collective-permute-start(bf16[1,256,1024]{2,1,0:T(8,128)(2,1)} %add.110.refs_0_), channel_id=1, source_target_pairs={{0,16},{1,17},{2,18},{3,19},{4,20},{5,21},{6,22},{7,23},{8,24},{9,... | collective-permute-start | bytes 1572872 | tf_op jit(solution)/shard_map/ppermute | solution.py:981
  279.0 33.5 %collective-permute-start.20 = (bf16[1,512,1024]{2,1,0:T(8,128)(2,1)}, bf16[1,512,1024]{2,1,0:T(8,128)(2,1)}, u32[]{:S(2)}, u32[]{:S(2)}) collective-permute-start(bf16[1,512,1024]{2,1,0:T(8,128)(2,1)} %add.111), channel_id=1, source_target_pairs={{0,2},{1,3},{2,0},{3,1},{4,5},{5,4},{6,7},{7,6},{8,10},{9,11},{10,... | collective-permute-start | bytes 3145736 | tf_op jit(solution)/shard_map/ppermute | solution.py:981
  320.6 17.7 %collective-permute-start.27 = (bf16[1,256,1024]{2,1,0:T(8,128)(2,1)}, bf16[1,256,1024]{2,1,0:T(8,128)(2,1)}, u32[]{:S(2)}, u32[]{:S(2)}) collective-permute-start(bf16[1,256,1024]{2,1,0:T(8,128)(2,1)} %get-tuple-element.352), channel_id=1, source_target_pairs={{0,8},{1,9},{2,10},{3,11},{4,12},{5,13},{6,14},{7,15},{8,0},{9,1},... | collective-permute-start | bytes 1572872 | tf_op jit(solution)/shard_map/ppermute | solution.py:981
  321.0 15.1 %collective-permute-start.26 = (bf16[2,128,2048]{2,1,0:T(8,128)(2,1)}, bf16[2,128,2048]{2,1,0:T(8,128)(2,1)}, u32[]{:S(2)}, u32[]{:S(2)}) collective-permute-start(bf16[2,128,2048]{2,1,0:T(8,128)(2,1)} %add.112), channel_id=1, source_target_pairs={{0,1},{1,0},{2,3},{3,2},{4,6},{5,7},{6,4},{7,5},{8,9},{9,8},{10,11... | collective-permute-start | bytes 3145736 | tf_op jit(solution)/shard_map/ppermute | solution.py:981
  347.7 24.5 %collective-permute-start.35 = (bf16[1,256,1024]{2,1,0:T(8,128)(2,1)}, bf16[1,256,1024]{2,1,0:T(8,128)(2,1)S(1)}, u32[]{:S(2)}, u32[]{:S(2)}) collective-permute-start(bf16[1,256,1024]{2,1,0:T(8,128)(2,1)} %add.114.refs_0_), channel_id=1, source_target_pairs={{0,16},{1,17},{2,18},{3,19},{4,20},{5,21},{6,22},{7,23},{8,24},{9,... | collective-permute-start | bytes 1572872 | tf_op jit(solution)/shard_map/ppermute | solution.py:981
  352.5 15.5 %collective-permute-start.34 = (bf16[1,64,2048]{2,1,0:T(8,128)(2,1)}, bf16[1,64,2048]{2,1,0:T(8,128)(2,1)S(1)}, u32[]{:S(2)}, u32[]{:S(2)}) collective-permute-start(bf16[1,64,2048]{2,1,0:T(8,128)(2,1)} %get-tuple-element.368), channel_id=1, source_target_pairs={{0,8},{1,9},{2,10},{3,11},{4,12},{5,13},{6,14},{7,15},{8,0},{9,1},... | collective-permute-start | bytes 786440 | tf_op jit(solution)/shard_map/ppermute | solution.py:981
  355.2 33.2 %collective-permute-start.30 = (bf16[1,256,1024]{2,1,0:T(8,128)(2,1)S(1)}, bf16[1,256,1024]{2,1,0:T(8,128)(2,1)S(1)}, u32[]{:S(2)}, u32[]{:S(2)}) collective-permute-start(bf16[1,256,1024]{2,1,0:T(8,128)(2,1)S(1)} %copy-done), channel_id=1, source_target_pairs={{0,8},{1,9},{2,10},{3,11},{4,12},{5,13},{6,14},{7,15},{8,0},{9,1},... | collective-permute-start | bytes 1572872 | tf_op jit(solution)/shard_map/ppermute | solution.py:981
  374.9 18.6 %collective-permute-start.39 = (bf16[1,256,1024]{2,1,0:T(8,128)(2,1)}, bf16[1,256,1024]{2,1,0:T(8,128)(2,1)S(1)}, u32[]{:S(2)}, u32[]{:S(2)}) collective-permute-start(bf16[1,256,1024]{2,1,0:T(8,128)(2,1)} %add.117.refs_4_), channel_id=1, source_target_pairs={{0,4},{1,5},{2,6},{3,7},{4,0},{5,1},{6,2},{7,3},{8,12},{9,13},{10,... | collective-permute-start | bytes 1572872 | tf_op jit(solution)/shard_map/ppermute | solution.py:981
  375.0 22.4 %collective-permute-start.38 = (bf16[1,256,1024]{2,1,0:T(8,128)(2,1)}, bf16[1,256,1024]{2,1,0:T(8,128)(2,1)S(1)}, u32[]{:S(2)}, u32[]{:S(2)}) collective-permute-start(bf16[1,256,1024]{2,1,0:T(8,128)(2,1)} %add.117.refs_4_), channel_id=1, source_target_pairs={{0,8},{1,9},{2,10},{3,11},{4,12},{5,13},{6,14},{7,15},{8,0},{9,1},... | collective-permute-start | bytes 1572872 | tf_op jit(solution)/shard_map/ppermute | solution.py:981
  375.6 17.9 %collective-permute-start.37 = (bf16[1,64,2048]{2,1,0:T(8,128)(2,1)}, bf16[1,64,2048]{2,1,0:T(8,128)(2,1)S(1)}, u32[]{:S(2)}, u32[]{:S(2)}) collective-permute-start(bf16[1,64,2048]{2,1,0:T(8,128)(2,1)} %add.116.refs_0_), channel_id=1, source_target_pairs={{0,16},{1,17},{2,18},{3,19},{4,20},{5,21},{6,22},{7,23},{8,24},{9,... | collective-permute-start | bytes 786440 | tf_op jit(solution)/shard_map/ppermute | solution.py:981
  388.4 13.7 %collective-permute-start.31 = (bf16[1,256,1024]{2,1,0:T(8,128)(2,1)S(1)}, bf16[1,256,1024]{2,1,0:T(8,128)(2,1)S(1)}, u32[]{:S(2)}, u32[]{:S(2)}) collective-permute-start(bf16[1,256,1024]{2,1,0:T(8,128)(2,1)S(1)} %copy-done), channel_id=1, source_target_pairs={{0,4},{1,5},{2,6},{3,7},{4,0},{5,1},{6,2},{7,3},{8,12},{9,13},{10,... | collective-permute-start | bytes 1572872 | tf_op jit(solution)/shard_map/ppermute | solution.py:981
  388.4 13.8 %collective-permute-start.32 = (bf16[1,256,1024]{2,1,0:T(8,128)(2,1)S(1)}, bf16[1,256,1024]{2,1,0:T(8,128)(2,1)S(1)}, u32[]{:S(2)}, u32[]{:S(2)}) collective-permute-start(bf16[1,256,1024]{2,1,0:T(8,128)(2,1)S(1)} %collective-permute-done.30.refs_1_), channel_id=1, source_target_pairs={{0,4},{1,5},{2,6},{3,7},{4,0},{5,1},{6,2},{7,3},{8,12},{9,13},{10,... | collective-permute-start | bytes 1572872 | tf_op jit(solution)/shard_map/ppermute | solution.py:981
  (34 other events, 177.8 us)
Sparse Core Ops, SparseCore 0:
  45.4 54.5 all-gather.5
  102.4 60.0 all-gather.3
  196.6 40.3 all-gather.7

commit v4 on v3

--- a/solution.py
+++ b/solution.py
@@ -699,15 +699,15 @@
             v[h, r, :] = values[:, c]
             dc[h, r, :] = context_grad[:, c]
 
-    block = 256
+    block = 512
     inside = lax.broadcasted_iota(jnp.int32, (1, T), 1) < table[1]
     outside = jnp.where(inside, 0.0, MASKED).astype(F32)
     below = lax.broadcasted_iota(jnp.int32, (block, block), 1) <= lax.broadcasted_iota(jnp.int32, (block, block), 0)
     causal = jnp.where(below, 0.0, MASKED).astype(F32)
 
     def head(h, carry):
-        dk[h] = jnp.zeros((T, HD), F32)
-        dv[h] = jnp.zeros((T, HD), F32)
+        dk[h] = jnp.zeros((HD, T), F32)
+        dv[h] = jnp.zeros((HD, T), F32)
         for i in range(T // block):
             r = rows_of(i, block)
             spans = ([slice(0, i * block)] if i else []) + [r]
@@ -725,9 +725,10 @@
             inner = scale * sum(jnp.sum(e * p, axis=1, keepdims=True) for e, p in zip(weights, probs_grad))
             score_grad = [(e * (p - inner)).astype(BF) for e, p in zip(weights, probs_grad)]
             dq[h, r, :] = sum(nn(s, k[h, c, :]) for s, c in zip(score_grad, spans))
+            query_turned, grad_turned = query.T, scaled_grad.T
             for s, e, c in zip(score_grad, low, spans):
-                dk[h, c, :] += tn(s, query)
-                dv[h, c, :] += tn(e, scaled_grad)
+                dk[h, :, c] += nn(query_turned, s)
+                dv[h, :, c] += nn(grad_turned, e)
         return carry
 
     lax.fori_loop(0, HEADS, head, 0)
@@ -749,8 +750,8 @@
         projected_grad = jnp.concatenate(
             [
                 turn(together(dq, r) * 0.125, r, True).astype(BF),
-                turn(together(dk, r), r, True).astype(BF),
-                together(dv, r).astype(BF),
+                turn(jnp.concatenate([dk[h, :, r] for h in range(HEADS)], axis=0).T, r, True).astype(BF),
+                jnp.concatenate([dv[h, :, r] for h in range(HEADS)], axis=0).T.astype(BF),
             ],
             axis=1,
         )
@@ -812,7 +813,7 @@
         input_output_aliases=aliases,
         scratch_shapes=[pltpu.VMEM((count, D, 3 * GROUP), BF), pltpu.VMEM((count, GROUP, D), BF)]
         + [head_rows(BF)] * 5
-        + [head_rows(F32)] * 3
+        + [head_rows(F32)] + [pltpu.VMEM((HEADS, HD, T), F32)] * 2
         + [
             pltpu.VMEM((T, 4 * GROUP), BF),
             pltpu.VMEM((T, D), F32),
@@ -942,29 +943,47 @@
     )(*(array for array, _, _ in sources))
 
 
-def split_add_kernel(table, *refs):
-    *sources, kept, sent = refs
-    total = sum(source[...].astype(F32) for source in sources).astype(BF)
-    half = total.shape[1] // 2
-    for parity in range(2):
-
-        @pl.when(table[10] == parity)
+def sums_kernel(plan, table, *refs):
+    refs = list(refs)
+    taken = [[refs.pop(0) for _ in range(count)] for count, _ in plan]
+    for sources, (_, split) in zip(taken, plan):
+        total = sum(source[...].astype(F32) for source in sources).astype(BF)
+        if not split:
+            refs.pop(0)[...] = total
+            continue
+        kept, sent = refs.pop(0), refs.pop(0)
+
+        @pl.when(pl.program_id(0) == table[10])
         def _():
-            kept[...] = total[:, rows_of(parity, half)]
-            sent[...] = total[:, rows_of(1 - parity, half)]
-
-
-def split_add(table, *arrays, cost=LONG):
-    rows, columns = arrays[0].shape[1:]
+            kept[...] = total
+
+        @pl.when(pl.program_id(0) != table[10])
+        def _():
+            sent[...] = total
+
+
+def sums(table, *jobs, cost=LONG):
+    specs, arrays, out_specs, out_shapes, plan = [], [], [], [], []
+    for split, sources in jobs:
+        sources = [source if isinstance(source, tuple) else (source, 0) for source in sources]
+        rows, columns = sources[0][0].shape[1] // 2, sources[0][0].shape[2]
+        for array, block in sources:
+            arrays.append(array)
+            specs.append(pl.BlockSpec((1, rows, columns), lambda i, block=block: (block, i, 0)))
+        plan.append((len(sources), split))
+        place = (lambda i: (0, 0, 0)) if split else (lambda i: (0, i, 0))
+        for _ in range(1 + split):
+            out_specs.append(pl.BlockSpec((1, rows, columns), place))
+            out_shapes.append(jax.ShapeDtypeStruct((1, rows * (1 if split else 2), columns), BF))
     return pl.pallas_call(
-        split_add_kernel,
-        grid=(1,),
-        in_specs=[pl.BlockSpec(memory_space=pltpu.SMEM)]
-        + [pl.BlockSpec((1, rows, columns), lambda i: (0, 0, 0))] * len(arrays),
-        out_specs=[pl.BlockSpec((1, rows // 2, columns), lambda i: (0, 0, 0))] * 2,
-        out_shape=[jax.ShapeDtypeStruct((1, rows // 2, columns), BF)] * 2,
+        functools.partial(sums_kernel, plan),
+        grid=(2,),
+        in_specs=[pl.BlockSpec(memory_space=pltpu.SMEM)] + specs,
+        out_specs=out_specs,
+        out_shape=out_shapes,
+        compiler_params=pltpu.CompilerParams(vmem_limit_bytes=VMEM // 2),
         cost_estimate=cost,
-        name="split_add",
+        name="sums",
     )(table, *arrays)
 
 
@@ -1000,10 +1019,10 @@
     dense_weight, dense_bias, inner_weight, inner_bias, outer_weight, outer_bias,
 ):
     core = lax.axis_index("core")
-    own = lax.axis_index("y") * 2 + lax.axis_index("x")
+    place_in_group = lax.axis_index("y") * 2 + lax.axis_index("x")
     steps = jnp.where(core == 0, jnp.array([0, 2, 1, 3], jnp.int32), jnp.array([0, 1, 2, 3], jnp.int32))
-    shard_of = own ^ steps
-    difference = own ^ jnp.arange(4, dtype=jnp.int32)
+    shard_of = place_in_group ^ steps
+    difference = place_in_group ^ jnp.arange(4, dtype=jnp.int32)
     block_of = jnp.where(core == 1, difference, ((difference & 1) << 1) | (difference >> 1))
     parity = lax.axis_index("z") % 2
     table = jnp.concatenate([core[None], seq_lengths, block_of, shard_of, parity[None]]).astype(jnp.int32)
@@ -1020,14 +1039,14 @@
         return lax.optimization_barrier((done,) + values)
 
     part, rest = pack_attn(0, 2)
-    vectors = (attn_gain, attn_shift, mlp_gain, mlp_shift, dense_bias, outer_bias, qkv_bias, inner_bias)
-    part, table = after(part, table)
     from_first = exchange(part, to_first)
     from_second = exchange(part, to_second)
-    packed = [pack_mlp(0), pack_mlp(1)]
+    vectors = (attn_gain, attn_shift, mlp_gain, mlp_shift, dense_bias, outer_bias, qkv_bias, inner_bias)
+    part, table, *vectors = after(part, table, *vectors)
     vectors = [vector.reshape(-1, 128) for vector in vectors]
     ends = np.cumsum([vector.shape[0] for vector in vectors])
     vectors = sum(jnp.pad(v, ((end - v.shape[0], 26 - end), (0, 0))) for v, end in zip(vectors, ends))
+    packed = [pack_mlp(0), pack_mlp(1)]
     vectors = [vectors] + [exchange(vectors, to) for to in (to_x, to_y, to_xy)]
     from_first, from_second, table, *packed = after(from_first, from_second, table, *packed)
     from_both = exchange(from_first, to_second)
@@ -1036,8 +1055,6 @@
     gain_a, shift_a, gain_m, shift_m, bias_out, *biases = spread(table, vectors)
     bias_pairs, bias_units = biases[:2], biases[2:]
     na, nm, gr = norm(table, layer_input, out_grad, (gain_a, shift_a, gain_m, shift_m))
-    packed_b = pack_attn(1, 1)[0]
-    from_both, na, packed_b, *packed = after(from_both, na, packed_b, *packed)
     pieces = [None] + [gather(piece) for piece in packed]
     na, from_both = after(na, from_both)
     core_both = exchange(from_both, to_core)
@@ -1045,9 +1062,9 @@
     tables = [jnp.asarray(t) for t in rotary_tables()]
 
     far_blocks = lambda keep, got, cost=LONG: add((keep, 2, 1), (got, 1, 2), count=2, cost=cost)
-    near_block = lambda keep, got, far, cost=LONG: add((keep, 1, 1), (got, 2, 1), (far, 1, 1), cost=cost)
-    own_block = lambda *arrays: add(*((array, 0, 1) for array in arrays))
-    plus = lambda total, got: add((total, 0, 1), (got, 0, 1), cost=None)
+    near = lambda keep, got, far: (False, [(keep, 1), (got, 2), (far, 1)])
+    own = lambda *arrays: (True, arrays)
+    plus = lambda *arrays: (False, arrays)
 
     none = (None, None)
     attn_call = lambda first, count, pair, parts, totals, rest=(): attn_unit(
@@ -1059,7 +1076,9 @@
 
     keep_a, send_a, gb0, out, dna = attn_call(0, 2, 0, none, none)
     got_a = exchange(send_a, to_core)
-    out, keep_a, got_a = after(out, keep_a, got_a)
+    out, table = after(out, table)
+    packed_b = pack_attn(1, 1)[0]
+    out, keep_a, got_a, packed_b = after(out, keep_a, got_a, packed_b)
     far_a = far_blocks(keep_a, got_a)
     out, far_a = after(out, far_a)
     far_a = exchange(far_a, to_first)
@@ -1067,7 +1086,7 @@
     keep_m, send_m, gbi0, out, dnm = mlp_call(0, 4, 0, none, (out, None))
     got_m = exchange(send_m, to_core)
     out, keep_a, got_a, far_a = after(out, keep_a, got_a, far_a)
-    near_a = near_block(keep_a, got_a, far_a)
+    (near_a,) = sums(table, near(keep_a, got_a, far_a))
     near_a, keep_m, got_m = after(near_a, keep_m, got_m)
     far_m = far_blocks(keep_m, got_m)
     out, near_a, far_m = after(out, near_a, far_m)
@@ -1078,8 +1097,7 @@
     out, keep_a, got_a, far_a, near_a, keep_m, got_m, far_m = after(
         out, keep_a, got_a, far_a, near_a, keep_m, got_m, far_m
     )
-    kept_a, sent_a = split_add(table, keep_a, got_a, far_a, near_a)
-    near_m = near_block(keep_m, got_m, far_m)
+    kept_a, sent_a, near_m = sums(table, own(keep_a, got_a, far_a, near_a), near(keep_m, got_m, far_m))
     out, kept_a, sent_a, near_m, packed_b = after(out, kept_a, sent_a, near_m, packed_b)
     pieces.append(gather(packed_b))
     sent_a = exchange(sent_a, to_below)
@@ -1090,8 +1108,7 @@
     out, kept_a, sent_a, keep_m, got_m, far_m, near_m = after(
         out, kept_a, sent_a, keep_m, got_m, far_m, near_m
     )
-    kept_m, sent_m = split_add(table, keep_m, got_m, far_m, near_m)
-    kept_a = plus(kept_a, sent_a)
+    kept_m, sent_m, kept_a = sums(table, own(keep_m, got_m, far_m, near_m), plus(kept_a, sent_a))
     kept_m, sent_m, kept_a, keep_n, got_n = after(kept_m, sent_m, kept_a, keep_n, got_n)
     far_n = far_blocks(keep_n, got_n)
     out, kept_m, sent_m, kept_a, far_n = after(out, kept_m, sent_m, kept_a, far_n)
@@ -1103,9 +1120,9 @@
     out, kept_a, got_kept_a, kept_m, sent_m, keep_n, got_n, far_n = after(
         out, kept_a, got_kept_a, kept_m, sent_m, keep_n, got_n, far_n
     )
-    kept_a = plus(kept_a, got_kept_a)
-    kept_m = plus(kept_m, sent_m)
-    near_n = near_block(keep_n, got_n, far_n)
+    kept_a, kept_m, near_n = sums(
+        table, plus(kept_a, got_kept_a), plus(kept_m, sent_m), near(keep_n, got_n, far_n)
+    )
     out, kept_a, kept_m, near_n = after(out, kept_a, kept_m, near_n)
     got_kept_m = exchange(kept_m, to_two)
     near_n = exchange(near_n, to_second)
@@ -1117,46 +1134,46 @@
     layer_output, keep_n, got_n, far_n, near_n, kept_m, got_kept_m, *pieces_a = after(
         layer_output, keep_n, got_n, far_n, near_n, kept_m, got_kept_m, *pieces_a
     )
-    kept_n, sent_n = split_add(table, keep_n, got_n, far_n, near_n)
+    kept_n, sent_n, kept_m = sums(table, own(keep_n, got_n, far_n, near_n), plus(kept_m, got_kept_m))
     kept_n, sent_n, keep_b, got_b = after(kept_n, sent_n, keep_b, got_b)
+    sent_n = exchange(sent_n, to_below)
+    pieces_m = [kept_m, exchange(kept_m, to_below), exchange(kept_m, to_core)]
     far_b = far_blocks(keep_b, got_b, None)
-    far_b, kept_n, sent_n, kept_m, got_kept_m, dna, dnm = after(far_b, kept_n, sent_n, kept_m, got_kept_m, dna, dnm)
+    far_b, dna, dnm = after(far_b, dna, dnm)
     far_b = exchange(far_b, to_first)
-    sent_n = exchange(sent_n, to_below)
     pieces_a.append(exchange(pieces_a[1], to_core))
 
     bias_sums = [gb0, gb1a, gb1b, gbi0, gbi1a, gbi1b]
     input_grad, small = finish(table, layer_input, gr, dna, dnm, (gain_a, gain_m), bias_sums)
-    small, far_b, keep_b, got_b = after(small, far_b, keep_b, got_b)
-    near_b = near_block(keep_b, got_b, far_b, None)
-    near_b, small, kept_n, sent_n = after(near_b, small, kept_n, sent_n)
+    small, kept_n, sent_n = after(small, kept_n, sent_n)
+    (kept_n,) = sums(table, plus(kept_n, sent_n), cost=None)
+    kept_n, small, far_b, keep_b, got_b = after(kept_n, small, far_b, keep_b, got_b)
+    got_kept_n = exchange(kept_n, to_two)
+    (near_b,) = sums(table, near(keep_b, got_b, far_b))
+    near_b, small = after(near_b, small)
     near_b = exchange(near_b, to_second)
     got_small = exchange(small, to_core)
-    kept_n = plus(kept_n, sent_n)
-    kept_m = plus(kept_m, got_kept_m)
-    kept_n, kept_m, near_b, small, got_small = after(kept_n, kept_m, near_b, small, got_small)
-    kept_b, sent_b = split_add(table, keep_b, got_b, far_b, near_b, cost=None)
+    near_b, small, got_small, *pieces_m = after(near_b, small, got_small, *pieces_m)
+    kept_b, sent_b = sums(table, own(keep_b, got_b, far_b, near_b), cost=None)
     small = small + got_small
-    kept_b, sent_b, small, kept_m = after(kept_b, sent_b, small, kept_m)
+    kept_b, sent_b, small, *pieces_m = after(kept_b, sent_b, small, *pieces_m)
     sent_b = exchange(sent_b, to_below)
-    got_kept_n = exchange(kept_n, to_two)
     got_small = exchange(small, to_x)
-    pieces_m = [kept_m, exchange(kept_m, to_below), exchange(kept_m, to_core)]
+    pieces_m.append(exchange(pieces_m[1], to_core))
     small, got_small, kept_b, sent_b = after(small, got_small, kept_b, sent_b)
-    kept_b = plus(kept_b, sent_b)
     small = small + got_small
+    (kept_b,) = sums(table, plus(kept_b, sent_b), cost=None)
     kept_b, small, kept_n, got_kept_n = after(kept_b, small, kept_n, got_kept_n)
     got_kept_b = exchange(kept_b, to_two)
     got_small = exchange(small, to_y)
-    kept_n = plus(kept_n, got_kept_n)
+    (kept_n,) = sums(table, plus(kept_n, got_kept_n), cost=None)
     pieces_n = [kept_n, exchange(kept_n, to_below), exchange(kept_n, to_core)]
     small, got_small, kept_b, got_kept_b, *pieces_n = after(small, got_small, kept_b, got_kept_b, *pieces_n)
-    kept_b = plus(kept_b, got_kept_b)
+    (kept_b,) = sums(table, plus(kept_b, got_kept_b), cost=None)
     small = small + got_small
     kept_b, small = after(kept_b, small)
     pieces_b = [kept_b, exchange(kept_b, to_below), exchange(kept_b, to_core)]
     pieces_n.append(exchange(pieces_n[1], to_core))
-    pieces_m.append(exchange(pieces_m[1], to_core))
     got_small = exchange(small, to_below)
     grad_wi, grad_wo = place(mlp_place_kernel, ((256, FF), (1024, D)), "mlp_place", table, *pieces_m, *pieces_n)
     grad_wi, small, got_small, *pieces_b = after(grad_wi, small, got_small, *pieces_b)
@@ -1167,7 +1184,7 @@
         attn_place_kernel, ((256, 3 * D), (256, D)), "attn_place", table, *pieces_a, *pieces_b
     )
     grad_d, small, got_small = after(grad_d, small, got_small)
-    small = lax.dynamic_index_in_dim(small + got_small, own, 0, keepdims=False)
+    small = lax.dynamic_index_in_dim(small + got_small, place_in_group, 0, keepdims=False)
     g_ga, g_sa, g_gm, g_sm, g_bd, g_bqkv, g_bi = jnp.split(small, np.cumsum([256] * 5 + [768]))
     return (
         layer_output, input_grad, g_ga, g_sa, g_gm, g_sm, grad_qkv, g_bqkv, grad_d, g_bd, grad_wi, g_bi, grad_wo, g_bd,

time: 430 us -> 405 us (0.942)
  Pallas kernels: 293 us -> 267 us
  waiting for transfers between devices: 63 us -> 71 us
    pallas_call x16 -> x4, Pallas kernels: 41.8 us -> 16 us  [add(): pl.pallas_call(add_kernel, grid=(count * steps,), in_specs=[read(first, s...]
    pallas_call x3, Pallas kernels: 117 us -> 108 us  [attn_unit(): pl.pallas_call(functools.partial(attn_unit_kernel, first, count, given, a...]
    ppermute x46, waiting for transfers between devices: 62.4 us -> 71 us  [exchange(): return lax.ppermute(value, AXES, pairs)]
    pallas_call x4 -> x11, Pallas kernels: 14.1 us -> 21.2 us  [sums(): pl.pallas_call(functools.partial(sums_kernel, plan), grid=(2,), in_specs=...]
  transfers between devices with their start and end apart: 49 -> 49, of which waited for: 18 -> 15; matrix products, arithmetic and copies ran while one was open for 0% -> 0% of each run, Pallas kernels for 65% -> 64%
where the time goes in v4:
time: 405 us; the launch traced here: 402 us
  Pallas kernels  267 us (66%)
  waiting for transfers between devices  71 us (18%)
  starting transfers between devices  40.8 us (10%)
  between operations  15.5 us (4%)
  local copies, waits for them, and re-layouts  6.65 us (2%)
    pallas_call x3, Pallas kernels, attn_unit(): pl.pallas_call(functools.partial(attn_unit_kernel, first, count, given, a...  108 us
    pallas_call x3, Pallas kernels, mlp_unit(): pl.pallas_call(functools.partial(mlp_unit_kernel, first, count, given), g...  82.2 us
    ppermute x46, waiting for transfers between devices, exchange(): return lax.ppermute(value, AXES, pairs)  71 us
    ppermute x46, starting transfers between devices, exchange(): return lax.ppermute(value, AXES, pairs)  40.5 us
    pallas_call x11, Pallas kernels, sums(): pl.pallas_call(functools.partial(sums_kernel, plan), grid=(2,), in_specs=...  21.2 us
    pallas_call x4, Pallas kernels, add(): pl.pallas_call(add_kernel, grid=(count * steps,), in_specs=[read(first, s...  16 us
    pallas_call x4, Pallas kernels, pack(): pl.pallas_call(kernel, in_specs=[pl.BlockSpec(memory_space=pltpu.SMEM)] +...  12 us
    pallas_call x2, Pallas kernels, place(): pl.pallas_call(kernel, in_specs=[pl.BlockSpec(memory_space=pltpu.SMEM)] +...  10.1 us
  transfers between devices with their start and end apart: 49, of which 15 were waited for; matrix products, arithmetic and copies ran while one was open for 0% of the time, Pallas kernels for 64%

profile of v4, /device:TPU:0, one launch (start us, length us, event | category | flops | bytes accessed | tf_op | source)
XLA Modules:
  0.0 402.0 jit_solution(5265414622848387477)
XLA Ops:
  9.2 3.3 attn_pack.2
  13.3 3.9 collective-permute-start.4
  21.2 3.0 mlp_pack.3
  24.2 3.0 mlp_pack.2
  27.2 4.8 %collective-permute-done.1.refs_1_ = bf16[1,128,2048]{2,1,0:T(8,128)(2,1)} collective-permute-done((bf16[1,128,2048]{2,1,0:T(8,128)(2,1)}, bf16[1,128,2048]{2,1,0:T(8,128)(2,1)}, u32[]{:S(2)}, u32[]{:S(2)}) %collective-permute-start.1) | collective-permute-done | bytes 524320 | tf_op jit(solution)/shard_map/ppermute | solution.py:1000
  35.2 6.4 %norm.1 = (bf16[1024,1024]{1,0:T(8,128)(2,1)}, bf16[1024,1024]{1,0:T(8,128)(2,1)}, bf16[1024,1024]{1,0:T(8,128)(2,1)}) custom-call(s32[11]{0:T(128)} %concatenate.3.table, bf16[1024,1024]{1,0:T(8,128)(2,1)} %x.19, bf16[1024,1024]{1,0:T(8,128)(2,1)} %grad.1, f32[1,1024]{1,0:T(1,128)} %get-tuple-element.231.gain_a, f32[1,1024]{1,0:T(1,128)} %get-tuple-element.232.shift_a, ...), custom_call_target="tpu_custom_call" | custom-call | flops 9999999827968 | bytes 1048576 | tf_op jit(solution)/shard_map/norm/pallas_call | solution.py:379
  44.6 48.6 %attn_unit.3 = (bf16[4,128,2048]{2,1,0:T(8,128)(2,1)}, bf16[4,128,2048]{2,1,0:T(8,128)(2,1)}, f32[1,1536]{1,0:T(1,128)}, f32[1024,1024]{1,0:T(8,128)}, f32[1024,1024]{1,0:T(8,128)}) custom-call(s32[11]{0:T(128)} %concatenate.3.table, bf16[1024,1024]{1,0:T(8,128)(2,1)} %get-tuple-element.237.na, bf16[1024,1024]{1,0:T(8,128)(2,1)} %get-tuple-element.238.gr, ...), custom_call_target="tpu_custom_call" | custom-call | flops 9999999827968 | bytes 1048576 | tf_op jit(solution)/shard_map/attn_unit/pallas_call | solution.py:801
  97.9 3.7 add.91
  102.2 36.7 %mlp_unit.3 = (bf16[4,512,1024]{2,1,0:T(8,128)(2,1)}, bf16[4,512,1024]{2,1,0:T(8,128)(2,1)}, f32[1,2048]{1,0:T(1,128)}, f32[1024,1024]{1,0:T(8,128)}, f32[1024,1024]{1,0:T(8,128)}) custom-call(s32[11]{0:T(128)} %concatenate.3.table, bf16[1024,1024]{1,0:T(8,128)(2,1)} %get-tuple-element.247.nm, ...), custom_call_target="tpu_custom_call", output_to_operand_aliasing={{3}: (5, {})} | custom-call | flops 9999999827968 | bytes 1048576 | tf_op jit(solution)/shard_map/mlp_unit/pallas_call | solution.py:591
  141.5 5.8 %collective-permute-done.11.refs_1_.refs_5_ = bf16[4,512,1024]{2,1,0:T(8,128)(2,1)} collective-permute-done((bf16[4,512,1024]{2,1,0:T(8,128)(2,1)}, bf16[4,512,1024]{2,1,0:T(8,128)(2,1)}, u32[]{:S(2)}, u32[]{:S(2)}) %collective-permute-start.11) | collective-permute-done | bytes 4194336 | tf_op jit(solution)/shard_map/ppermute | solution.py:1000
  147.3 4.3 %add.92 = bf16[2,512,1024]{2,1,0:T(8,128)(2,1)} custom-call(bf16[4,512,1024]{2,1,0:T(8,128)(2,1)} %get-tuple-element.298.refs_0_.refs_4_, bf16[4,512,1024]{2,1,0:T(8,128)(2,1)} %collective-permute-done.11.refs_1_.refs_5_), custom_call_target="tpu_custom_call" | custom-call | flops 9999999827968 | bytes 1048576 | tf_op jit(solution)/shard_map/add/pallas_call | solution.py:935
  153.5 22.9 %mlp_unit.4 = (bf16[4,512,1024]{2,1,0:T(8,128)(2,1)}, bf16[4,512,1024]{2,1,0:T(8,128)(2,1)}, f32[1,1024]{1,0:T(1,128)}, f32[1024,1024]{1,0:T(8,128)}, f32[1024,1024]{1,0:T(8,128)}) custom-call(s32[11]{0:T(128)} %concatenate.3.table, bf16[1024,1024]{1,0:T(8,128)(2,1)} %get-tuple-element.247.nm, ...), custom_call_target="tpu_custom_call", output_to_operand_aliasing={{3}: (5, {}), {4}: (6, {})} | custom-call | flops 9999999827968 | bytes 1048576 | tf_op jit(solution)/shard_map/mlp_unit/pallas_call | solution.py:591
  176.4 6.8 %collective-permute-done.13.refs_6_.refs_2_ = bf16[2,512,1024]{2,1,0:T(8,128)(2,1)} collective-permute-done((bf16[2,512,1024]{2,1,0:T(8,128)(2,1)}, bf16[2,512,1024]{2,1,0:T(8,128)(2,1)}, u32[]{:S(2)}, u32[]{:S(2)}) %collective-permute-start.13) | collective-permute-done | bytes 2097184 | tf_op jit(solution)/shard_map/ppermute | solution.py:1000
  183.2 3.3 sums.12
  188.4 22.6 %mlp_unit.5 = (bf16[4,512,1024]{2,1,0:T(8,128)(2,1)}, bf16[4,512,1024]{2,1,0:T(8,128)(2,1)}, f32[1,1024]{1,0:T(1,128)}, f32[1024,1024]{1,0:T(8,128)}, f32[1024,1024]{1,0:T(8,128)}) custom-call(s32[11]{0:T(128)} %concatenate.3.table, ...), custom_call_target="tpu_custom_call", output_to_operand_aliasing={{0}: (5, {}), {1}: (6, {}), {3}: (7, {}), {4}: (8, {})} | custom-call | flops 9999999827968 | bytes 1048576 | tf_op jit(solution)/shard_map/mlp_unit/pallas_call | solution.py:591
  211.2 3.3 sums.13
  214.5 4.6 %collective-permute-done.16.refs_1_.refs_5_ = bf16[4,512,1024]{2,1,0:T(8,128)(2,1)} collective-permute-done((bf16[4,512,1024]{2,1,0:T(8,128)(2,1)}, bf16[4,512,1024]{2,1,0:T(8,128)(2,1)}, u32[]{:S(2)}, u32[]{:S(2)}) %collective-permute-start.16) | collective-permute-done | bytes 4194336 | tf_op jit(solution)/shard_map/ppermute | solution.py:1000
  219.1 4.4 %add.93 = bf16[2,512,1024]{2,1,0:T(8,128)(2,1)} custom-call(bf16[4,512,1024]{2,1,0:T(8,128)(2,1)} %get-tuple-element.341.refs_0_.refs_4_, bf16[4,512,1024]{2,1,0:T(8,128)(2,1)} %collective-permute-done.16.refs_1_.refs_5_), custom_call_target="tpu_custom_call" | custom-call | flops 9999999827968 | bytes 1048576 | tf_op jit(solution)/shard_map/add/pallas_call | solution.py:935
  227.8 29.1 %attn_unit.4 = (bf16[4,128,2048]{2,1,0:T(8,128)(2,1)}, bf16[4,128,2048]{2,1,0:T(8,128)(2,1)}, f32[1,768]{1,0:T(1,128)}, f32[1024,1024]{1,0:T(8,128)}, f32[1024,1024]{1,0:T(8,128)}) custom-call(s32[11]{0:T(128)} %concatenate.3.table, bf16[1024,1024]{1,0:T(8,128)(2,1)} %get-tuple-element.237.na, ...), custom_call_target="tpu_custom_call", output_to_operand_aliasing={{3}: (8, {}), {4}: (9, {})} | custom-call | flops 9999999827968 | bytes 1048576 | tf_op jit(solution)/shard_map/attn_unit/pallas_call | solution.py:801
  257.0 3.0 sums.14
  263.8 29.8 %attn_unit.5 = (bf16[4,128,2048]{2,1,0:T(8,128)(2,1)}, bf16[4,128,2048]{2,1,0:T(8,128)(2,1)}, f32[1,768]{1,0:T(1,128)}, f32[1024,1024]{1,0:T(8,128)}, f32[1024,1024]{1,0:T(8,128)}) custom-call(s32[11]{0:T(128)} %concatenate.3.table, ...), custom_call_target="tpu_custom_call", output_to_operand_aliasing={{0}: (10, {}), {1}: (11, {}), {3}: (12, {}), {4}: (13, {})} | custom-call | flops 9999999827968 | bytes 1048576 | tf_op jit(solution)/shard_map/attn_unit/pallas_call | solution.py:801
  293.7 3.6 sums.15
  299.8 3.6 add.94
  304.1 9.6 %finish.1 = (f32[1024,1024]{1,0:T(8,128)}, f32[4,3072]{1,0:T(4,128)}) custom-call(s32[11]{0:T(128)} %concatenate.3.table, bf16[1024,1024]{1,0:T(8,128)(2,1)} %x.19, bf16[1024,1024]{1,0:T(8,128)(2,1)} %get-tuple-element.238.gr, f32[1024,1024]{1,0:T(8,128)} %get-tuple-element.355.dna, f32[1024,1024]{1,0:T(8,128)} %get-tuple-element.356.dnm, ...), custom_call_target="tpu_custom_call" | custom-call | flops 9999999827968 | bytes 1048576 | tf_op jit(solution)/shard_map/finish/pallas_call | solution.py:435
  313.7 9.5 %collective-permute-done.26.refs_1_ = bf16[1,256,1024]{2,1,0:T(8,128)(2,1)} collective-permute-done((bf16[1,256,1024]{2,1,0:T(8,128)(2,1)}, bf16[1,256,1024]{2,1,0:T(8,128)(2,1)}, u32[]{:S(2)}, u32[]{:S(2)}) %collective-permute-start.26) | collective-permute-done | bytes 524320 | tf_op jit(solution)/shard_map/ppermute | solution.py:1000
  330.1 4.8 %collective-permute-done.28.refs_3_ = bf16[1,128,2048]{2,1,0:T(8,128)(2,1)S(1)} collective-permute-done((bf16[1,128,2048]{2,1,0:T(8,128)(2,1)S(1)}, bf16[1,128,2048]{2,1,0:T(8,128)(2,1)S(1)}, u32[]{:S(2)}, u32[]{:S(2)}) %collective-permute-start.28) | collective-permute-done | bytes 524320 | tf_op jit(solution)/shard_map/ppermute | solution.py:1000
  341.2 12.1 %collective-permute-done.34.refs_1_ = bf16[1,64,2048]{2,1,0:T(8,128)(2,1)S(1)} collective-permute-done((bf16[1,64,2048]{2,1,0:T(8,128)(2,1)S(1)}, bf16[1,64,2048]{2,1,0:T(8,128)(2,1)S(1)}, u32[]{:S(2)}, u32[]{:S(2)}) %collective-permute-start.34) | collective-permute-done | bytes 262176 | tf_op jit(solution)/shard_map/ppermute | solution.py:1000
  354.9 2.9 collective-permute-start.37
  359.0 2.9 collective-permute-done.36
  361.9 10.7 %collective-permute-done.37.refs_1_ = bf16[1,64,2048]{2,1,0:T(8,128)(2,1)S(1)} collective-permute-done((bf16[1,64,2048]{2,1,0:T(8,128)(2,1)S(1)}, bf16[1,64,2048]{2,1,0:T(8,128)(2,1)S(1)}, u32[]{:S(2)}, u32[]{:S(2)}) %collective-permute-start.37) | collective-permute-done | bytes 262176 | tf_op jit(solution)/shard_map/ppermute | solution.py:1000
  379.7 6.2 %mlp_place.1 = (f32[256,4096]{1,0:T(8,128)}, f32[1024,1024]{1,0:T(8,128)}) custom-call(s32[11]{0:T(128)} %concatenate.3.table, bf16[1,256,1024]{2,1,0:T(8,128)(2,1)} %get-tuple-element.389.refs_0_, bf16[1,256,1024]{2,1,0:T(8,128)(2,1)} %collective-permute-done.30.refs_1_, bf16[1,256,1024]{2,1,0:T(8,128)(2,1)} %collective-permute-done.31.refs_2_, ...), custom_call_target="tpu_custom_call" | custom-call | tf_op jit(solution)/shard_map/mlp_place/pallas_call | solution.py:914
  388.8 3.9 attn_place.1
  (177 shorter events, 63.4 us)
Async XLA Ops:
  7.2 95.1 %all-gather.6.cloned.1.call-start = ((), (), s32[]{:S(2)}) async-start(), calls=%async_computation.1 | async-start | bytes 9437184 | tf_op jit(solution)/shard_map/all_gather | solution.py:1030
  13.3 20.2 %collective-permute-start.4 = (bf16[26,128]{1,0:T(8,128)(2,1)}, bf16[26,128]{1,0:T(8,128)(2,1)}, u32[]{:S(2)}, u32[]{:S(2)}) collective-permute-start(bf16[26,128]{1,0:T(8,128)(2,1)} %pad_add_fusion.refs_0_), channel_id=1, source_target_pairs={{0,3},{1,2},{2,1},{3,0},{4,7},{5,6},{6,5},{7,4},{8,11},{9,10},{10,... | collective-permute-start | bytes 19976 | tf_op jit(solution)/shard_map/ppermute | solution.py:1000
  17.1 16.4 %collective-permute-start.3 = (bf16[26,128]{1,0:T(8,128)(2,1)}, bf16[26,128]{1,0:T(8,128)(2,1)}, u32[]{:S(2)}, u32[]{:S(2)}) collective-permute-start(bf16[26,128]{1,0:T(8,128)(2,1)} %pad_add_fusion.refs_0_), channel_id=1, source_target_pairs={{0,2},{1,3},{2,0},{3,1},{4,6},{5,7},{6,4},{7,5},{8,10},{9,11},{10,... | collective-permute-start | bytes 19976 | tf_op jit(solution)/shard_map/ppermute | solution.py:1000
  17.7 15.9 %collective-permute-start.2 = (bf16[26,128]{1,0:T(8,128)(2,1)}, bf16[26,128]{1,0:T(8,128)(2,1)}, u32[]{:S(2)}, u32[]{:S(2)}) collective-permute-start(bf16[26,128]{1,0:T(8,128)(2,1)} %pad_add_fusion.refs_0_), channel_id=1, source_target_pairs={{0,1},{1,0},{2,3},{3,2},{4,5},{5,4},{6,7},{7,6},{8,9},{9,8},{10,11... | collective-permute-start | bytes 19976 | tf_op jit(solution)/shard_map/ppermute | solution.py:1000
  17.7 14.3 %collective-permute-start.1 = (bf16[1,128,2048]{2,1,0:T(8,128)(2,1)}, bf16[1,128,2048]{2,1,0:T(8,128)(2,1)}, u32[]{:S(2)}, u32[]{:S(2)}) collective-permute-start(bf16[1,128,2048]{2,1,0:T(8,128)(2,1)} %get-tuple-element.240.refs_0_), channel_id=1, source_target_pairs={{0,2},{1,3},{2,0},{3,1},{4,5},{5,4},{6,7},{7,6},{8,10},{9,11},{10,... | collective-permute-start | bytes 1572872 | tf_op jit(solution)/shard_map/ppermute | solution.py:1000
  19.7 12.3 %collective-permute-start = (bf16[1,128,2048]{2,1,0:T(8,128)(2,1)}, bf16[1,128,2048]{2,1,0:T(8,128)(2,1)}, u32[]{:S(2)}, u32[]{:S(2)}) collective-permute-start(bf16[1,128,2048]{2,1,0:T(8,128)(2,1)} %get-tuple-element.240.refs_0_), channel_id=1, source_target_pairs={{0,1},{1,0},{2,3},{3,2},{4,6},{5,7},{6,4},{7,5},{8,9},{9,8},{10,11... | collective-permute-start | bytes 1572872 | tf_op jit(solution)/shard_map/ppermute | solution.py:1000
  32.0 10.4 %collective-permute-start.6 = (bf16[1,128,2048]{2,1,0:T(8,128)(2,1)}, bf16[1,128,2048]{2,1,0:T(8,128)(2,1)}, u32[]{:S(2)}, u32[]{:S(2)}) collective-permute-start(bf16[1,128,2048]{2,1,0:T(8,128)(2,1)} %collective-permute-done.refs_2_), channel_id=1, source_target_pairs={{0,4},{1,5},{2,6},{3,7},{4,0},{5,1},{6,2},{7,3},{8,12},{9,13},{10,... | collective-permute-start | bytes 1572872 | tf_op jit(solution)/shard_map/ppermute | solution.py:1000
  33.4 120.0 %all-gather.4.cloned.1.call-start = ((), (), s32[]{:S(2)}) async-start(), calls=%async_computation | async-start | bytes 9437184 | tf_op jit(solution)/shard_map/all_gather | solution.py:1030
  42.1 185.7 %all-gather.8.cloned.1.call-start = ((), (), s32[]{:S(2)}) async-start(), calls=%async_computation.2 | async-start | bytes 4718592 | tf_op jit(solution)/shard_map/all_gather | solution.py:1030
  101.6 37.4 %collective-permute-start.10 = (bf16[2,128,2048]{2,1,0:T(8,128)(2,1)}, bf16[2,128,2048]{2,1,0:T(8,128)(2,1)}, u32[]{:S(2)}, u32[]{:S(2)}) collective-permute-start(bf16[2,128,2048]{2,1,0:T(8,128)(2,1)} %add.91), channel_id=1, source_target_pairs={{0,1},{1,0},{2,3},{3,2},{4,6},{5,7},{6,4},{7,5},{8,9},{9,8},{10,11... | collective-permute-start | bytes 3145736 | tf_op jit(solution)/shard_map/ppermute | solution.py:1000
  151.6 24.7 %collective-permute-start.12 = (bf16[1,128,2048]{2,1,0:T(8,128)(2,1)}, bf16[1,128,2048]{2,1,0:T(8,128)(2,1)}, u32[]{:S(2)}, u32[]{:S(2)}) collective-permute-start(bf16[1,128,2048]{2,1,0:T(8,128)(2,1)} %sums.11), channel_id=1, source_target_pairs={{0,2},{1,3},{2,0},{3,1},{4,5},{5,4},{6,7},{7,6},{8,10},{9,11},{10,... | collective-permute-start | bytes 1572872 | tf_op jit(solution)/shard_map/ppermute | solution.py:1000
  152.3 30.8 %collective-permute-start.13 = (bf16[2,512,1024]{2,1,0:T(8,128)(2,1)}, bf16[2,512,1024]{2,1,0:T(8,128)(2,1)}, u32[]{:S(2)}, u32[]{:S(2)}) collective-permute-start(bf16[2,512,1024]{2,1,0:T(8,128)(2,1)} %add.92), channel_id=1, source_target_pairs={{0,1},{1,0},{2,3},{3,2},{4,6},{5,7},{6,4},{7,5},{8,9},{9,8},{10,11... | collective-permute-start | bytes 6291464 | tf_op jit(solution)/shard_map/ppermute | solution.py:1000
  186.4 24.7 %collective-permute-start.14 = (bf16[1,64,2048]{2,1,0:T(8,128)(2,1)}, bf16[1,64,2048]{2,1,0:T(8,128)(2,1)}, u32[]{:S(2)}, u32[]{:S(2)}) collective-permute-start(bf16[1,64,2048]{2,1,0:T(8,128)(2,1)} %get-tuple-element.295), channel_id=1, source_target_pairs={{0,8},{1,9},{2,10},{3,11},{4,12},{5,13},{6,14},{7,15},{8,0},{9,1},... | collective-permute-start | bytes 786440 | tf_op jit(solution)/shard_map/ppermute | solution.py:1000
  187.4 23.7 %collective-permute-start.15 = (bf16[1,512,1024]{2,1,0:T(8,128)(2,1)}, bf16[1,512,1024]{2,1,0:T(8,128)(2,1)}, u32[]{:S(2)}, u32[]{:S(2)}) collective-permute-start(bf16[1,512,1024]{2,1,0:T(8,128)(2,1)} %get-tuple-element.296), channel_id=1, source_target_pairs={{0,2},{1,3},{2,0},{3,1},{4,5},{5,4},{6,7},{7,6},{8,10},{9,11},{10,... | collective-permute-start | bytes 3145736 | tf_op jit(solution)/shard_map/ppermute | solution.py:1000
  223.5 33.4 %collective-permute-start.17 = (bf16[1,64,2048]{2,1,0:T(8,128)(2,1)}, bf16[1,64,2048]{2,1,0:T(8,128)(2,1)}, u32[]{:S(2)}, u32[]{:S(2)}) collective-permute-start(bf16[1,64,2048]{2,1,0:T(8,128)(2,1)} %get-tuple-element.324.refs_0_), channel_id=1, source_target_pairs={{0,16},{1,17},{2,18},{3,19},{4,20},{5,21},{6,22},{7,23},{8,24},{9,... | collective-permute-start | bytes 786440 | tf_op jit(solution)/shard_map/ppermute | solution.py:1000
  226.2 30.7 %collective-permute-start.18 = (bf16[1,256,1024]{2,1,0:T(8,128)(2,1)}, bf16[1,256,1024]{2,1,0:T(8,128)(2,1)}, u32[]{:S(2)}, u32[]{:S(2)}) collective-permute-start(bf16[1,256,1024]{2,1,0:T(8,128)(2,1)} %get-tuple-element.321), channel_id=1, source_target_pairs={{0,8},{1,9},{2,10},{3,11},{4,12},{5,13},{6,14},{7,15},{8,0},{9,1},... | collective-permute-start | bytes 1572872 | tf_op jit(solution)/shard_map/ppermute | solution.py:1000
  227.8 29.1 %collective-permute-start.19 = (bf16[2,512,1024]{2,1,0:T(8,128)(2,1)}, bf16[2,512,1024]{2,1,0:T(8,128)(2,1)}, u32[]{:S(2)}, u32[]{:S(2)}) collective-permute-start(bf16[2,512,1024]{2,1,0:T(8,128)(2,1)} %add.93), channel_id=1, source_target_pairs={{0,1},{1,0},{2,3},{3,2},{4,6},{5,7},{6,4},{7,5},{8,9},{9,8},{10,11... | collective-permute-start | bytes 6291464 | tf_op jit(solution)/shard_map/ppermute | solution.py:1000
  259.9 33.7 %collective-permute-start.23 = (bf16[1,64,2048]{2,1,0:T(8,128)(2,1)}, bf16[1,64,2048]{2,1,0:T(8,128)(2,1)}, u32[]{:S(2)}, u32[]{:S(2)}) collective-permute-start(bf16[1,64,2048]{2,1,0:T(8,128)(2,1)} %get-tuple-element.364.refs_0_), channel_id=1, source_target_pairs={{0,4},{1,5},{2,6},{3,7},{4,0},{5,1},{6,2},{7,3},{8,12},{9,13},{10,... | collective-permute-start | bytes 786440 | tf_op jit(solution)/shard_map/ppermute | solution.py:1000
  259.9 33.7 %collective-permute-start.22 = (bf16[1,64,2048]{2,1,0:T(8,128)(2,1)}, bf16[1,64,2048]{2,1,0:T(8,128)(2,1)}, u32[]{:S(2)}, u32[]{:S(2)}) collective-permute-start(bf16[1,64,2048]{2,1,0:T(8,128)(2,1)} %get-tuple-element.364.refs_0_), channel_id=1, source_target_pairs={{0,8},{1,9},{2,10},{3,11},{4,12},{5,13},{6,14},{7,15},{8,0},{9,1},... | collective-permute-start | bytes 786440 | tf_op jit(solution)/shard_map/ppermute | solution.py:1000
  261.9 31.8 %collective-permute-start.21 = (bf16[1,256,1024]{2,1,0:T(8,128)(2,1)}, bf16[1,256,1024]{2,1,0:T(8,128)(2,1)}, u32[]{:S(2)}, u32[]{:S(2)}) collective-permute-start(bf16[1,256,1024]{2,1,0:T(8,128)(2,1)} %get-tuple-element.345.refs_4_), channel_id=1, source_target_pairs={{0,16},{1,17},{2,18},{3,19},{4,20},{5,21},{6,22},{7,23},{8,24},{9,... | collective-permute-start | bytes 1572872 | tf_op jit(solution)/shard_map/ppermute | solution.py:1000
  262.4 31.2 %collective-permute-start.20 = (bf16[1,512,1024]{2,1,0:T(8,128)(2,1)}, bf16[1,512,1024]{2,1,0:T(8,128)(2,1)}, u32[]{:S(2)}, u32[]{:S(2)}) collective-permute-start(bf16[1,512,1024]{2,1,0:T(8,128)(2,1)} %get-tuple-element.337), channel_id=1, source_target_pairs={{0,2},{1,3},{2,0},{3,1},{4,5},{5,4},{6,7},{7,6},{8,10},{9,11},{10,... | collective-permute-start | bytes 3145736 | tf_op jit(solution)/shard_map/ppermute | solution.py:1000
  297.3 31.6 %collective-permute-start.31 = (bf16[1,256,1024]{2,1,0:T(8,128)(2,1)}, bf16[1,256,1024]{2,1,0:T(8,128)(2,1)}, u32[]{:S(2)}, u32[]{:S(2)}) collective-permute-start(bf16[1,256,1024]{2,1,0:T(8,128)(2,1)} %get-tuple-element.389.refs_0_), channel_id=1, source_target_pairs={{0,4},{1,5},{2,6},{3,7},{4,0},{5,1},{6,2},{7,3},{8,12},{9,13},{10,... | collective-permute-start | bytes 1572872 | tf_op jit(solution)/shard_map/ppermute | solution.py:1000
  297.8 31.1 %collective-permute-start.30 = (bf16[1,256,1024]{2,1,0:T(8,128)(2,1)}, bf16[1,256,1024]{2,1,0:T(8,128)(2,1)}, u32[]{:S(2)}, u32[]{:S(2)}) collective-permute-start(bf16[1,256,1024]{2,1,0:T(8,128)(2,1)} %get-tuple-element.389.refs_0_), channel_id=1, source_target_pairs={{0,8},{1,9},{2,10},{3,11},{4,12},{5,13},{6,14},{7,15},{8,0},{9,1},... | collective-permute-start | bytes 1572872 | tf_op jit(solution)/shard_map/ppermute | solution.py:1000
  298.3 24.9 %collective-permute-start.26 = (bf16[1,256,1024]{2,1,0:T(8,128)(2,1)}, bf16[1,256,1024]{2,1,0:T(8,128)(2,1)}, u32[]{:S(2)}, u32[]{:S(2)}) collective-permute-start(bf16[1,256,1024]{2,1,0:T(8,128)(2,1)} %get-tuple-element.369), channel_id=1, source_target_pairs={{0,8},{1,9},{2,10},{3,11},{4,12},{5,13},{6,14},{7,15},{8,0},{9,1},... | collective-permute-start | bytes 1572872 | tf_op jit(solution)/shard_map/ppermute | solution.py:1000
  303.4 20.9 %collective-permute-start.27 = (bf16[2,128,2048]{2,1,0:T(8,128)(2,1)}, bf16[2,128,2048]{2,1,0:T(8,128)(2,1)}, u32[]{:S(2)}, u32[]{:S(2)}) collective-permute-start(bf16[2,128,2048]{2,1,0:T(8,128)(2,1)} %add.94), channel_id=1, source_target_pairs={{0,1},{1,0},{2,3},{3,2},{4,6},{5,7},{6,4},{7,5},{8,9},{9,8},{10,11... | collective-permute-start | bytes 3145736 | tf_op jit(solution)/shard_map/ppermute | solution.py:1000
  326.5 27.6 %collective-permute-start.35 = (bf16[1,256,1024]{2,1,0:T(8,128)(2,1)S(1)}, bf16[1,256,1024]{2,1,0:T(8,128)(2,1)S(1)}, u32[]{:S(2)}, u32[]{:S(2)}) collective-permute-start(bf16[1,256,1024]{2,1,0:T(8,128)(2,1)S(1)} %sums.16.refs_0_), channel_id=1, source_target_pairs={{0,16},{1,17},{2,18},{3,19},{4,20},{5,21},{6,22},{7,23},{8,24},{9,... | collective-permute-start | bytes 1572872 | tf_op jit(solution)/shard_map/ppermute | solution.py:1000
  336.5 16.8 %collective-permute-start.34 = (bf16[1,64,2048]{2,1,0:T(8,128)(2,1)S(1)}, bf16[1,64,2048]{2,1,0:T(8,128)(2,1)S(1)}, u32[]{:S(2)}, u32[]{:S(2)}) collective-permute-start(bf16[1,64,2048]{2,1,0:T(8,128)(2,1)S(1)} %get-tuple-element.394), channel_id=1, source_target_pairs={{0,8},{1,9},{2,10},{3,11},{4,12},{5,13},{6,14},{7,15},{8,0},{9,1},... | collective-permute-start | bytes 786440 | tf_op jit(solution)/shard_map/ppermute | solution.py:1000
  354.8 17.8 %collective-permute-start.39 = (bf16[1,256,1024]{2,1,0:T(8,128)(2,1)S(1)}, bf16[1,256,1024]{2,1,0:T(8,128)(2,1)S(1)}, u32[]{:S(2)}, u32[]{:S(2)}) collective-permute-start(bf16[1,256,1024]{2,1,0:T(8,128)(2,1)S(1)} %sums.20.refs_4_), channel_id=1, source_target_pairs={{0,4},{1,5},{2,6},{3,7},{4,0},{5,1},{6,2},{7,3},{8,12},{9,13},{10,... | collective-permute-start | bytes 1572872 | tf_op jit(solution)/shard_map/ppermute | solution.py:1000
  354.9 20.0 %collective-permute-start.38 = (bf16[1,256,1024]{2,1,0:T(8,128)(2,1)S(1)}, bf16[1,256,1024]{2,1,0:T(8,128)(2,1)S(1)}, u32[]{:S(2)}, u32[]{:S(2)}) collective-permute-start(bf16[1,256,1024]{2,1,0:T(8,128)(2,1)S(1)} %sums.20.refs_4_), channel_id=1, source_target_pairs={{0,8},{1,9},{2,10},{3,11},{4,12},{5,13},{6,14},{7,15},{8,0},{9,1},... | collective-permute-start | bytes 1572872 | tf_op jit(solution)/shard_map/ppermute | solution.py:1000
  354.9 17.7 %collective-permute-start.37 = (bf16[1,64,2048]{2,1,0:T(8,128)(2,1)S(1)}, bf16[1,64,2048]{2,1,0:T(8,128)(2,1)S(1)}, u32[]{:S(2)}, u32[]{:S(2)}) collective-permute-start(bf16[1,64,2048]{2,1,0:T(8,128)(2,1)S(1)} %sums.19.refs_0_), channel_id=1, source_target_pairs={{0,16},{1,17},{2,18},{3,19},{4,20},{5,21},{6,22},{7,23},{8,24},{9,... | collective-permute-start | bytes 786440 | tf_op jit(solution)/shard_map/ppermute | solution.py:1000
  359.0 19.1 %collective-permute-start.32 = (bf16[1,256,1024]{2,1,0:T(8,128)(2,1)}, bf16[1,256,1024]{2,1,0:T(8,128)(2,1)S(1)}, u32[]{:S(2)}, u32[]{:S(2)}) collective-permute-start(bf16[1,256,1024]{2,1,0:T(8,128)(2,1)} %collective-permute-done.30.refs_1_), channel_id=1, source_target_pairs={{0,4},{1,5},{2,6},{3,7},{4,0},{5,1},{6,2},{7,3},{8,12},{9,13},{10,... | collective-permute-start | bytes 1572872 | tf_op jit(solution)/shard_map/ppermute | solution.py:1000
  375.5 10.4 %collective-permute-start.43 = (bf16[1,64,2048]{2,1,0:T(8,128)(2,1)S(1)}, bf16[1,64,2048]{2,1,0:T(8,128)(2,1)S(1)}, u32[]{:S(2)}, u32[]{:S(2)}) collective-permute-start(bf16[1,64,2048]{2,1,0:T(8,128)(2,1)S(1)} %sums.21.refs_4_), channel_id=1, source_target_pairs={{0,4},{1,5},{2,6},{3,7},{4,0},{5,1},{6,2},{7,3},{8,12},{9,13},{10,... | collective-permute-start | bytes 786440 | tf_op jit(solution)/shard_map/ppermute | solution.py:1000
  (50 other events, 524.7 us)
Sparse Core Ops, SparseCore 0:
  33.6 54.5 all-gather.5
  90.6 58.9 all-gather.3
  186.6 39.5 all-gather.7

commit v5 on v4

--- a/solution.py
+++ b/solution.py
@@ -529,8 +529,8 @@
     slot = step % 2
 
     bias_sum = jnp.zeros(gbi.shape, F32)
-    for t in range(T // ROWS):
-        r = rows_of(t, ROWS)
+    for t in range(T // WIDE):
+        r = rows_of(t, WIDE)
         inner = nn(nm[r, :], wi[slot]) + bi[...]
         grad = nt(gr[r, :], wo[slot])
         normal = 0.5 * lax.erf(inner * 0.7071067811865476) + 0.5
@@ -545,8 +545,8 @@
     def _():
         totals.ready()
 
-    for t in range(T // ROWS):
-        r = rows_of(t, ROWS)
+    for t in range(T // WIDE):
+        r = rows_of(t, WIDE)
         out[r, :] += nn(act[r, :], wo[slot])
         dn[r, :] += nt(ig[r, :], wi[slot])
 
@@ -731,7 +731,7 @@
                 dv[h, :, c] += nn(grad_turned, e)
         return carry
 
-    lax.fori_loop(0, HEADS, head, 0)
+    lax.fori_loop(0, HEADS // 2, lambda p, carry: head(2 * p + 1, head(2 * p, carry)), 0)
 
     @pl.when(step == 0)
     def _():

time: 405 us -> 406 us (level)
  transfers between devices with their start and end apart: 49 -> 49, of which waited for: 15 -> 16; matrix products, arithmetic and copies ran while one was open for 0% -> 0% of each run, Pallas kernels for 64% -> 63%
where the time goes in v5:
time: 406 us; the launch traced here: 402 us
  Pallas kernels  265 us (65%)
  waiting for transfers between devices  73.9 us (18%)
  starting transfers between devices  40 us (10%)
  between operations  15.3 us (4%)
  local copies, waits for them, and re-layouts  6.65 us (2%)
    pallas_call x3, Pallas kernels, attn_unit(): pl.pallas_call(functools.partial(attn_unit_kernel, first, count, given, a...  107 us
    pallas_call x3, Pallas kernels, mlp_unit(): pl.pallas_call(functools.partial(mlp_unit_kernel, first, count, given), g...  80.7 us
    ppermute x46, waiting for transfers between devices, exchange(): return lax.ppermute(value, AXES, pairs)  73.8 us
    ppermute x46, starting transfers between devices, exchange(): return lax.ppermute(value, AXES, pairs)  39.9 us
    pallas_call x11, Pallas kernels, sums(): pl.pallas_call(functools.partial(sums_kernel, plan), grid=(2,), in_specs=...  21.6 us
    pallas_call x4, Pallas kernels, add(): pl.pallas_call(add_kernel, grid=(count * steps,), in_specs=[read(first, s...  16.1 us
    pallas_call x4, Pallas kernels, pack(): pl.pallas_call(kernel, in_specs=[pl.BlockSpec(memory_space=pltpu.SMEM)] +...  12 us
    pallas_call x2, Pallas kernels, place(): pl.pallas_call(kernel, in_specs=[pl.BlockSpec(memory_space=pltpu.SMEM)] +...  10.1 us
  transfers between devices with their start and end apart: 49, of which 16 were waited for; matrix products, arithmetic and copies ran while one was open for 0% of the time, Pallas kernels for 63%

profile of v5, /device:TPU:0, one launch (start us, length us, event | category | flops | bytes accessed | tf_op | source)
XLA Modules:
  0.0 402.3 jit_solution(16580414091998610453)
XLA Ops:
  9.2 3.3 attn_pack.2
  13.3 3.9 collective-permute-start.4
  21.2 3.0 mlp_pack.3
  24.2 3.0 mlp_pack.2
  27.2 4.8 %collective-permute-done.1.refs_1_ = bf16[1,128,2048]{2,1,0:T(8,128)(2,1)} collective-permute-done((bf16[1,128,2048]{2,1,0:T(8,128)(2,1)}, bf16[1,128,2048]{2,1,0:T(8,128)(2,1)}, u32[]{:S(2)}, u32[]{:S(2)}) %collective-permute-start.1) | collective-permute-done | bytes 524320 | tf_op jit(solution)/shard_map/ppermute | solution.py:1000
  35.2 6.4 %norm.1 = (bf16[1024,1024]{1,0:T(8,128)(2,1)}, bf16[1024,1024]{1,0:T(8,128)(2,1)}, bf16[1024,1024]{1,0:T(8,128)(2,1)}) custom-call(s32[11]{0:T(128)} %concatenate.3.table, bf16[1024,1024]{1,0:T(8,128)(2,1)} %x.19, bf16[1024,1024]{1,0:T(8,128)(2,1)} %grad.1, f32[1,1024]{1,0:T(1,128)} %get-tuple-element.231.gain_a, f32[1,1024]{1,0:T(1,128)} %get-tuple-element.232.shift_a, ...), custom_call_target="tpu_custom_call" | custom-call | flops 9999999827968 | bytes 1048576 | tf_op jit(solution)/shard_map/norm/pallas_call | solution.py:379
  44.6 48.7 %attn_unit.3 = (bf16[4,128,2048]{2,1,0:T(8,128)(2,1)}, bf16[4,128,2048]{2,1,0:T(8,128)(2,1)}, f32[1,1536]{1,0:T(1,128)}, f32[1024,1024]{1,0:T(8,128)}, f32[1024,1024]{1,0:T(8,128)}) custom-call(s32[11]{0:T(128)} %concatenate.3.table, bf16[1024,1024]{1,0:T(8,128)(2,1)} %get-tuple-element.237.na, bf16[1024,1024]{1,0:T(8,128)(2,1)} %get-tuple-element.238.gr, ...), custom_call_target="tpu_custom_call" | custom-call | flops 9999999827968 | bytes 1048576 | tf_op jit(solution)/shard_map/attn_unit/pallas_call | solution.py:801
  97.9 3.7 add.91
  102.3 35.9 %mlp_unit.3 = (bf16[4,512,1024]{2,1,0:T(8,128)(2,1)}, bf16[4,512,1024]{2,1,0:T(8,128)(2,1)}, f32[1,2048]{1,0:T(1,128)}, f32[1024,1024]{1,0:T(8,128)}, f32[1024,1024]{1,0:T(8,128)}) custom-call(s32[11]{0:T(128)} %concatenate.3.table, bf16[1024,1024]{1,0:T(8,128)(2,1)} %get-tuple-element.247.nm, ...), custom_call_target="tpu_custom_call", output_to_operand_aliasing={{3}: (5, {})} | custom-call | flops 9999999827968 | bytes 1048576 | tf_op jit(solution)/shard_map/mlp_unit/pallas_call | solution.py:591
  140.7 5.1 %collective-permute-done.11.refs_1_.refs_5_ = bf16[4,512,1024]{2,1,0:T(8,128)(2,1)} collective-permute-done((bf16[4,512,1024]{2,1,0:T(8,128)(2,1)}, bf16[4,512,1024]{2,1,0:T(8,128)(2,1)}, u32[]{:S(2)}, u32[]{:S(2)}) %collective-permute-start.11) | collective-permute-done | bytes 4194336 | tf_op jit(solution)/shard_map/ppermute | solution.py:1000
  145.8 4.4 %add.92 = bf16[2,512,1024]{2,1,0:T(8,128)(2,1)} custom-call(bf16[4,512,1024]{2,1,0:T(8,128)(2,1)} %get-tuple-element.298.refs_0_.refs_4_, bf16[4,512,1024]{2,1,0:T(8,128)(2,1)} %collective-permute-done.11.refs_1_.refs_5_), custom_call_target="tpu_custom_call" | custom-call | flops 9999999827968 | bytes 1048576 | tf_op jit(solution)/shard_map/add/pallas_call | solution.py:935
  152.8 22.5 %mlp_unit.4 = (bf16[4,512,1024]{2,1,0:T(8,128)(2,1)}, bf16[4,512,1024]{2,1,0:T(8,128)(2,1)}, f32[1,1024]{1,0:T(1,128)}, f32[1024,1024]{1,0:T(8,128)}, f32[1024,1024]{1,0:T(8,128)}) custom-call(s32[11]{0:T(128)} %concatenate.3.table, bf16[1024,1024]{1,0:T(8,128)(2,1)} %get-tuple-element.247.nm, ...), custom_call_target="tpu_custom_call", output_to_operand_aliasing={{3}: (5, {}), {4}: (6, {})} | custom-call | flops 9999999827968 | bytes 1048576 | tf_op jit(solution)/shard_map/mlp_unit/pallas_call | solution.py:591
  175.4 6.1 %collective-permute-done.13.refs_6_.refs_2_ = bf16[2,512,1024]{2,1,0:T(8,128)(2,1)} collective-permute-done((bf16[2,512,1024]{2,1,0:T(8,128)(2,1)}, bf16[2,512,1024]{2,1,0:T(8,128)(2,1)}, u32[]{:S(2)}, u32[]{:S(2)}) %collective-permute-start.13) | collective-permute-done | bytes 2097184 | tf_op jit(solution)/shard_map/ppermute | solution.py:1000
  181.5 3.3 sums.12
  188.3 22.3 %mlp_unit.5 = (bf16[4,512,1024]{2,1,0:T(8,128)(2,1)}, bf16[4,512,1024]{2,1,0:T(8,128)(2,1)}, f32[1,1024]{1,0:T(1,128)}, f32[1024,1024]{1,0:T(8,128)}, f32[1024,1024]{1,0:T(8,128)}) custom-call(s32[11]{0:T(128)} %concatenate.3.table, ...), custom_call_target="tpu_custom_call", output_to_operand_aliasing={{0}: (5, {}), {1}: (6, {}), {3}: (7, {}), {4}: (8, {})} | custom-call | flops 9999999827968 | bytes 1048576 | tf_op jit(solution)/shard_map/mlp_unit/pallas_call | solution.py:591
  210.8 3.3 sums.13
  214.1 4.4 %collective-permute-done.16.refs_1_.refs_5_ = bf16[4,512,1024]{2,1,0:T(8,128)(2,1)} collective-permute-done((bf16[4,512,1024]{2,1,0:T(8,128)(2,1)}, bf16[4,512,1024]{2,1,0:T(8,128)(2,1)}, u32[]{:S(2)}, u32[]{:S(2)}) %collective-permute-start.16) | collective-permute-done | bytes 4194336 | tf_op jit(solution)/shard_map/ppermute | solution.py:1000
  218.5 4.4 %add.93 = bf16[2,512,1024]{2,1,0:T(8,128)(2,1)} custom-call(bf16[4,512,1024]{2,1,0:T(8,128)(2,1)} %get-tuple-element.341.refs_0_.refs_4_, bf16[4,512,1024]{2,1,0:T(8,128)(2,1)} %collective-permute-done.16.refs_1_.refs_5_), custom_call_target="tpu_custom_call" | custom-call | flops 9999999827968 | bytes 1048576 | tf_op jit(solution)/shard_map/add/pallas_call | solution.py:935
  227.1 28.9 %attn_unit.4 = (bf16[4,128,2048]{2,1,0:T(8,128)(2,1)}, bf16[4,128,2048]{2,1,0:T(8,128)(2,1)}, f32[1,768]{1,0:T(1,128)}, f32[1024,1024]{1,0:T(8,128)}, f32[1024,1024]{1,0:T(8,128)}) custom-call(s32[11]{0:T(128)} %concatenate.3.table, bf16[1024,1024]{1,0:T(8,128)(2,1)} %get-tuple-element.237.na, ...), custom_call_target="tpu_custom_call", output_to_operand_aliasing={{3}: (8, {}), {4}: (9, {})} | custom-call | flops 9999999827968 | bytes 1048576 | tf_op jit(solution)/shard_map/attn_unit/pallas_call | solution.py:801
  256.0 3.3 sums.14
  263.6 29.5 %attn_unit.5 = (bf16[4,128,2048]{2,1,0:T(8,128)(2,1)}, bf16[4,128,2048]{2,1,0:T(8,128)(2,1)}, f32[1,768]{1,0:T(1,128)}, f32[1024,1024]{1,0:T(8,128)}, f32[1024,1024]{1,0:T(8,128)}) custom-call(s32[11]{0:T(128)} %concatenate.3.table, ...), custom_call_target="tpu_custom_call", output_to_operand_aliasing={{0}: (10, {}), {1}: (11, {}), {3}: (12, {}), {4}: (13, {})} | custom-call | flops 9999999827968 | bytes 1048576 | tf_op jit(solution)/shard_map/attn_unit/pallas_call | solution.py:801
  293.3 3.6 sums.15
  299.3 3.6 add.94
  303.4 9.6 %finish.1 = (f32[1024,1024]{1,0:T(8,128)}, f32[4,3072]{1,0:T(4,128)}) custom-call(s32[11]{0:T(128)} %concatenate.3.table, bf16[1024,1024]{1,0:T(8,128)(2,1)} %x.19, bf16[1024,1024]{1,0:T(8,128)(2,1)} %get-tuple-element.238.gr, f32[1024,1024]{1,0:T(8,128)} %get-tuple-element.355.dna, f32[1024,1024]{1,0:T(8,128)} %get-tuple-element.356.dnm, ...), custom_call_target="tpu_custom_call" | custom-call | flops 9999999827968 | bytes 1048576 | tf_op jit(solution)/shard_map/finish/pallas_call | solution.py:435
  313.1 9.7 %collective-permute-done.26.refs_1_ = bf16[1,256,1024]{2,1,0:T(8,128)(2,1)} collective-permute-done((bf16[1,256,1024]{2,1,0:T(8,128)(2,1)}, bf16[1,256,1024]{2,1,0:T(8,128)(2,1)}, u32[]{:S(2)}, u32[]{:S(2)}) %collective-permute-start.26) | collective-permute-done | bytes 524320 | tf_op jit(solution)/shard_map/ppermute | solution.py:1000
  329.4 5.1 %collective-permute-done.28.refs_3_ = bf16[1,128,2048]{2,1,0:T(8,128)(2,1)S(1)} collective-permute-done((bf16[1,128,2048]{2,1,0:T(8,128)(2,1)S(1)}, bf16[1,128,2048]{2,1,0:T(8,128)(2,1)S(1)}, u32[]{:S(2)}, u32[]{:S(2)}) %collective-permute-start.28) | collective-permute-done | bytes 524320 | tf_op jit(solution)/shard_map/ppermute | solution.py:1000
  337.1 3.4 collective-permute-done.33
  340.5 13.3 %collective-permute-done.34.refs_1_ = bf16[1,64,2048]{2,1,0:T(8,128)(2,1)S(1)} collective-permute-done((bf16[1,64,2048]{2,1,0:T(8,128)(2,1)S(1)}, bf16[1,64,2048]{2,1,0:T(8,128)(2,1)S(1)}, u32[]{:S(2)}, u32[]{:S(2)}) %collective-permute-start.34) | collective-permute-done | bytes 262176 | tf_op jit(solution)/shard_map/ppermute | solution.py:1000
  358.2 3.2 collective-permute-done.36
  361.3 11.8 %collective-permute-done.37.refs_1_ = bf16[1,64,2048]{2,1,0:T(8,128)(2,1)S(1)} collective-permute-done((bf16[1,64,2048]{2,1,0:T(8,128)(2,1)S(1)}, bf16[1,64,2048]{2,1,0:T(8,128)(2,1)S(1)}, u32[]{:S(2)}, u32[]{:S(2)}) %collective-permute-start.37) | collective-permute-done | bytes 262176 | tf_op jit(solution)/shard_map/ppermute | solution.py:1000
  380.2 6.2 %mlp_place.1 = (f32[256,4096]{1,0:T(8,128)}, f32[1024,1024]{1,0:T(8,128)}) custom-call(s32[11]{0:T(128)} %concatenate.3.table, bf16[1,256,1024]{2,1,0:T(8,128)(2,1)} %get-tuple-element.389.refs_0_, bf16[1,256,1024]{2,1,0:T(8,128)(2,1)} %collective-permute-done.30.refs_1_, bf16[1,256,1024]{2,1,0:T(8,128)(2,1)} %collective-permute-done.31.refs_2_, ...), custom_call_target="tpu_custom_call" | custom-call | tf_op jit(solution)/shard_map/mlp_place/pallas_call | solution.py:914
  389.3 3.9 attn_place.1
  (177 shorter events, 63.4 us)
Async XLA Ops:
  7.2 95.1 %all-gather.6.cloned.1.call-start = ((), (), s32[]{:S(2)}) async-start(), calls=%async_computation.1 | async-start | bytes 9437184 | tf_op jit(solution)/shard_map/all_gather | solution.py:1030
  13.3 20.2 %collective-permute-start.4 = (bf16[26,128]{1,0:T(8,128)(2,1)}, bf16[26,128]{1,0:T(8,128)(2,1)}, u32[]{:S(2)}, u32[]{:S(2)}) collective-permute-start(bf16[26,128]{1,0:T(8,128)(2,1)} %pad_add_fusion.refs_0_), channel_id=1, source_target_pairs={{0,3},{1,2},{2,1},{3,0},{4,7},{5,6},{6,5},{7,4},{8,11},{9,10},{10,... | collective-permute-start | bytes 19976 | tf_op jit(solution)/shard_map/ppermute | solution.py:1000
  17.1 16.4 %collective-permute-start.3 = (bf16[26,128]{1,0:T(8,128)(2,1)}, bf16[26,128]{1,0:T(8,128)(2,1)}, u32[]{:S(2)}, u32[]{:S(2)}) collective-permute-start(bf16[26,128]{1,0:T(8,128)(2,1)} %pad_add_fusion.refs_0_), channel_id=1, source_target_pairs={{0,2},{1,3},{2,0},{3,1},{4,6},{5,7},{6,4},{7,5},{8,10},{9,11},{10,... | collective-permute-start | bytes 19976 | tf_op jit(solution)/shard_map/ppermute | solution.py:1000
  17.7 15.9 %collective-permute-start.2 = (bf16[26,128]{1,0:T(8,128)(2,1)}, bf16[26,128]{1,0:T(8,128)(2,1)}, u32[]{:S(2)}, u32[]{:S(2)}) collective-permute-start(bf16[26,128]{1,0:T(8,128)(2,1)} %pad_add_fusion.refs_0_), channel_id=1, source_target_pairs={{0,1},{1,0},{2,3},{3,2},{4,5},{5,4},{6,7},{7,6},{8,9},{9,8},{10,11... | collective-permute-start | bytes 19976 | tf_op jit(solution)/shard_map/ppermute | solution.py:1000
  17.7 14.3 %collective-permute-start.1 = (bf16[1,128,2048]{2,1,0:T(8,128)(2,1)}, bf16[1,128,2048]{2,1,0:T(8,128)(2,1)}, u32[]{:S(2)}, u32[]{:S(2)}) collective-permute-start(bf16[1,128,2048]{2,1,0:T(8,128)(2,1)} %get-tuple-element.240.refs_0_), channel_id=1, source_target_pairs={{0,2},{1,3},{2,0},{3,1},{4,5},{5,4},{6,7},{7,6},{8,10},{9,11},{10,... | collective-permute-start | bytes 1572872 | tf_op jit(solution)/shard_map/ppermute | solution.py:1000
  19.7 12.3 %collective-permute-start = (bf16[1,128,2048]{2,1,0:T(8,128)(2,1)}, bf16[1,128,2048]{2,1,0:T(8,128)(2,1)}, u32[]{:S(2)}, u32[]{:S(2)}) collective-permute-start(bf16[1,128,2048]{2,1,0:T(8,128)(2,1)} %get-tuple-element.240.refs_0_), channel_id=1, source_target_pairs={{0,1},{1,0},{2,3},{3,2},{4,6},{5,7},{6,4},{7,5},{8,9},{9,8},{10,11... | collective-permute-start | bytes 1572872 | tf_op jit(solution)/shard_map/ppermute | solution.py:1000
  32.0 10.2 %collective-permute-start.6 = (bf16[1,128,2048]{2,1,0:T(8,128)(2,1)}, bf16[1,128,2048]{2,1,0:T(8,128)(2,1)}, u32[]{:S(2)}, u32[]{:S(2)}) collective-permute-start(bf16[1,128,2048]{2,1,0:T(8,128)(2,1)} %collective-permute-done.refs_2_), channel_id=1, source_target_pairs={{0,4},{1,5},{2,6},{3,7},{4,0},{5,1},{6,2},{7,3},{8,12},{9,13},{10,... | collective-permute-start | bytes 1572872 | tf_op jit(solution)/shard_map/ppermute | solution.py:1000
  33.4 119.4 %all-gather.4.cloned.1.call-start = ((), (), s32[]{:S(2)}) async-start(), calls=%async_computation | async-start | bytes 9437184 | tf_op jit(solution)/shard_map/all_gather | solution.py:1030
  42.1 185.0 %all-gather.8.cloned.1.call-start = ((), (), s32[]{:S(2)}) async-start(), calls=%async_computation.2 | async-start | bytes 4718592 | tf_op jit(solution)/shard_map/all_gather | solution.py:1030
  101.6 36.5 %collective-permute-start.10 = (bf16[2,128,2048]{2,1,0:T(8,128)(2,1)}, bf16[2,128,2048]{2,1,0:T(8,128)(2,1)}, u32[]{:S(2)}, u32[]{:S(2)}) collective-permute-start(bf16[2,128,2048]{2,1,0:T(8,128)(2,1)} %add.91), channel_id=1, source_target_pairs={{0,1},{1,0},{2,3},{3,2},{4,6},{5,7},{6,4},{7,5},{8,9},{9,8},{10,11... | collective-permute-start | bytes 3145736 | tf_op jit(solution)/shard_map/ppermute | solution.py:1000
  150.2 25.1 %collective-permute-start.12 = (bf16[1,128,2048]{2,1,0:T(8,128)(2,1)}, bf16[1,128,2048]{2,1,0:T(8,128)(2,1)}, u32[]{:S(2)}, u32[]{:S(2)}) collective-permute-start(bf16[1,128,2048]{2,1,0:T(8,128)(2,1)} %sums.11), channel_id=1, source_target_pairs={{0,2},{1,3},{2,0},{3,1},{4,5},{5,4},{6,7},{7,6},{8,10},{9,11},{10,... | collective-permute-start | bytes 1572872 | tf_op jit(solution)/shard_map/ppermute | solution.py:1000
  151.5 30.0 %collective-permute-start.13 = (bf16[2,512,1024]{2,1,0:T(8,128)(2,1)}, bf16[2,512,1024]{2,1,0:T(8,128)(2,1)}, u32[]{:S(2)}, u32[]{:S(2)}) collective-permute-start(bf16[2,512,1024]{2,1,0:T(8,128)(2,1)} %add.92), channel_id=1, source_target_pairs={{0,1},{1,0},{2,3},{3,2},{4,6},{5,7},{6,4},{7,5},{8,9},{9,8},{10,11... | collective-permute-start | bytes 6291464 | tf_op jit(solution)/shard_map/ppermute | solution.py:1000
  184.8 25.9 %collective-permute-start.14 = (bf16[1,64,2048]{2,1,0:T(8,128)(2,1)}, bf16[1,64,2048]{2,1,0:T(8,128)(2,1)}, u32[]{:S(2)}, u32[]{:S(2)}) collective-permute-start(bf16[1,64,2048]{2,1,0:T(8,128)(2,1)} %get-tuple-element.295), channel_id=1, source_target_pairs={{0,8},{1,9},{2,10},{3,11},{4,12},{5,13},{6,14},{7,15},{8,0},{9,1},... | collective-permute-start | bytes 786440 | tf_op jit(solution)/shard_map/ppermute | solution.py:1000
  186.9 23.9 %collective-permute-start.15 = (bf16[1,512,1024]{2,1,0:T(8,128)(2,1)}, bf16[1,512,1024]{2,1,0:T(8,128)(2,1)}, u32[]{:S(2)}, u32[]{:S(2)}) collective-permute-start(bf16[1,512,1024]{2,1,0:T(8,128)(2,1)} %get-tuple-element.296), channel_id=1, source_target_pairs={{0,2},{1,3},{2,0},{3,1},{4,5},{5,4},{6,7},{7,6},{8,10},{9,11},{10,... | collective-permute-start | bytes 3145736 | tf_op jit(solution)/shard_map/ppermute | solution.py:1000
  222.9 33.1 %collective-permute-start.17 = (bf16[1,64,2048]{2,1,0:T(8,128)(2,1)}, bf16[1,64,2048]{2,1,0:T(8,128)(2,1)}, u32[]{:S(2)}, u32[]{:S(2)}) collective-permute-start(bf16[1,64,2048]{2,1,0:T(8,128)(2,1)} %get-tuple-element.324.refs_0_), channel_id=1, source_target_pairs={{0,16},{1,17},{2,18},{3,19},{4,20},{5,21},{6,22},{7,23},{8,24},{9,... | collective-permute-start | bytes 786440 | tf_op jit(solution)/shard_map/ppermute | solution.py:1000
  225.6 30.4 %collective-permute-start.18 = (bf16[1,256,1024]{2,1,0:T(8,128)(2,1)}, bf16[1,256,1024]{2,1,0:T(8,128)(2,1)}, u32[]{:S(2)}, u32[]{:S(2)}) collective-permute-start(bf16[1,256,1024]{2,1,0:T(8,128)(2,1)} %get-tuple-element.321), channel_id=1, source_target_pairs={{0,8},{1,9},{2,10},{3,11},{4,12},{5,13},{6,14},{7,15},{8,0},{9,1},... | collective-permute-start | bytes 1572872 | tf_op jit(solution)/shard_map/ppermute | solution.py:1000
  226.9 29.0 %collective-permute-start.19 = (bf16[2,512,1024]{2,1,0:T(8,128)(2,1)}, bf16[2,512,1024]{2,1,0:T(8,128)(2,1)}, u32[]{:S(2)}, u32[]{:S(2)}) collective-permute-start(bf16[2,512,1024]{2,1,0:T(8,128)(2,1)} %add.93), channel_id=1, source_target_pairs={{0,1},{1,0},{2,3},{3,2},{4,6},{5,7},{6,4},{7,5},{8,9},{9,8},{10,11... | collective-permute-start | bytes 6291464 | tf_op jit(solution)/shard_map/ppermute | solution.py:1000
  259.3 33.9 %collective-permute-start.23 = (bf16[1,64,2048]{2,1,0:T(8,128)(2,1)}, bf16[1,64,2048]{2,1,0:T(8,128)(2,1)}, u32[]{:S(2)}, u32[]{:S(2)}) collective-permute-start(bf16[1,64,2048]{2,1,0:T(8,128)(2,1)} %get-tuple-element.364.refs_0_), channel_id=1, source_target_pairs={{0,4},{1,5},{2,6},{3,7},{4,0},{5,1},{6,2},{7,3},{8,12},{9,13},{10,... | collective-permute-start | bytes 786440 | tf_op jit(solution)/shard_map/ppermute | solution.py:1000
  259.4 33.8 %collective-permute-start.22 = (bf16[1,64,2048]{2,1,0:T(8,128)(2,1)}, bf16[1,64,2048]{2,1,0:T(8,128)(2,1)}, u32[]{:S(2)}, u32[]{:S(2)}) collective-permute-start(bf16[1,64,2048]{2,1,0:T(8,128)(2,1)} %get-tuple-element.364.refs_0_), channel_id=1, source_target_pairs={{0,8},{1,9},{2,10},{3,11},{4,12},{5,13},{6,14},{7,15},{8,0},{9,1},... | collective-permute-start | bytes 786440 | tf_op jit(solution)/shard_map/ppermute | solution.py:1000
  261.5 31.7 %collective-permute-start.21 = (bf16[1,256,1024]{2,1,0:T(8,128)(2,1)}, bf16[1,256,1024]{2,1,0:T(8,128)(2,1)}, u32[]{:S(2)}, u32[]{:S(2)}) collective-permute-start(bf16[1,256,1024]{2,1,0:T(8,128)(2,1)} %get-tuple-element.345.refs_4_), channel_id=1, source_target_pairs={{0,16},{1,17},{2,18},{3,19},{4,20},{5,21},{6,22},{7,23},{8,24},{9,... | collective-permute-start | bytes 1572872 | tf_op jit(solution)/shard_map/ppermute | solution.py:1000
  262.1 31.1 %collective-permute-start.20 = (bf16[1,512,1024]{2,1,0:T(8,128)(2,1)}, bf16[1,512,1024]{2,1,0:T(8,128)(2,1)}, u32[]{:S(2)}, u32[]{:S(2)}) collective-permute-start(bf16[1,512,1024]{2,1,0:T(8,128)(2,1)} %get-tuple-element.337), channel_id=1, source_target_pairs={{0,2},{1,3},{2,0},{3,1},{4,5},{5,4},{6,7},{7,6},{8,10},{9,11},{10,... | collective-permute-start | bytes 3145736 | tf_op jit(solution)/shard_map/ppermute | solution.py:1000
  296.8 31.3 %collective-permute-start.31 = (bf16[1,256,1024]{2,1,0:T(8,128)(2,1)}, bf16[1,256,1024]{2,1,0:T(8,128)(2,1)}, u32[]{:S(2)}, u32[]{:S(2)}) collective-permute-start(bf16[1,256,1024]{2,1,0:T(8,128)(2,1)} %get-tuple-element.389.refs_0_), channel_id=1, source_target_pairs={{0,4},{1,5},{2,6},{3,7},{4,0},{5,1},{6,2},{7,3},{8,12},{9,13},{10,... | collective-permute-start | bytes 1572872 | tf_op jit(solution)/shard_map/ppermute | solution.py:1000
  297.3 30.9 %collective-permute-start.30 = (bf16[1,256,1024]{2,1,0:T(8,128)(2,1)}, bf16[1,256,1024]{2,1,0:T(8,128)(2,1)}, u32[]{:S(2)}, u32[]{:S(2)}) collective-permute-start(bf16[1,256,1024]{2,1,0:T(8,128)(2,1)} %get-tuple-element.389.refs_0_), channel_id=1, source_target_pairs={{0,8},{1,9},{2,10},{3,11},{4,12},{5,13},{6,14},{7,15},{8,0},{9,1},... | collective-permute-start | bytes 1572872 | tf_op jit(solution)/shard_map/ppermute | solution.py:1000
  297.7 25.1 %collective-permute-start.26 = (bf16[1,256,1024]{2,1,0:T(8,128)(2,1)}, bf16[1,256,1024]{2,1,0:T(8,128)(2,1)}, u32[]{:S(2)}, u32[]{:S(2)}) collective-permute-start(bf16[1,256,1024]{2,1,0:T(8,128)(2,1)} %get-tuple-element.369), channel_id=1, source_target_pairs={{0,8},{1,9},{2,10},{3,11},{4,12},{5,13},{6,14},{7,15},{8,0},{9,1},... | collective-permute-start | bytes 1572872 | tf_op jit(solution)/shard_map/ppermute | solution.py:1000
  303.0 20.9 %collective-permute-start.27 = (bf16[2,128,2048]{2,1,0:T(8,128)(2,1)}, bf16[2,128,2048]{2,1,0:T(8,128)(2,1)}, u32[]{:S(2)}, u32[]{:S(2)}) collective-permute-start(bf16[2,128,2048]{2,1,0:T(8,128)(2,1)} %add.94), channel_id=1, source_target_pairs={{0,1},{1,0},{2,3},{3,2},{4,6},{5,7},{6,4},{7,5},{8,9},{9,8},{10,11... | collective-permute-start | bytes 3145736 | tf_op jit(solution)/shard_map/ppermute | solution.py:1000
  325.8 28.7 %collective-permute-start.35 = (bf16[1,256,1024]{2,1,0:T(8,128)(2,1)S(1)}, bf16[1,256,1024]{2,1,0:T(8,128)(2,1)S(1)}, u32[]{:S(2)}, u32[]{:S(2)}) collective-permute-start(bf16[1,256,1024]{2,1,0:T(8,128)(2,1)S(1)} %sums.16.refs_0_), channel_id=1, source_target_pairs={{0,16},{1,17},{2,18},{3,19},{4,20},{5,21},{6,22},{7,23},{8,24},{9,... | collective-permute-start | bytes 1572872 | tf_op jit(solution)/shard_map/ppermute | solution.py:1000
  336.1 17.8 %collective-permute-start.34 = (bf16[1,64,2048]{2,1,0:T(8,128)(2,1)S(1)}, bf16[1,64,2048]{2,1,0:T(8,128)(2,1)S(1)}, u32[]{:S(2)}, u32[]{:S(2)}) collective-permute-start(bf16[1,64,2048]{2,1,0:T(8,128)(2,1)S(1)} %get-tuple-element.394), channel_id=1, source_target_pairs={{0,8},{1,9},{2,10},{3,11},{4,12},{5,13},{6,14},{7,15},{8,0},{9,1},... | collective-permute-start | bytes 786440 | tf_op jit(solution)/shard_map/ppermute | solution.py:1000
  355.3 17.8 %collective-permute-start.39 = (bf16[1,256,1024]{2,1,0:T(8,128)(2,1)S(1)}, bf16[1,256,1024]{2,1,0:T(8,128)(2,1)S(1)}, u32[]{:S(2)}, u32[]{:S(2)}) collective-permute-start(bf16[1,256,1024]{2,1,0:T(8,128)(2,1)S(1)} %sums.20.refs_4_), channel_id=1, source_target_pairs={{0,4},{1,5},{2,6},{3,7},{4,0},{5,1},{6,2},{7,3},{8,12},{9,13},{10,... | collective-permute-start | bytes 1572872 | tf_op jit(solution)/shard_map/ppermute | solution.py:1000
  355.4 20.0 %collective-permute-start.38 = (bf16[1,256,1024]{2,1,0:T(8,128)(2,1)S(1)}, bf16[1,256,1024]{2,1,0:T(8,128)(2,1)S(1)}, u32[]{:S(2)}, u32[]{:S(2)}) collective-permute-start(bf16[1,256,1024]{2,1,0:T(8,128)(2,1)S(1)} %sums.20.refs_4_), channel_id=1, source_target_pairs={{0,8},{1,9},{2,10},{3,11},{4,12},{5,13},{6,14},{7,15},{8,0},{9,1},... | collective-permute-start | bytes 1572872 | tf_op jit(solution)/shard_map/ppermute | solution.py:1000
  355.4 17.7 %collective-permute-start.37 = (bf16[1,64,2048]{2,1,0:T(8,128)(2,1)S(1)}, bf16[1,64,2048]{2,1,0:T(8,128)(2,1)S(1)}, u32[]{:S(2)}, u32[]{:S(2)}) collective-permute-start(bf16[1,64,2048]{2,1,0:T(8,128)(2,1)S(1)} %sums.19.refs_0_), channel_id=1, source_target_pairs={{0,16},{1,17},{2,18},{3,19},{4,20},{5,21},{6,22},{7,23},{8,24},{9,... | collective-permute-start | bytes 786440 | tf_op jit(solution)/shard_map/ppermute | solution.py:1000
  358.1 20.5 %collective-permute-start.32 = (bf16[1,256,1024]{2,1,0:T(8,128)(2,1)}, bf16[1,256,1024]{2,1,0:T(8,128)(2,1)S(1)}, u32[]{:S(2)}, u32[]{:S(2)}) collective-permute-start(bf16[1,256,1024]{2,1,0:T(8,128)(2,1)} %collective-permute-done.30.refs_1_), channel_id=1, source_target_pairs={{0,4},{1,5},{2,6},{3,7},{4,0},{5,1},{6,2},{7,3},{8,12},{9,13},{10,... | collective-permute-start | bytes 1572872 | tf_op jit(solution)/shard_map/ppermute | solution.py:1000
  376.0 10.4 %collective-permute-start.43 = (bf16[1,64,2048]{2,1,0:T(8,128)(2,1)S(1)}, bf16[1,64,2048]{2,1,0:T(8,128)(2,1)S(1)}, u32[]{:S(2)}, u32[]{:S(2)}) collective-permute-start(bf16[1,64,2048]{2,1,0:T(8,128)(2,1)S(1)} %sums.21.refs_4_), channel_id=1, source_target_pairs={{0,4},{1,5},{2,6},{3,7},{4,0},{5,1},{6,2},{7,3},{8,12},{9,13},{10,... | collective-permute-start | bytes 786440 | tf_op jit(solution)/shard_map/ppermute | solution.py:1000
  (50 other events, 518.5 us)
Sparse Core Ops, SparseCore 0:
  33.6 54.5 all-gather.5
  90.6 58.9 all-gather.3
  184.9 40.6 all-gather.7
